TPU v7x, 32 devices: a whole 2x2x4 slice. The times are simulated.
32 devices in a mesh: fsdp: 4 (over x, core), seq: 4 (over z), tp: 2 (over y).
Axes of the slice: x: 2, y: 2, z: 4, core: 2. Of those that a mesh axis runs over, the one named last changes fastest.
Arguments:
- tokens: bfloat16 [4096, 2560], P(('fsdp', 'seq', 'tp')), may hold values from -6 to 6
- doc_lengths: int32 [4, 3], P('fsdp'), may hold values from 1 to 769, 1024 in all within a row
- w_query: bfloat16 [2560, 2560], P(('fsdp', 'seq'), 'tp'), may hold values from -0.15625 to 0.15625
- w_key: bfloat16 [2560, 640], P(('fsdp', 'seq'), 'tp'), may hold values from -0.15625 to 0.15625
- w_value: bfloat16 [2560, 640], P(('fsdp', 'seq'), 'tp'), may hold values from -0.125 to 0.125
- w_out: bfloat16 [2560, 2560], P('tp', ('fsdp', 'seq')), may hold values from -1 to 1
- w_gate: bfloat16 [2560, 6912], P(('fsdp', 'seq'), 'tp'), may hold values from -0.125 to 0.125
- w_up: bfloat16 [2560, 6912], P(('fsdp', 'seq'), 'tp'), may hold values from -0.125 to 0.125
- w_down: bfloat16 [6912, 2560], P('tp', ('fsdp', 'seq')), may hold values from -0.078125 to 0.078125
- norm_gains: bfloat16 [2, 2560], P(None, ('fsdp', 'seq')), may hold values from 0.5 to 1.5
- cotangent: bfloat16 [4096, 2560], P(('fsdp', 'seq', 'tp')), may hold values from -6 to 6
Outputs:
- mixed_out: bfloat16 [4096, 2560], P(('fsdp', 'seq', 'tp'))
- grad_tokens: float32 [4096, 2560], P(('fsdp', 'seq', 'tp'))
- grad_query: float32 [2560, 2560], P(('fsdp', 'seq'), 'tp')
- grad_key: float32 [2560, 640], P(('fsdp', 'seq'), 'tp')
- grad_value: float32 [2560, 640], P(('fsdp', 'seq'), 'tp')
- grad_out: float32 [2560, 2560], P('tp', ('fsdp', 'seq'))
- grad_gate: float32 [2560, 6912], P(('fsdp', 'seq'), 'tp')
- grad_up: float32 [2560, 6912], P(('fsdp', 'seq'), 'tp')
- grad_down: float32 [6912, 2560], P('tp', ('fsdp', 'seq'))
- grad_gains: float32 [2, 2560], P(None, ('fsdp', 'seq'))
Inputs may be any that keep to these rules, and one draw needn't show every extreme that they name: `doc_lengths`: in each sequence the document lengths sum to 1024 and the longest has exactly 769 tokens.
All inputs are finite; a program needn't handle non-finite values.
Results may differ from a plain program's by a relative error of at most 0.022.
Values may be sent and summed in bfloat16 or wider, within the bound.
No kernel may reach another device: no remote copies, remote signals or barrier semaphores. Data moves between devices by JAX's collectives and lax.ppermute only.
A program may use at most 192 MiB of HBM per device.

v0:
```python
import math

import jax
import jax.numpy as jnp
from jax import lax
from jax.sharding import PartitionSpec as P

D = 2560
HEAD_DIM = 80
BLOCK = 256
DOCS = 3
GROUP = 4


norm_eps = 1e-05
rope_base = 10000.0
mask_fill = -1000000000.0


def rope_tables(positions):
    half_dim = HEAD_DIM // 2
    freq_row = rope_base ** (-jnp.arange(half_dim, dtype=jnp.float32) * 2.0 / HEAD_DIM)
    angles = positions.astype(jnp.float32)[:, None] * freq_row[None, :]
    return (jnp.cos(angles), jnp.sin(angles))


def rotate(values, cos_tab, sin_tab):
    half_dim = HEAD_DIM // 2
    first_half = values[..., :half_dim]
    second_half = values[..., half_dim:]
    cos_wide = cos_tab[:, None, :]
    sin_wide = sin_tab[:, None, :]
    return jnp.concatenate(
        [
            first_half * cos_wide - second_half * sin_wide,
            second_half * cos_wide + first_half * sin_wide,
        ],
        axis=-1,
    )


def document_ids(lengths, positions):
    doc_ends = jnp.cumsum(lengths)
    return jnp.sum((positions[:, None] >= doc_ends[None, : DOCS - 1]).astype(jnp.int32), axis=1)


def rms_scale(row_values):
    return lax.rsqrt(jnp.mean(row_values * row_values, axis=-1, keepdims=True) + norm_eps)


def per_device(
    tokens, doc_lengths, w_query, w_key, w_value, w_out, w_gate, w_up, w_down, norm_gains, cotangent
):
    tp_count = lax.axis_size("tp")
    seq_count = lax.axis_size("seq")
    tp_index = lax.axis_index("tp")
    seq_index = lax.axis_index("seq")
    local_rows = tokens.shape[0]
    span_len = local_rows * tp_count
    seq_length = span_len * seq_count
    score_scale = 1.0 / math.sqrt(HEAD_DIM)
    key_step = math.gcd(512, seq_length)
    gathered = (
        lax.all_gather(w_query, ("fsdp", "seq"), axis=0, tiled=True),
        lax.all_gather(w_key, ("fsdp", "seq"), axis=0, tiled=True),
        lax.all_gather(w_value, ("fsdp", "seq"), axis=0, tiled=True),
        lax.all_gather(w_out, ("fsdp", "seq"), axis=1, tiled=True),
        lax.all_gather(w_gate, ("fsdp", "seq"), axis=0, tiled=True),
        lax.all_gather(w_up, ("fsdp", "seq"), axis=0, tiled=True),
        lax.all_gather(w_down, ("fsdp", "seq"), axis=1, tiled=True),
        lax.all_gather(norm_gains, ("fsdp", "seq"), axis=1, tiled=True),
    )
    query_full, key_full, value_full, out_full, gate_full, up_full, down_full, gains_low = gathered
    gain_one = gains_low[0].astype(jnp.float32)
    gain_two = gains_low[1].astype(jnp.float32)
    query_heads = query_full.shape[1] // HEAD_DIM
    kv_local = key_full.shape[1] // HEAD_DIM
    span_in = lax.all_gather(tokens, "tp", axis=0, tiled=True)
    span_float = span_in.astype(jnp.float32)
    inv_one = rms_scale(span_float)
    normed_one = (span_float * inv_one * gain_one).astype(jnp.bfloat16)
    span_start = seq_index * span_len
    positions = span_start + jnp.arange(span_len, dtype=jnp.int32)
    cos_tab, sin_tab = rope_tables(positions)
    query_raw = jnp.dot(normed_one, query_full, preferred_element_type=jnp.float32).reshape(
        span_len, query_heads, HEAD_DIM
    )
    key_raw = jnp.dot(normed_one, key_full, preferred_element_type=jnp.float32).reshape(
        span_len, kv_local, HEAD_DIM
    )
    value_raw = jnp.dot(normed_one, value_full, preferred_element_type=jnp.float32).reshape(
        span_len, kv_local, HEAD_DIM
    )
    query_rot = rotate(query_raw, cos_tab, sin_tab).astype(jnp.bfloat16)
    key_rot = rotate(key_raw, cos_tab, sin_tab).astype(jnp.bfloat16)
    value_low = value_raw.astype(jnp.bfloat16)
    query_group = query_rot.reshape(span_len, kv_local, GROUP, HEAD_DIM)
    key_all, value_all = (
        lax.all_gather(key_rot, "seq", axis=0, tiled=True),
        lax.all_gather(value_low, "seq", axis=0, tiled=True),
    )
    key_positions = jnp.arange(seq_length, dtype=jnp.int32)
    doc_keys = document_ids(doc_lengths[0], key_positions)
    doc_query = lax.dynamic_slice_in_dim(doc_keys, span_start, span_len, 0)
    key_blocks = key_positions // BLOCK
    query_block = positions // BLOCK
    blocks_used = (span_start + span_len + key_step - 1) // key_step
    stat_shape = (kv_local, GROUP, span_len)
    head_shape = (span_len, kv_local, GROUP, HEAD_DIM)

    def masked_scores(block_index):
        key_start = block_index * key_step
        key_part = lax.dynamic_slice_in_dim(key_all, key_start, key_step, 0)
        scores = (
            jnp.einsum("ckgd,nkd->kgcn", query_group, key_part, preferred_element_type=jnp.float32)
            * score_scale
        )
        block_part = lax.dynamic_slice_in_dim(key_blocks, key_start, key_step, 0)
        doc_part = lax.dynamic_slice_in_dim(doc_keys, key_start, key_step, 0)
        allowed = (block_part[None, :] <= query_block[:, None]) & (
            doc_part[None, :] == doc_query[:, None]
        )
        return (jnp.where(allowed[None, None], scores, mask_fill), key_start, key_part)

    def total_step(block_index, carry):
        row_max, row_sum = carry
        scores = masked_scores(block_index)[0]
        new_max = jnp.maximum(row_max, jnp.max(scores, axis=-1))
        row_sum = row_sum * jnp.exp(row_max - new_max) + jnp.sum(
            jnp.exp(scores - new_max[..., None]), axis=-1
        )
        return (new_max, row_sum)

    row_max, row_sum = lax.fori_loop(
        0,
        blocks_used,
        total_step,
        (jnp.full(stat_shape, mask_fill, jnp.float32), jnp.zeros(stat_shape, jnp.float32)),
    )
    log_total = row_max + jnp.log(row_sum)

    def out_step(block_index, running):
        scores, key_start, key_part = masked_scores(block_index)
        attn_prob = jnp.exp(scores - log_total[..., None]).astype(jnp.bfloat16)
        value_part = lax.dynamic_slice_in_dim(value_all, key_start, key_step, 0)
        return running + jnp.einsum(
            "kgcn,nkd->ckgd", attn_prob, value_part, preferred_element_type=jnp.float32
        )

    attended = lax.fori_loop(0, blocks_used, out_step, jnp.zeros(head_shape, jnp.float32))
    attended_low = attended.reshape(span_len, query_heads * HEAD_DIM).astype(jnp.bfloat16)
    attn_branch = lax.psum_scatter(
        jnp.dot(attended_low, out_full, preferred_element_type=jnp.float32).astype(jnp.bfloat16),
        "tp",
        scatter_dimension=0,
        tiled=True,
    ).astype(jnp.float32)
    token_rows = tokens.astype(jnp.float32)
    residual = token_rows + attn_branch
    inv_two = rms_scale(residual)
    normed_two = (residual * inv_two * gain_two).astype(jnp.bfloat16)
    span_two = lax.all_gather(normed_two, "tp", axis=0, tiled=True)
    gate_pre = jnp.dot(span_two, gate_full, preferred_element_type=jnp.float32)
    up_pre = jnp.dot(span_two, up_full, preferred_element_type=jnp.float32)
    sig_gate = jax.nn.sigmoid(gate_pre)
    silu_gate = gate_pre * sig_gate
    hidden_low = (silu_gate * up_pre).astype(jnp.bfloat16)
    mlp_branch = lax.psum_scatter(
        jnp.dot(hidden_low, down_full, preferred_element_type=jnp.float32).astype(jnp.bfloat16),
        "tp",
        scatter_dimension=0,
        tiled=True,
    ).astype(jnp.float32)
    mixed_out = (residual + mlp_branch).astype(jnp.bfloat16)
    cot_span = lax.all_gather(cotangent, "tp", axis=0, tiled=True)
    grad_down_w = jnp.einsum("cf,cd->fd", hidden_low, cot_span, preferred_element_type=jnp.float32)
    grad_hidden = jnp.einsum("cd,fd->cf", cot_span, down_full, preferred_element_type=jnp.float32)
    grad_gate_pre = (
        grad_hidden * up_pre * (sig_gate * (1.0 + gate_pre * (1.0 - sig_gate)))
    ).astype(jnp.bfloat16)
    grad_up_pre = (grad_hidden * silu_gate).astype(jnp.bfloat16)
    grad_gate_w = jnp.einsum(
        "cd,cf->df", span_two, grad_gate_pre, preferred_element_type=jnp.float32
    )
    grad_up_w = jnp.einsum("cd,cf->df", span_two, grad_up_pre, preferred_element_type=jnp.float32)
    grad_normed_two = lax.psum_scatter(
        (
            jnp.einsum("cf,df->cd", grad_gate_pre, gate_full, preferred_element_type=jnp.float32)
            + jnp.einsum("cf,df->cd", grad_up_pre, up_full, preferred_element_type=jnp.float32)
        ).astype(jnp.bfloat16),
        "tp",
        scatter_dimension=0,
        tiled=True,
    ).astype(jnp.float32)
    gain_two_term = jnp.sum(grad_normed_two * residual * inv_two, axis=0)
    scaled_two = grad_normed_two * gain_two
    grad_residual = (
        cotangent.astype(jnp.float32)
        + inv_two * scaled_two
        - residual
        * (inv_two * inv_two * inv_two)
        * jnp.mean(scaled_two * residual, axis=-1, keepdims=True)
    )
    grad_span = lax.all_gather(grad_residual.astype(jnp.bfloat16), "tp", axis=0, tiled=True)
    grad_out_w = jnp.einsum(
        "ce,cd->ed", attended_low, grad_span, preferred_element_type=jnp.float32
    )
    grad_attended = (
        jnp.einsum("cd,ed->ce", grad_span, out_full, preferred_element_type=jnp.float32)
        .astype(jnp.bfloat16)
        .reshape(head_shape)
    )

    def prob_grads(block_index):
        scores, key_start, key_part = masked_scores(block_index)
        probs_full = jnp.exp(scores - log_total[..., None])
        value_part = lax.dynamic_slice_in_dim(value_all, key_start, key_step, 0)
        grad_prob = jnp.einsum(
            "ckgd,nkd->kgcn", grad_attended, value_part, preferred_element_type=jnp.float32
        )
        return (probs_full, grad_prob, key_start, key_part)

    def delta_step(block_index, running):
        grads_here = prob_grads(block_index)
        return running + jnp.sum(grads_here[0] * grads_here[1], axis=-1)

    row_delta = lax.fori_loop(0, blocks_used, delta_step, jnp.zeros(stat_shape, jnp.float32))

    def grad_step(block_index, carry):
        query_acc, key_acc, value_acc = carry
        probs_full, grad_prob, key_start, key_part = prob_grads(block_index)
        grad_scores = (probs_full * (grad_prob - row_delta[..., None])).astype(jnp.bfloat16)
        query_acc = query_acc + jnp.einsum(
            "kgcn,nkd->ckgd", grad_scores, key_part, preferred_element_type=jnp.float32
        )
        key_term = (
            jnp.einsum(
                "kgcn,ckgd->nkd", grad_scores, query_group, preferred_element_type=jnp.float32
            )
            * score_scale
        )
        value_term = jnp.einsum(
            "kgcn,ckgd->nkd",
            probs_full.astype(jnp.bfloat16),
            grad_attended,
            preferred_element_type=jnp.float32,
        )
        key_old = lax.dynamic_slice_in_dim(key_acc, key_start, key_step, 0)
        value_old = lax.dynamic_slice_in_dim(value_acc, key_start, key_step, 0)
        key_acc = lax.dynamic_update_slice_in_dim(key_acc, key_old + key_term, key_start, 0)
        value_acc = lax.dynamic_update_slice_in_dim(value_acc, value_old + value_term, key_start, 0)
        return (query_acc, key_acc, value_acc)

    kv_zeros = jnp.zeros((seq_length, kv_local, HEAD_DIM), jnp.float32)
    query_acc, key_acc, value_acc = lax.fori_loop(
        0, blocks_used, grad_step, (jnp.zeros(head_shape, jnp.float32), kv_zeros, kv_zeros)
    )
    key_own, value_own = (
        lax.psum_scatter(
            key_acc.astype(jnp.bfloat16), "seq", scatter_dimension=0, tiled=True
        ).astype(jnp.float32),
        lax.psum_scatter(
            value_acc.astype(jnp.bfloat16), "seq", scatter_dimension=0, tiled=True
        ).astype(jnp.float32),
    )
    grad_query_rot = (query_acc * score_scale).reshape(span_len, query_heads, HEAD_DIM)
    grad_query_raw = (
        rotate(grad_query_rot, cos_tab, -sin_tab)
        .reshape(span_len, query_heads * HEAD_DIM)
        .astype(jnp.bfloat16)
    )
    grad_key_raw = (
        rotate(key_own, cos_tab, -sin_tab)
        .reshape(span_len, kv_local * HEAD_DIM)
        .astype(jnp.bfloat16)
    )
    grad_value_raw = value_own.reshape(span_len, kv_local * HEAD_DIM).astype(jnp.bfloat16)
    grad_query_w = jnp.einsum(
        "cd,ce->de", normed_one, grad_query_raw, preferred_element_type=jnp.float32
    )
    grad_key_w = jnp.einsum(
        "cd,ce->de", normed_one, grad_key_raw, preferred_element_type=jnp.float32
    )
    grad_value_w = jnp.einsum(
        "cd,ce->de", normed_one, grad_value_raw, preferred_element_type=jnp.float32
    )
    normed_part = jnp.einsum(
        "ce,de->cd", grad_query_raw, query_full, preferred_element_type=jnp.float32
    )
    normed_part = normed_part + jnp.einsum(
        "ce,de->cd", grad_key_raw, key_full, preferred_element_type=jnp.float32
    )
    normed_part = normed_part + jnp.einsum(
        "ce,de->cd", grad_value_raw, value_full, preferred_element_type=jnp.float32
    )
    gain_one_term = jnp.sum(normed_part * span_float * inv_one, axis=0)
    gain_block = jnp.broadcast_to(jnp.stack([gain_one_term, gain_two_term])[None], (tp_count, 2, D))
    grad_normed_one, gains_summed = (
        lax.psum_scatter(
            normed_part.astype(jnp.bfloat16), "tp", scatter_dimension=0, tiled=True
        ).astype(jnp.float32),
        lax.psum_scatter(
            gain_block.astype(jnp.bfloat16), "tp", scatter_dimension=0, tiled=True
        ).astype(jnp.float32),
    )
    gains_total = gains_summed[0]
    inv_rows = lax.dynamic_slice_in_dim(inv_one, tp_index * local_rows, local_rows, 0)
    scaled_one = grad_normed_one * gain_one
    grad_tokens = (
        grad_residual
        + inv_rows * scaled_one
        - token_rows
        * (inv_rows * inv_rows * inv_rows)
        * jnp.mean(scaled_one * token_rows, axis=-1, keepdims=True)
    )
    summed = (
        lax.psum_scatter(
            grad_query_w.astype(jnp.bfloat16), ("fsdp", "seq"), scatter_dimension=0, tiled=True
        ).astype(jnp.float32),
        lax.psum_scatter(
            grad_key_w.astype(jnp.bfloat16), ("fsdp", "seq"), scatter_dimension=0, tiled=True
        ).astype(jnp.float32),
        lax.psum_scatter(
            grad_value_w.astype(jnp.bfloat16), ("fsdp", "seq"), scatter_dimension=0, tiled=True
        ).astype(jnp.float32),
        lax.psum_scatter(
            grad_out_w.astype(jnp.bfloat16), ("fsdp", "seq"), scatter_dimension=1, tiled=True
        ).astype(jnp.float32),
        lax.psum_scatter(
            grad_gate_w.astype(jnp.bfloat16), ("fsdp", "seq"), scatter_dimension=0, tiled=True
        ).astype(jnp.float32),
        lax.psum_scatter(
            grad_up_w.astype(jnp.bfloat16), ("fsdp", "seq"), scatter_dimension=0, tiled=True
        ).astype(jnp.float32),
        lax.psum_scatter(
            grad_down_w.astype(jnp.bfloat16), ("fsdp", "seq"), scatter_dimension=1, tiled=True
        ).astype(jnp.float32),
        lax.psum_scatter(
            gains_total.astype(jnp.bfloat16), ("fsdp", "seq"), scatter_dimension=1, tiled=True
        ).astype(jnp.float32),
    )
    return (
        mixed_out,
        grad_tokens,
        summed[0],
        summed[1],
        summed[2],
        summed[3],
        summed[4],
        summed[5],
        summed[6],
        summed[7],
    )


def solution(mesh):
    in_specs = (
        P(("fsdp", "seq", "tp"), None),
        P("fsdp", None),
        P(("fsdp", "seq"), "tp"),
        P(("fsdp", "seq"), "tp"),
        P(("fsdp", "seq"), "tp"),
        P("tp", ("fsdp", "seq")),
        P(("fsdp", "seq"), "tp"),
        P(("fsdp", "seq"), "tp"),
        P("tp", ("fsdp", "seq")),
        P(None, ("fsdp", "seq")),
        P(("fsdp", "seq", "tp"), None),
    )
    out_specs = (
        P(("fsdp", "seq", "tp"), None),
        P(("fsdp", "seq", "tp"), None),
        P(("fsdp", "seq"), "tp"),
        P(("fsdp", "seq"), "tp"),
        P(("fsdp", "seq"), "tp"),
        P("tp", ("fsdp", "seq")),
        P(("fsdp", "seq"), "tp"),
        P(("fsdp", "seq"), "tp"),
        P("tp", ("fsdp", "seq")),
        P(None, ("fsdp", "seq")),
    )
    return jax.shard_map(
        per_device, mesh=mesh, in_specs=in_specs, out_specs=out_specs, check_vma=False
    )
```

profile of v0, /device:TPU:18, one launch (start us, length us, event | category | flops | bytes accessed | tf_op | source)
XLA Modules:
  0.0 1828.6 jit_solution(10414388531975396074)
XLA Ops:
  10.7 28.7 %all-gather = bf16[16,160,2]{1,2,0:T(2,128)(2,1)S(1)} all-gather(bf16[1,160,2]{1,2,0:T(2,128)(2,1)} %bitcast.309), channel_id=1, replica_groups=mesh['fsdp'=4,'seq'=4,'tp'=2] {'fsdp','seq'}, dimensions={0}, use_global_device_ids=true | all-gather | bytes 10880 | tf_op jit(solution)/shard_map/all_gather | solution.py:71
  43.1 32.4 %all-gather.17.cloned.1.call-done = bf16[2560,320]{1,0:T(8,128)(2,1)} async-done(((bf16[160,320]{1,0:T(8,128)(2,1)}), bf16[2560,320]{1,0:T(8,128)(2,1)}) %all-gather.17.cloned.1.call-update) | async-done | bytes 1638416 | tf_op jit(solution)/shard_map/all_gather | solution.py:65
  78.5 19.7 %all_gather.47 = bf16[1024,4,80]{0,2,1:T(8,128)(2,1)S(1)} all-gather(bf16[256,4,80]{0,2,1:T(8,128)(2,1)S(1)} %pad_maximum_fusion.2), channel_id=1, replica_groups=mesh['fsdp'=4,'seq'=4,'tp'=2] {'seq'}, dimensions={0}, use_global_device_ids=true | all-gather | bytes 819200 | tf_op jit(solution)/shard_map/all_gather | solution.py:99
  98.2 20.9 %all-gather.15.cloned.1.call-done = bf16[2560,320]{1,0:T(8,128)(2,1)} async-done(((bf16[160,320]{1,0:T(8,128)(2,1)}), bf16[2560,320]{1,0:T(8,128)(2,1)}) %all-gather.15.cloned.1.call-update) | async-done | bytes 1638416 | tf_op jit(solution)/shard_map/all_gather | solution.py:66
  121.6 21.6 %all_gather.45 = bf16[1024,4,80]{0,2,1:T(8,128)(2,1)S(1)} all-gather(bf16[256,4,80]{0,2,1:T(8,128)(2,1)S(1)} %bitcast.303), channel_id=1, replica_groups=mesh['fsdp'=4,'seq'=4,'tp'=2] {'seq'}, dimensions={0}, use_global_device_ids=true | all-gather | bytes 819200 | tf_op jit(solution)/shard_map/all_gather | solution.py:100
  143.3 45.9 %all-gather.19.cloned.1.call-done = bf16[2560,1280]{1,0:T(8,128)(2,1)} async-done(((bf16[160,1280]{1,0:T(8,128)(2,1)}), bf16[2560,1280]{1,0:T(8,128)(2,1)}) %all-gather.19.cloned.1.call-update) | async-done | bytes 6553616 | tf_op jit(solution)/shard_map/all_gather | solution.py:64
  210.4 42.8 %all-gather.21.cloned.1.call-done = bf16[1280,2560]{0,1:T(8,128)(2,1)} async-done(((bf16[1280,160]{0,1:T(8,128)(2,1)}), bf16[1280,2560]{0,1:T(8,128)(2,1)}) %all-gather.21.cloned.1.call-update) | async-done | bytes 6553616 | tf_op jit(solution)/shard_map/all_gather | solution.py:67
  259.3 23.3 %reduce-scatter.17.cloned.1.call-done = bf16[128,2560]{1,0:T(8,128)(2,1)} async-done(((bf16[256,2560]{1,0:T(8,128)(2,1)}), bf16[128,2560]{1,0:T(8,128)(2,1)}) %reduce-scatter.17.cloned.1.call-update) | async-done | bytes 655376 | tf_op jit(solution)/shard_map/reduce_scatter | solution.py:152
  289.0 21.6 %all-gather.23.cloned.1.call-done = bf16[256,2560]{1,0:T(8,128)(2,1)} async-done(((bf16[128,2560]{1,0:T(8,128)(2,1)}), bf16[256,2560]{1,0:T(8,128)(2,1)}) %all-gather.23.cloned.1.call-update) | async-done | bytes 1310736 | tf_op jit(solution)/shard_map/all_gather | solution.py:162
  310.6 99.0 %all-gather.25.cloned.1.call-done = bf16[2560,3456]{1,0:T(8,128)(2,1)} async-done(((bf16[160,3456]{1,0:T(8,128)(2,1)}), bf16[2560,3456]{1,0:T(8,128)(2,1)}) %all-gather.25.cloned.1.call-update) | async-done | bytes 17694736 | tf_op jit(solution)/shard_map/all_gather | solution.py:68
  409.6 13.2 fusion.115
  422.7 86.8 %all-gather.27.cloned.1.call-done = bf16[2560,3456]{1,0:T(8,128)(2,1)} async-done(((bf16[160,3456]{1,0:T(8,128)(2,1)}), bf16[2560,3456]{1,0:T(8,128)(2,1)}) %all-gather.27.cloned.1.call-update) | async-done | bytes 17694736 | tf_op jit(solution)/shard_map/all_gather | solution.py:69
  509.5 10.9 fusion.116
  520.4 15.8 all-gather.31.cloned.1.call-done
  536.2 99.0 %all-gather.29.cloned.1.call-done = bf16[3456,2560]{0,1:T(8,128)(2,1)} async-done(((bf16[3456,160]{0,1:T(8,128)(2,1)}), bf16[3456,2560]{0,1:T(8,128)(2,1)}) %all-gather.29.cloned.1.call-update) | async-done | bytes 17694736 | tf_op jit(solution)/shard_map/all_gather | solution.py:70
  635.2 16.5 multiply_convert_fusion
  651.7 13.0 fusion.117
  664.7 13.3 fusion.81
  678.3 24.1 %reduce-scatter.21.cloned.1.call-done = bf16[128,2560]{1,0:T(8,128)(2,1)} async-done(((bf16[256,2560]{1,0:T(8,128)(2,1)}), bf16[128,2560]{1,0:T(8,128)(2,1)}) %reduce-scatter.21.cloned.1.call-update) | async-done | bytes 655376 | tf_op jit(solution)/shard_map/reduce_scatter | solution.py:186
  705.6 24.3 %all-gather.33.cloned.1.call-done = bf16[256,2560]{1,0:T(8,128)(2,1)} async-done(((bf16[128,2560]{1,0:T(8,128)(2,1)}), bf16[256,2560]{1,0:T(8,128)(2,1)}) %all-gather.33.cloned.1.call-update) | async-done | bytes 1310736 | tf_op jit(solution)/shard_map/all_gather | solution.py:204
  747.8 22.6 %while.53 = (s32[]{:T(128)}, f32[256,4,4,80]{0,3,2,1:T(8,128)S(1)}, f32[1024,4,80]{0,2,1:T(8,128)}, f32[1024,4,80]{0,2,1:T(8,128)}, s32[]{:T(128)}, /*index=5*/b...) while((s32[]{:T(128)}, f32[256,4,4,80]{0,3,2,1:T(8,128)S(1)}, ...), condition=%wide.region_18.19_spmd.clone, body=%wide.region_17.18_spmd.clone.sunk | while | flops 1699909632 | bytes 60161356 | solution.py:255
  799.2 18.0 reduce-scatter.25.cloned.1.call-done
  837.3 12.9 convolution_convert_fusion.8
  894.3 57.5 %reduce-scatter.31.cloned.1.call-done = bf16[160,320]{1,0:T(8,128)(2,1)} async-done(((bf16[2560,320]{1,0:T(8,128)(2,1)}), bf16[160,320]{1,0:T(8,128)(2,1)}) %reduce-scatter.31.cloned.1.call-update) | async-done | bytes 102416 | tf_op jit(solution)/shard_map/reduce_scatter | solution.py:320
  953.3 63.2 %reduce-scatter.33.cloned.1.call-done = bf16[160,320]{1,0:T(8,128)(2,1)} async-done(((bf16[2560,320]{1,0:T(8,128)(2,1)}), bf16[160,320]{1,0:T(8,128)(2,1)}) %reduce-scatter.33.cloned.1.call-update) | async-done | bytes 102416 | tf_op jit(solution)/shard_map/reduce_scatter | solution.py:323
  1018.2 24.5 %reduce-scatter.27.cloned.1.call-done = bf16[128,2560]{1,0:T(8,128)(2,1)} async-done(((bf16[256,2560]{1,0:T(8,128)(2,1)}), bf16[128,2560]{1,0:T(8,128)(2,1)}) %reduce-scatter.27.cloned.1.call-update) | async-done | bytes 655376 | tf_op jit(solution)/shard_map/reduce_scatter | solution.py:299
  1044.1 23.9 %reduce-scatter.19.cloned.1.call-done = bf16[128,2560]{1,0:T(8,128)(2,1)} async-done(((bf16[256,2560]{1,0:T(8,128)(2,1)}), bf16[128,2560]{1,0:T(8,128)(2,1)}) %reduce-scatter.19.cloned.1.call-update) | async-done | bytes 655376 | tf_op jit(solution)/shard_map/reduce_scatter | solution.py:168
  1071.7 86.8 %reduce-scatter.35.cloned.1.call-done = bf16[1280,160]{0,1:T(8,128)(2,1)} async-done(((bf16[1280,2560]{0,1:T(8,128)(2,1)}), bf16[1280,160]{0,1:T(8,128)(2,1)}) %reduce-scatter.35.cloned.1.call-update) | async-done | bytes 409616 | tf_op jit(solution)/shard_map/reduce_scatter | solution.py:326
  1160.4 87.9 %reduce-scatter.29.cloned.1.call-done = bf16[160,1280]{1,0:T(8,128)(2,1)} async-done(((bf16[2560,1280]{1,0:T(8,128)(2,1)}), bf16[160,1280]{1,0:T(8,128)(2,1)}) %reduce-scatter.29.cloned.1.call-update) | async-done | bytes 409616 | tf_op jit(solution)/shard_map/reduce_scatter | solution.py:317
  1250.3 188.3 %reduce-scatter.37.cloned.1.call-done = bf16[160,3456]{1,0:T(8,128)(2,1)} async-done(((bf16[2560,3456]{1,0:T(8,128)(2,1)}), bf16[160,3456]{1,0:T(8,128)(2,1)}) %reduce-scatter.37.cloned.1.call-update) | async-done | bytes 1105936 | tf_op jit(solution)/shard_map/reduce_scatter | solution.py:329
  1441.3 187.3 %reduce-scatter.39.cloned.1.call-done = bf16[160,3456]{1,0:T(8,128)(2,1)} async-done(((bf16[2560,3456]{1,0:T(8,128)(2,1)}), bf16[160,3456]{1,0:T(8,128)(2,1)}) %reduce-scatter.39.cloned.1.call-update) | async-done | bytes 1105936 | tf_op jit(solution)/shard_map/reduce_scatter | solution.py:332
  1631.4 187.5 %reduce-scatter.41.cloned.1.call-done = bf16[3456,160]{0,1:T(8,128)(2,1)} async-done(((bf16[3456,2560]{0,1:T(8,128)(2,1)}), bf16[3456,160]{0,1:T(8,128)(2,1)}) %reduce-scatter.41.cloned.1.call-update) | async-done | bytes 1105936 | tf_op jit(solution)/shard_map/reduce_scatter | solution.py:335
  (281 shorter events, 225.5 us)
Async XLA Ops:
  7.2 34.2 %all-gather.13.cloned.1.call-start = ((), (), s32[]{:S(2)}) async-start(), calls=%async_computation.14 | async-start | bytes 1966080 | tf_op jit(solution)/shard_map/all_gather | solution.py:78
  7.9 67.6 %all-gather.17.cloned.1.call-start = ((), (), s32[]{:S(2)}) async-start(), calls=%async_computation.16 | async-start | bytes 2088960 | tf_op jit(solution)/shard_map/all_gather | solution.py:65
  8.7 110.5 %all-gather.15.cloned.1.call-start = ((), (), s32[]{:S(2)}) async-start(), calls=%async_computation.15 | async-start | bytes 2088960 | tf_op jit(solution)/shard_map/all_gather | solution.py:66
  9.4 179.8 %all-gather.19.cloned.1.call-start = ((), (), s32[]{:S(2)}) async-start(), calls=%async_computation.17 | async-start | bytes 6963200 | tf_op jit(solution)/shard_map/all_gather | solution.py:64
  10.0 243.3 %all-gather.21.cloned.1.call-start = ((), (), s32[]{:S(2)}) async-start(), calls=%async_computation.18 | async-start | bytes 6963200 | tf_op jit(solution)/shard_map/all_gather | solution.py:67
  10.6 272.0 %reduce-scatter.17.cloned.1.call-start = ((), (), s32[]{:S(2)}) async-start(), calls=%async_computation.19 | async-start | bytes 1966080 | tf_op jit(solution)/shard_map/reduce_scatter | solution.py:152
  39.6 664.5 %copy-start.27 = (f32[2560]{0:T(1024)}, f32[2560]{0:T(1024)S(1)}, u32[]{:S(2)}) copy-start(f32[2560]{0:T(1024)S(1)} %get-tuple-element.435) | copy-start | bytes 30724
  259.2 51.4 %all-gather.23.cloned.1.call-start = ((), (), s32[]{:S(2)}) async-start(), calls=%async_computation.20 | async-start | bytes 1966080 | tf_op jit(solution)/shard_map/all_gather | solution.py:162
  284.0 420.1 %copy-start.34 = (f32[128]{0:T(128)}, f32[128]{0:T(128)S(1)}, u32[]{:S(2)}) copy-start(f32[128]{0:T(128)S(1)} %get-tuple-element.556) | copy-start | bytes 1540
  284.0 420.1 %copy-start.36 = (f32[128]{0:T(128)}, f32[128]{0:T(128)S(1)}, u32[]{:S(2)}) copy-start(f32[128]{0:T(128)S(1)} %get-tuple-element.555) | copy-start | bytes 1540
  286.2 123.4 %all-gather.25.cloned.1.call-start = ((), (), s32[]{:S(2)}) async-start(), calls=%async_computation.21 | async-start | bytes 18800640 | tf_op jit(solution)/shard_map/all_gather | solution.py:68
  286.9 222.6 %all-gather.27.cloned.1.call-start = ((), (), s32[]{:S(2)}) async-start(), calls=%async_computation.22 | async-start | bytes 18800640 | tf_op jit(solution)/shard_map/all_gather | solution.py:69
  287.7 248.5 %all-gather.31.cloned.1.call-start = ((), (), s32[]{:S(2)}) async-start(), calls=%async_computation.25 | async-start | bytes 1966080 | tf_op jit(solution)/shard_map/all_gather | solution.py:175
  288.2 346.9 %all-gather.29.cloned.1.call-start = ((), (), s32[]{:S(2)}) async-start(), calls=%async_computation.23 | async-start | bytes 18800640 | tf_op jit(solution)/shard_map/all_gather | solution.py:70
  289.0 413.3 %reduce-scatter.21.cloned.1.call-start = ((), (), s32[]{:S(2)}) async-start(), calls=%async_computation.26 | async-start | bytes 1966080 | tf_op jit(solution)/shard_map/reduce_scatter | solution.py:186
  310.6 198.9 %copy-start.8 = (bf16[256,2560]{1,0:T(8,128)(2,1)S(1)}, bf16[256,2560]{1,0:T(8,128)(2,1)}, u32[]{:S(2)}) copy-start(bf16[256,2560]{1,0:T(8,128)(2,1)} %all-gather.23.cloned.1.call-done) | copy-start | bytes 3932164
  678.0 51.9 %all-gather.33.cloned.1.call-start = ((), (), s32[]{:S(2)}) async-start(), calls=%async_computation.27 | async-start | bytes 1966080 | tf_op jit(solution)/shard_map/all_gather | solution.py:204
  705.6 87.8 %reduce-scatter.23.cloned.1.call-start = ((), (), s32[]{:S(2)}) async-start(), calls=%async_computation.28 | async-start | bytes 819200 | tf_op jit(solution)/shard_map/reduce_scatter | solution.py:259
  772.7 44.5 %reduce-scatter.25.cloned.1.call-start = ((), (), s32[]{:S(2)}) async-start(), calls=%async_computation.29 | async-start | bytes 819200 | tf_op jit(solution)/shard_map/reduce_scatter | solution.py:262
  776.3 116.4 %reduce-scatter.43.cloned.1.call-start = ((), (), s32[]{:S(2)}) async-start(), calls=%async_computation.38 | async-start | bytes 696320
  831.9 119.9 %reduce-scatter.31.cloned.1.call-start = ((), (), s32[]{:S(2)}) async-start(), calls=%async_computation.32 | async-start | bytes 2088960 | tf_op jit(solution)/shard_map/reduce_scatter | solution.py:320
  834.2 182.4 %reduce-scatter.33.cloned.1.call-start = ((), (), s32[]{:S(2)}) async-start(), calls=%async_computation.33 | async-start | bytes 2088960 | tf_op jit(solution)/shard_map/reduce_scatter | solution.py:323
  836.5 206.2 %reduce-scatter.27.cloned.1.call-start = ((), (), s32[]{:S(2)}) async-start(), calls=%async_computation.30 | async-start | bytes 1966080 | tf_op jit(solution)/shard_map/reduce_scatter | solution.py:299
  837.3 230.7 %reduce-scatter.19.cloned.1.call-start = ((), (), s32[]{:S(2)}) async-start(), calls=%async_computation.24 | async-start | bytes 1966080 | tf_op jit(solution)/shard_map/reduce_scatter | solution.py:168
  850.2 308.3 %reduce-scatter.35.cloned.1.call-start = ((), (), s32[]{:S(2)}) async-start(), calls=%async_computation.34 | async-start | bytes 6963200 | tf_op jit(solution)/shard_map/reduce_scatter | solution.py:326
  856.2 392.1 %reduce-scatter.29.cloned.1.call-start = ((), (), s32[]{:S(2)}) async-start(), calls=%async_computation.31 | async-start | bytes 6963200 | tf_op jit(solution)/shard_map/reduce_scatter | solution.py:317
  861.2 577.4 %reduce-scatter.37.cloned.1.call-start = ((), (), s32[]{:S(2)}) async-start(), calls=%async_computation.35 | async-start | bytes 18800640 | tf_op jit(solution)/shard_map/reduce_scatter | solution.py:329
  871.8 756.9 %reduce-scatter.39.cloned.1.call-start = ((), (), s32[]{:S(2)}) async-start(), calls=%async_computation.36 | async-start | bytes 18800640 | tf_op jit(solution)/shard_map/reduce_scatter | solution.py:332
  881.9 936.9 %reduce-scatter.41.cloned.1.call-start = ((), (), s32[]{:S(2)}) async-start(), calls=%async_computation.37 | async-start | bytes 18800640 | tf_op jit(solution)/shard_map/reduce_scatter | solution.py:335
  892.5 175.5 %copy-start.5 = (bf16[128,2560]{1,0:T(8,128)(2,1)S(1)}, bf16[128,2560]{1,0:T(8,128)(2,1)}, u32[]{:S(2)}) copy-start(bf16[128,2560]{1,0:T(8,128)(2,1)} %reduce-scatter.17.cloned.1.call-done) | copy-start | bytes 1966084
  892.5 175.5 %copy-start.11 = (bf16[128,2560]{1,0:T(8,128)(2,1)S(1)}, bf16[128,2560]{1,0:T(8,128)(2,1)}, u32[]{:S(2)}) copy-start(bf16[128,2560]{1,0:T(8,128)(2,1)} %param.29) | copy-start | bytes 1966084
  892.5 175.5 %copy-start.13 = (bf16[128,2560]{1,0:T(8,128)(2,1)S(1)}, bf16[128,2560]{1,0:T(8,128)(2,1)}, u32[]{:S(2)}) copy-start(bf16[128,2560]{1,0:T(8,128)(2,1)} %reduce-scatter.21.cloned.1.call-done) | copy-start | bytes 1966084
  (37 other events, 1622.9 us)
Sparse Core Ops, SparseCore 0:
  9.6 25.2 all-gather.12
  37.2 38.2 all-gather.16
  77.8 41.3 all-gather.14
  121.3 67.8 all-gather.18
  191.3 61.9 all-gather.20
  259.3 23.1 reduce-scatter.16
  286.3 24.2 all-gather.22
  312.2 97.3 all-gather.24
  411.2 98.2 all-gather.26
  511.0 25.1 all-gather.30
  537.8 97.3 all-gather.28
  678.2 24.1 reduce-scatter.20
  705.7 24.2 all-gather.32
  772.8 20.5 reduce-scatter.22
  796.1 21.0 reduce-scatter.24
  832.0 54.9 reduce-scatter.42
  891.6 60.1 reduce-scatter.30
  956.4 60.1 reduce-scatter.32
  1019.5 23.1 reduce-scatter.26
  1044.8 23.1 reduce-scatter.18
  1072.5 85.9 reduce-scatter.34
  1162.4 85.8 reduce-scatter.28
  1253.1 185.4 reduce-scatter.36
  1443.2 185.3 reduce-scatter.38
  1633.4 185.3 reduce-scatter.40
where the time goes:
time: 1840 us; the launch traced here: 1830 us
  waiting for transfers between devices  1480 us (80%)
  matrix products  197 us (11%)
  blocking collectives  78.3 us (4%)
  other arithmetic  42.8 us (2%)
    reduce_scatter x1, waiting for transfers between devices, per_device(): lax.psum_scatter(grad_gate_w.astype(jnp.bfloat16), ('fsdp', 'seq'), scatt...  188 us
    reduce_scatter x1, waiting for transfers between devices, per_device(): lax.psum_scatter(grad_down_w.astype(jnp.bfloat16), ('fsdp', 'seq'), scatt...  187 us
    reduce_scatter x1, waiting for transfers between devices, per_device(): lax.psum_scatter(grad_up_w.astype(jnp.bfloat16), ('fsdp', 'seq'), scatter...  187 us
    all_gather x1, waiting for transfers between devices, per_device(): lax.all_gather(w_down, ('fsdp', 'seq'), axis=1, tiled=True)  99 us
    all_gather x1, waiting for transfers between devices, per_device(): lax.all_gather(w_gate, ('fsdp', 'seq'), axis=0, tiled=True)  99 us
    reduce_scatter x1, waiting for transfers between devices, per_device(): lax.psum_scatter(grad_query_w.astype(jnp.bfloat16), ('fsdp', 'seq'), scat...  87.9 us
    reduce_scatter x1, waiting for transfers between devices, per_device(): lax.psum_scatter(grad_out_w.astype(jnp.bfloat16), ('fsdp', 'seq'), scatte...  86.8 us
    all_gather x1, waiting for transfers between devices, per_device(): lax.all_gather(w_up, ('fsdp', 'seq'), axis=0, tiled=True)  86.8 us
  transfers between devices with their start and end apart: 25, of which 23 were waited for; matrix products, arithmetic and copies ran while one was open for 8% of the time, Pallas kernels for 0%

commit v1 on v0

--- a/solution.py
+++ b/solution.py
@@ -353,7 +353,343 @@
     )
 
 
+def to_core(value):
+    return lax.ppermute(value, "fsdp", [(i, i ^ 1) for i in range(4)])
+
+
+def to_x(value):
+    return lax.ppermute(value, "fsdp", [(i, i ^ 2) for i in range(4)])
+
+
+def to_near(value):
+    return lax.ppermute(value, "seq", [(i, i ^ 1) for i in range(4)])
+
+
+def to_far(value):
+    return lax.ppermute(value, "seq", [(i, i ^ 2) for i in range(4)])
+
+
+def to_tp(value):
+    return lax.ppermute(value, "tp", [(0, 1), (1, 0)])
+
+
+def float_of(value):
+    return value.astype(jnp.float32)
+
+
+def low_of(value):
+    return value.astype(jnp.bfloat16)
+
+
+def rows_dot(left, right):
+    return lax.dot_general(left, right, (((0,), (0,)), ((), ())), preferred_element_type=jnp.float32)
+
+
+def cols_dot(left, right):
+    return lax.dot_general(left, right, (((1,), (1,)), ((), ())), preferred_element_type=jnp.float32)
+
+
+def wide_dot(left, pieces):
+    depth = pieces[0].shape[0]
+    return sum(
+        jnp.dot(left[:, i * depth : (i + 1) * depth], piece, preferred_element_type=jnp.float32)
+        for i, piece in enumerate(pieces)
+    )
+
+
+def half_plan(
+    tokens, doc_lengths, w_query, w_key, w_value, w_out, w_gate, w_up, w_down, norm_gains, cotangent
+):
+    fsdp_index = lax.axis_index("fsdp")
+    seq_index = lax.axis_index("seq")
+    tp_index = lax.axis_index("tp")
+    near = seq_index % 2
+    far = seq_index // 2
+    local_rows = tokens.shape[0]
+    group_rows = 4 * local_rows
+    quarter = D // 4
+    block_rows = D // 16
+    score_scale = 1.0 / math.sqrt(HEAD_DIM)
+    order = (0, 2, 1, 3)
+
+    def columns_in(value):
+        return jnp.concatenate(
+            [
+                lax.dynamic_slice_in_dim(value, (fsdp_index ^ k) * quarter, quarter, 1)
+                for k in order
+            ],
+            axis=1,
+        )
+
+    def columns_out(value):
+        pieces = []
+        for block in range(4):
+            k = fsdp_index ^ block
+            place = (k // 2) + (k % 2) * 2
+            pieces.append(lax.dynamic_slice_in_dim(value, place * quarter, quarter, 1))
+        return jnp.concatenate(pieces, axis=1)
+
+    def both_halves(array, axis):
+        size = array.shape[axis] // 2
+        low_part = lax.slice_in_dim(array, 0, size, axis=axis)
+        high_part = lax.slice_in_dim(array, size, 2 * size, axis=axis)
+        first = near == 0
+        return jnp.where(first, low_part, high_part), jnp.where(first, high_part, low_part)
+
+    def spread(own, other):
+        received = to_near(other)
+        first = near == 0
+        pair = jnp.concatenate(
+            [jnp.where(first, own, received), jnp.where(first, received, own)], axis=0
+        )
+        pair_far = to_far(pair)
+        left = far == 0
+        plane = jnp.concatenate(
+            [jnp.where(left, pair, pair_far), jnp.where(left, pair_far, pair)], axis=0
+        )
+        mine = jnp.concatenate([plane, to_x(plane)], axis=0)
+        return mine, to_core(mine)
+
+    def collect(grad_mine, grad_other):
+        from_core = to_core(grad_other)
+        send_x = low_of(float_of(grad_mine[quarter:]) + float_of(from_core[quarter:]))
+        from_x = to_x(send_x)
+        plane = low_of(
+            float_of(grad_mine[:quarter]) + float_of(from_core[:quarter]) + float_of(from_x)
+        )
+        size = 2 * block_rows
+        from_far = to_far(lax.dynamic_slice_in_dim(plane, (1 - far) * size, size, 0))
+        pair = lax.dynamic_slice_in_dim(plane, far * size, size, 0)
+        pair = low_of(float_of(pair) + float_of(from_far))
+        received = to_near(lax.dynamic_slice_in_dim(pair, (1 - near) * block_rows, block_rows, 0))
+        own = lax.dynamic_slice_in_dim(pair, near * block_rows, block_rows, 0)
+        return own, received
+
+    def joined(own, received):
+        first = near == 0
+        return float_of(
+            jnp.concatenate(
+                [jnp.where(first, own, received), jnp.where(first, received, own)], axis=1
+            )
+        )
+
+    def gather_rows(value):
+        half = value.shape[1] // 2
+        one, two = value[:, :half], value[:, half:]
+        one = jnp.concatenate([one, to_near(one)], axis=0)
+        two = jnp.concatenate([two, to_tp(two)], axis=0)
+        one_far = to_tp(one)
+        two_far = to_near(two)
+        one = jnp.concatenate(
+            [one[:local_rows], one_far[:local_rows], one[local_rows:], one_far[local_rows:]], axis=0
+        )
+        two = jnp.concatenate([two, two_far], axis=0)
+        return jnp.concatenate([one, two], axis=1)
+
+    def scatter_rows(one, two):
+        n = local_rows
+        send_one = jnp.concatenate([one[n : 2 * n], one[3 * n :]], axis=0)
+        got_one = to_tp(send_one)
+        got_two = to_near(two[2 * n :])
+        next_one = low_of(float_of(one[2 * n : 3 * n]) + float_of(got_one[n:]))
+        next_two = low_of(float_of(two[n : 2 * n]) + float_of(got_two[n:]))
+        last_one = to_near(next_one)
+        last_two = to_tp(next_two)
+        sum_one = float_of(one[:n]) + float_of(got_one[:n]) + float_of(last_one)
+        sum_two = float_of(two[:n]) + float_of(got_two[:n]) + float_of(last_two)
+        return jnp.concatenate([sum_one, sum_two], axis=1)
+
+    query_own, query_other = both_halves(w_query, 1)
+    key_own, key_other = both_halves(w_key, 1)
+    value_own, value_other = both_halves(w_value, 1)
+    heads_weights = spread(
+        jnp.concatenate([query_own, key_own, value_own], axis=1),
+        jnp.concatenate([query_other, key_other, value_other], axis=1),
+    )
+    out_weights = spread(*both_halves(w_out.T, 1))
+    gate_weights = spread(*both_halves(w_gate, 1))
+    up_weights = spread(*both_halves(w_up, 1))
+    down_weights = spread(*both_halves(w_down.T, 1))
+    gains_low = columns_in(lax.all_gather(norm_gains, ("fsdp", "seq"), axis=1, tiled=True))
+    gain_one = float_of(gains_low[0])
+    gain_two = float_of(gains_low[1])
+
+    tokens_in = columns_in(tokens)
+    cot_in = columns_in(cotangent)
+    span_in = gather_rows(tokens_in)
+    cot_span = gather_rows(cot_in)
+
+    span_float = float_of(span_in)
+    inv_one = rms_scale(span_float)
+    normed_one = low_of(span_float * inv_one * gain_one)
+
+    query_width = query_own.shape[1]
+    key_width = key_own.shape[1]
+    kv_local = key_width // HEAD_DIM
+    query_heads = query_width // HEAD_DIM
+    row_ids = jnp.arange(local_rows, dtype=jnp.int32)
+    own_positions = jnp.concatenate(
+        [
+            far * (2 * 2 * local_rows)
+            + (near ^ i) * (2 * local_rows)
+            + (tp_index ^ j) * local_rows
+            + row_ids
+            for i in range(2)
+            for j in range(2)
+        ]
+    )
+    cos_tab, sin_tab = rope_tables(own_positions)
+    raw = wide_dot(normed_one, heads_weights)
+    query_raw = raw[:, :query_width].reshape(group_rows, query_heads, HEAD_DIM)
+    key_raw = raw[:, query_width : query_width + key_width].reshape(group_rows, kv_local, HEAD_DIM)
+    query_rot = low_of(rotate(query_raw, cos_tab, sin_tab)).reshape(
+        group_rows, kv_local, GROUP, HEAD_DIM
+    )
+    key_rot = low_of(rotate(key_raw, cos_tab, sin_tab))
+    value_low = low_of(raw[:, query_width + key_width :]).reshape(group_rows, kv_local, HEAD_DIM)
+    own_kv = jnp.stack([key_rot, value_low])
+    early_kv = lax.ppermute(own_kv, "seq", [(0, 2), (1, 3)])
+    key_all = jnp.concatenate([early_kv[0], own_kv[0]], axis=0)
+    value_all = jnp.concatenate([early_kv[1], own_kv[1]], axis=0)
+    key_positions = jnp.concatenate([own_positions - group_rows, own_positions])
+    doc_ends = jnp.cumsum(doc_lengths[0])[: DOCS - 1]
+
+    def doc_of(positions):
+        return jnp.sum((positions[:, None] >= doc_ends[None, :]).astype(jnp.int32), axis=1)
+
+    allowed = (
+        (key_positions[None, :] // BLOCK <= own_positions[:, None] // BLOCK)
+        & (key_positions[None, :] >= 0)
+        & (doc_of(key_positions)[None, :] == doc_of(own_positions)[:, None])
+    )
+    scores = (
+        jnp.einsum("ckgd,nkd->kgcn", query_rot, key_all, preferred_element_type=jnp.float32)
+        * score_scale
+    )
+    scores = jnp.where(allowed[None, None], scores, mask_fill)
+    row_max = jnp.max(scores, axis=-1, keepdims=True)
+    log_total = row_max + jnp.log(jnp.sum(jnp.exp(scores - row_max), axis=-1, keepdims=True))
+    probs_full = jnp.exp(scores - log_total)
+    attn_prob = low_of(probs_full)
+    attended = jnp.einsum(
+        "kgcn,nkd->ckgd", attn_prob, value_all, preferred_element_type=jnp.float32
+    )
+    attended_low = low_of(attended.reshape(group_rows, query_width))
+    attn_branch = scatter_rows(*[low_of(cols_dot(attended_low, w)) for w in out_weights])
+    token_rows = float_of(tokens_in)
+    residual = token_rows + attn_branch
+    inv_two = rms_scale(residual)
+    normed_two = low_of(residual * inv_two * gain_two)
+    span_two = gather_rows(normed_two)
+    gate_pre = wide_dot(span_two, gate_weights)
+    up_pre = wide_dot(span_two, up_weights)
+    sig_gate = jax.nn.sigmoid(gate_pre)
+    silu_gate = gate_pre * sig_gate
+    hidden_low = low_of(silu_gate * up_pre)
+    grad_hidden = wide_dot(cot_span, down_weights)
+    grad_gate_pre = low_of(grad_hidden * up_pre * (sig_gate * (1.0 + gate_pre * (1.0 - sig_gate))))
+    grad_up_pre = low_of(grad_hidden * silu_gate)
+    mlp_branch = scatter_rows(*[low_of(cols_dot(hidden_low, w)) for w in down_weights])
+    mixed_out = columns_out(low_of(residual + mlp_branch))
+    grad_normed_two = scatter_rows(
+        *[
+            low_of(cols_dot(grad_gate_pre, gate_w) + cols_dot(grad_up_pre, up_w))
+            for gate_w, up_w in zip(gate_weights, up_weights)
+        ]
+    )
+    middle = D // 2
+
+    def weight_grad(left, right):
+        return collect(
+            low_of(rows_dot(left[:, :middle], right)), low_of(rows_dot(left[:, middle:], right))
+        )
+
+    down_grad = weight_grad(cot_span, hidden_low)
+    gate_grad = weight_grad(span_two, grad_gate_pre)
+    up_grad = weight_grad(span_two, grad_up_pre)
+    gain_two_term = jnp.sum(grad_normed_two * residual * inv_two, axis=0)
+    scaled_two = grad_normed_two * gain_two
+    grad_residual = (
+        float_of(cot_in)
+        + inv_two * scaled_two
+        - residual
+        * (inv_two * inv_two * inv_two)
+        * jnp.mean(scaled_two * residual, axis=-1, keepdims=True)
+    )
+    grad_span = gather_rows(low_of(grad_residual))
+    out_grad = weight_grad(grad_span, attended_low)
+    grad_attended = low_of(wide_dot(grad_span, out_weights)).reshape(
+        group_rows, kv_local, GROUP, HEAD_DIM
+    )
+    grad_prob = jnp.einsum(
+        "ckgd,nkd->kgcn", grad_attended, value_all, preferred_element_type=jnp.float32
+    )
+    row_delta = jnp.sum(probs_full * grad_prob, axis=-1, keepdims=True)
+    grad_scores = low_of(probs_full * (grad_prob - row_delta))
+    query_acc = jnp.einsum(
+        "kgcn,nkd->ckgd", grad_scores, key_all, preferred_element_type=jnp.float32
+    )
+    key_acc = jnp.einsum(
+        "kgcn,ckgd->nkd", grad_scores, query_rot, preferred_element_type=jnp.float32
+    )
+    value_acc = jnp.einsum(
+        "kgcn,ckgd->nkd", attn_prob, grad_attended, preferred_element_type=jnp.float32
+    )
+    kv_grads = jnp.stack([key_acc * score_scale, value_acc])
+    late_kv = lax.ppermute(low_of(kv_grads[:, :group_rows]), "seq", [(2, 0), (3, 1)])
+    own_grads = kv_grads[:, group_rows:] + float_of(late_kv)
+    grad_query_raw = low_of(
+        rotate(
+            (query_acc * score_scale).reshape(group_rows, query_heads, HEAD_DIM), cos_tab, -sin_tab
+        )
+    ).reshape(group_rows, query_width)
+    grad_key_raw = low_of(rotate(own_grads[0], cos_tab, -sin_tab)).reshape(group_rows, key_width)
+    grad_value_raw = low_of(own_grads[1]).reshape(group_rows, key_width)
+    grad_raw = jnp.concatenate([grad_query_raw, grad_key_raw, grad_value_raw], axis=1)
+    heads_grad = weight_grad(normed_one, grad_raw)
+    normed_parts = [cols_dot(grad_raw, w) for w in heads_weights]
+    gain_one_term = jnp.sum(
+        jnp.concatenate(normed_parts, axis=1) * span_float * inv_one, axis=0
+    )
+    grad_normed_one = scatter_rows(*[low_of(part) for part in normed_parts])
+    inv_rows = inv_one[:local_rows]
+    scaled_one = grad_normed_one * gain_one
+    grad_tokens = columns_out(
+        grad_residual
+        + inv_rows * scaled_one
+        - token_rows
+        * (inv_rows * inv_rows * inv_rows)
+        * jnp.mean(scaled_one * token_rows, axis=-1, keepdims=True)
+    )
+    gain_rows = columns_out(jnp.stack([gain_one_term, gain_two_term]))
+    gain_grads = lax.psum_scatter(
+        lax.psum(gain_rows, "tp"), ("fsdp", "seq"), scatter_dimension=1, tiled=True
+    )
+    heads_own, heads_other = heads_grad
+    splits = (query_width, query_width + key_width)
+    grad_query, grad_key, grad_value = (
+        joined(own, other)
+        for own, other in zip(
+            jnp.split(heads_own, splits, axis=1), jnp.split(heads_other, splits, axis=1)
+        )
+    )
+    return (
+        mixed_out,
+        grad_tokens,
+        grad_query,
+        grad_key,
+        grad_value,
+        joined(*out_grad).T,
+        joined(*gate_grad),
+        joined(*up_grad),
+        joined(*down_grad).T,
+        gain_grads,
+    )
+
+
 def solution(mesh):
+    halves = mesh.shape["seq"] == 4 and mesh.shape["tp"] == 2 and mesh.shape["fsdp"] == 4
+    plan = half_plan if halves else per_device
     in_specs = (
         P(("fsdp", "seq", "tp"), None),
         P("fsdp", None),
@@ -380,5 +716,5 @@
         P(None, ("fsdp", "seq")),
     )
     return jax.shard_map(
-        per_device, mesh=mesh, in_specs=in_specs, out_specs=out_specs, check_vma=False
-    )
+        plan, mesh=mesh, in_specs=in_specs, out_specs=out_specs, check_vma=False
+    )

time: 1840 us -> 1140 us (0.62)
  waiting for transfers between devices: 1480 us -> 510 us
  local copies, waits for them, and re-layouts: 14.7 us -> 139 us
  other arithmetic: 42.8 us -> 148 us
  starting transfers between devices: 1.64 us -> 93.2 us
  matrix products: 197 us -> 161 us
  blocking collectives: 78.3 us -> 54.6 us
    reduce_scatter x13 -> x0, waiting for transfers between devices: 983 us -> none  [the longest x1 188 us: per_device(): lax.psum_scatter(grad_gate_w.astype(jnp.bfloat16), ('fsdp', 'seq'), scatt...]
    all_gather x11 -> x0, waiting for transfers between devices: 488 us -> none  [the longest x1 99 us: per_device(): lax.all_gather(w_down, ('fsdp', 'seq'), axis=1, tiled=True)]
    ppermute x0 -> x74, waiting for transfers between devices: none -> 458 us  [the longest x10 166 us: to_far(): return lax.ppermute(value, 'seq', [(i, i ^ 2) for i in range(4)])]
    ppermute x0 -> x74, starting transfers between devices: none -> 93.2 us  [the longest x26 43.6 us: to_near(): return lax.ppermute(value, 'seq', [(i, i ^ 1) for i in range(4)])]
    unnamed x26 -> x2, waiting for transfers between devices: 6.65 us -> 52.4 us
    concatenate x0 -> x9, local copies, waits for them, and re-layouts: none -> 42.2 us  [the longest x5 32.5 us: spread(): mine = jnp.concatenate([plane, to_x(plane)], axis=0)]
    dot_general x39 -> x36, matrix products: 197 us -> 161 us  [the longest x10 43.3 us: wide_dot(): jnp.dot(left[:, i * depth:(i + 1) * depth], piece, preferred_element_type...]
    select_n x9 -> x24, other arithmetic: 0.08 us -> 30.8 us  [the longest x5 9.37 us: spread(): jnp.where(first, own, received)]
  transfers between devices with their start and end apart: 25 -> 75, of which waited for: 23 -> 39; matrix products, arithmetic and copies ran while one was open for 8% -> 36% of each run, Pallas kernels for 0% -> 0%
where the time goes in v1:
time: 1140 us; the launch traced here: 1120 us
  waiting for transfers between devices  510 us (45%)
  matrix products  161 us (14%)
  other arithmetic  148 us (13%)
  local copies, waits for them, and re-layouts  139 us (12%)
  starting transfers between devices  93.2 us (8%)
  blocking collectives  54.6 us (5%)
  between operations  16.8 us (1%)
    ppermute x10, waiting for transfers between devices, to_far(): return lax.ppermute(value, 'seq', [(i, i ^ 2) for i in range(4)])  166 us
    ppermute x10, waiting for transfers between devices, to_x(): return lax.ppermute(value, 'fsdp', [(i, i ^ 2) for i in range(4)])  150 us
    ppermute x26, waiting for transfers between devices, to_near(): return lax.ppermute(value, 'seq', [(i, i ^ 1) for i in range(4)])  75 us
    ppermute x16, waiting for transfers between devices, to_tp(): return lax.ppermute(value, 'tp', [(0, 1), (1, 0)])  54.4 us
    unnamed x2, waiting for transfers between devices  52.4 us
    convert_element_type x27, other arithmetic, low_of(): return value.astype(jnp.bfloat16)  49.8 us
    all_gather x1, blocking collectives, half_plan(): lax.all_gather(norm_gains, ('fsdp', 'seq'), axis=1, tiled=True)  48.9 us
    ppermute x26, starting transfers between devices, to_near(): return lax.ppermute(value, 'seq', [(i, i ^ 1) for i in range(4)])  43.6 us
  transfers between devices with their start and end apart: 75, of which 39 were waited for; matrix products, arithmetic and copies ran while one was open for 36% of the time, Pallas kernels for 0%

profile of v1, /device:TPU:18, one launch (start us, length us, event | category | flops | bytes accessed | tf_op | source)
XLA Modules:
  0.0 1123.4 jit_solution(14293209350299295506)
XLA Ops:
  24.5 48.9 %all-gather = bf16[16,160,2]{1,2,0:T(2,128)(2,1)S(1)} all-gather(bf16[1,160,2]{1,2,0:T(2,128)(2,1)S(1)} %bitcast.202), channel_id=1, replica_groups=mesh['fsdp'=4,'seq'=4,'tp'=2] {'fsdp','seq'}, dimensions={0}, use_global_device_ids=true | all-gather | bytes 10880 | tf_op jit(solution)/shard_map/all_gather | solution.py:513
  125.2 8.0 collective-permute-done.29
  167.8 11.3 %fusion.5 = (f32[512]{0:T(512)S(1)}, bf16[512,2560]{1,0:T(8,128)(2,1)S(1)}) fusion(bf16[256,1280]{1,0:T(8,128)(2,1)} %collective-permute-done.3, bf16[128,1280]{1,0:T(8,128)(2,1)} %collective-permute-done.2, bf16[128,640]{1,0:T(8,128)(2,1)S(1)} %copy-done.17, bf16[128,640]{1,0:T(8,128)(2,1)S(1)} %copy-done.21, bf16[128,1280]{1,0:T(8,128)(2,1)S(1)} %get-tuple-element.137, ...), kind=kLoop, calls=%fused_computation.19 | loop fusion | flops 27524608 | bytes 5244928 | tf_op jit(solution)/shard_map/reduce_sum | solution.py:48
  179.7 7.9 collective-permute-done.6
  205.5 45.9 %collective-permute-done.20 = bf16[320,1728]{1,0:T(8,128)(2,1)} collective-permute-done((bf16[320,1728]{1,0:T(8,128)(2,1)}, bf16[320,1728]{1,0:T(8,128)(2,1)}, u32[]{:S(2)}, u32[]{:S(2)}) %collective-permute-start.20) | collective-permute-done | bytes 1105952 | tf_op jit(solution)/shard_map/ppermute | solution.py:369
  259.5 16.4 %collective-permute-done.26 = bf16[320,1728]{1,0:T(8,128)(2,1)} collective-permute-done((bf16[320,1728]{1,0:T(8,128)(2,1)}, bf16[320,1728]{1,0:T(8,128)(2,1)}, u32[]{:S(2)}, u32[]{:S(2)}) %collective-permute-start.26) | collective-permute-done | bytes 1105952 | tf_op jit(solution)/shard_map/ppermute | solution.py:369
  285.4 10.2 collective-permute-done.30
  326.1 9.2 exponential_reduce_fusion
  335.4 8.2 convolution_convert_fusion.14
  360.2 7.7 concatenate.314
  376.2 7.8 concatenate.319
  384.0 27.4 %collective-permute-done.31 = bf16[640,1728]{0,1:T(8,128)(2,1)} collective-permute-done((bf16[640,1728]{0,1:T(8,128)(2,1)}, bf16[640,1728]{0,1:T(8,128)(2,1)}, u32[]{:S(2)}, u32[]{:S(2)}) %collective-permute-start.31) | collective-permute-done | bytes 2211872 | tf_op jit(solution)/shard_map/ppermute | solution.py:361
  411.4 8.0 concatenate.322
  446.2 7.6 collective-permute-done.17
  457.1 7.6 collective-permute-done.22
  466.8 10.7 collective-permute-done.18
  580.0 7.8 collective-permute-done.42
  617.3 9.0 collective-permute-done.46
  632.0 14.3 %fusion = (f32[2,4,512]{2,1,0:T(4,128)S(1)}, f32[2,1024,512,4]{2,1,3,0:T(8,128)}) fusion(f32[2,1024,512,4]{2,1,3,0:T(8,128)} %get-tuple-element.178, f32[2,4,512]{2,1,0:T(4,128)S(1)} %bitcast.196, pred[512,1024]{0,1:T(8,128)(4,1)S(1)} %compare_and_fusion, bf16[512,2,4,80]{0,3,2,1:T(8,128)(2,1)S(1)} %bitcast.175, bf16[512,2,80]{0,2,1:T(8,128)(2,1)S(1)} %bitcast.179, ...), kind=kOutput, calls=%fused_computation.2 | convolution fusion | flops 692711424 | bytes 35094528 | tf_op jit(solution)/shard_map/ckgd,nkd->kgcn/dot_general | solution.py:624
  646.4 11.2 convolution_bitcast_fusion
  657.6 8.4 fusion.2
  703.1 52.4 %reduce-scatter.4.cloned.1.call-done = f32[160,2]{1,0:T(8,128)} async-done(((f32[2560,2]{1,0:T(8,128)}), f32[160,2]{1,0:T(8,128)}) %reduce-scatter.4.cloned.1.call-update) | async-done | bytes 1296
  765.2 8.4 collective-permute-done.51
  793.9 14.4 %collective-permute-done.59 = bf16[640,640]{0,1:T(8,128)(2,1)S(1)} collective-permute-done((bf16[640,640]{0,1:T(8,128)(2,1)S(1)}, bf16[640,640]{0,1:T(8,128)(2,1)S(1)}, u32[]{:S(2)}, u32[]{:S(2)}) %collective-permute-start.59) | collective-permute-done | bytes 819232 | tf_op jit(solution)/shard_map/ppermute | solution.py:361
  814.5 16.2 %collective-permute-done.60 = bf16[320,640]{0,1:T(8,128)(2,1)S(1)} collective-permute-done((bf16[320,640]{0,1:T(8,128)(2,1)S(1)}, bf16[320,640]{0,1:T(8,128)(2,1)S(1)}, u32[]{:S(2)}, u32[]{:S(2)}) %collective-permute-start.60) | collective-permute-done | bytes 409632 | tf_op jit(solution)/shard_map/ppermute | solution.py:369
  833.8 48.2 %collective-permute-done.55 = bf16[640,960]{0,1:T(8,128)(2,1)S(1)} collective-permute-done((bf16[640,960]{0,1:T(8,128)(2,1)S(1)}, bf16[640,960]{0,1:T(8,128)(2,1)S(1)}, u32[]{:S(2)}, u32[]{:S(2)}) %collective-permute-start.55) | collective-permute-done | bytes 1228832 | tf_op jit(solution)/shard_map/ppermute | solution.py:361
  892.0 20.0 %collective-permute-done.56 = bf16[320,960]{1,0:T(8,128)(2,1)} collective-permute-done((bf16[320,960]{1,0:T(8,128)(2,1)S(1)}, bf16[320,960]{1,0:T(8,128)(2,1)}, u32[]{:S(2)}, u32[]{:S(2)}) %collective-permute-start.56) | collective-permute-done | bytes 614432 | tf_op jit(solution)/shard_map/ppermute | solution.py:369
  939.0 37.5 %collective-permute-done.63 = bf16[640,1728]{0,1:T(8,128)(2,1)} collective-permute-done((bf16[640,1728]{0,1:T(8,128)(2,1)}, bf16[640,1728]{0,1:T(8,128)(2,1)}, u32[]{:S(2)}, u32[]{:S(2)}) %collective-permute-start.63) | collective-permute-done | bytes 2211872 | tf_op jit(solution)/shard_map/ppermute | solution.py:361
  992.3 33.7 %collective-permute-done.68 = bf16[320,1728]{1,0:T(8,128)(2,1)} collective-permute-done((bf16[320,1728]{1,0:T(8,128)(2,1)}, bf16[320,1728]{1,0:T(8,128)(2,1)}, u32[]{:S(2)}, u32[]{:S(2)}) %collective-permute-start.68) | collective-permute-done | bytes 1105952 | tf_op jit(solution)/shard_map/ppermute | solution.py:369
  1037.6 13.1 %collective-permute-done.72 = bf16[320,1728]{1,0:T(8,128)(2,1)} collective-permute-done((bf16[320,1728]{1,0:T(8,128)(2,1)}, bf16[320,1728]{1,0:T(8,128)(2,1)}, u32[]{:S(2)}, u32[]{:S(2)}) %collective-permute-start.72) | collective-permute-done | bytes 1105952 | tf_op jit(solution)/shard_map/ppermute | solution.py:369
  1063.3 10.6 collective-permute-done.64
  1087.8 10.9 collective-permute-done.73
  (690 shorter events, 547.6 us)
Async XLA Ops:
  7.2 748.4 %reduce-scatter.4.cloned.1.call-start = ((), (), s32[]{:S(2)}) async-start(), calls=%async_computation.1 | async-start | bytes 1392640
  11.0 92.5 %collective-permute-start.19 = (bf16[160,1728]{1,0:T(8,128)(2,1)}, bf16[160,1728]{1,0:T(8,128)(2,1)}, u32[]{:S(2)}, u32[]{:S(2)}) collective-permute-start(bf16[160,1728]{1,0:T(8,128)(2,1)} %copy.154), channel_id=1, source_target_pairs={{0,2},{2,0},{4,6},{6,4},{1,3},{3,1},{5,7},{7,5},{8,10},{10,8},{12,... | collective-permute-start | bytes 1658888 | tf_op jit(solution)/shard_map/ppermute | solution.py:365
  13.6 73.1 %collective-permute-start.9 = (bf16[160,640]{0,1:T(8,128)(2,1)}, bf16[160,640]{0,1:T(8,128)(2,1)}, u32[]{:S(2)}, u32[]{:S(2)}) collective-permute-start(bf16[160,640]{0,1:T(8,128)(2,1)} %broadcast_select_fusion.36), channel_id=1, source_target_pairs={{0,2},{2,0},{4,6},{6,4},{1,3},{3,1},{5,7},{7,5},{8,10},{10,8},{12,... | collective-permute-start | bytes 614408 | tf_op jit(solution)/shard_map/ppermute | solution.py:365
  15.0 81.4 %collective-permute-start = (bf16[128,1280]{1,0:T(8,128)(2,1)}, bf16[128,1280]{1,0:T(8,128)(2,1)}, u32[]{:S(2)}, u32[]{:S(2)}) collective-permute-start(bf16[128,1280]{1,0:T(8,128)(2,1)} %pad_maximum_fusion.42), channel_id=1, source_target_pairs={{0,2},{2,0},{4,6},{6,4},{1,3},{3,1},{5,7},{7,5},{8,10},{10,8},{12,... | collective-permute-start | bytes 983048 | tf_op jit(solution)/shard_map/ppermute | solution.py:365
  17.3 81.0 %collective-permute-start.2 = (bf16[128,1280]{1,0:T(8,128)(2,1)}, bf16[128,1280]{1,0:T(8,128)(2,1)}, u32[]{:S(2)}, u32[]{:S(2)}) collective-permute-start(bf16[128,1280]{1,0:T(8,128)(2,1)} %pad_maximum_fusion.43), channel_id=1, source_target_pairs={{0,1},{1,0},{2,3},{3,2},{4,5},{5,4},{6,7},{7,6},{8,9},{9,8},{10,11... | collective-permute-start | bytes 983048 | tf_op jit(solution)/shard_map/ppermute | solution.py:373
  96.3 255.5 %collective-permute-start.37 = (bf16[128,1280]{1,0:T(8,128)(2,1)}, bf16[128,1280]{1,0:T(8,128)(2,1)}, u32[]{:S(2)}, u32[]{:S(2)}) collective-permute-start(bf16[128,1280]{1,0:T(8,128)(2,1)} %pad_maximum_fusion.45), channel_id=1, source_target_pairs={{0,2},{2,0},{4,6},{6,4},{1,3},{3,1},{5,7},{7,5},{8,10},{10,8},{12,... | collective-permute-start | bytes 983048 | tf_op jit(solution)/shard_map/ppermute | solution.py:365
  149.0 102.4 %collective-permute-start.20 = (bf16[320,1728]{1,0:T(8,128)(2,1)}, bf16[320,1728]{1,0:T(8,128)(2,1)}, u32[]{:S(2)}, u32[]{:S(2)}) collective-permute-start(bf16[320,1728]{1,0:T(8,128)(2,1)} %copy.157), channel_id=1, source_target_pairs={{0,4},{2,6},{4,0},{6,2},{1,5},{3,7},{5,1},{7,3},{8,12},{10,14},{12... | collective-permute-start | bytes 3317768 | tf_op jit(solution)/shard_map/ppermute | solution.py:369
  154.8 121.1 %collective-permute-start.26 = (bf16[320,1728]{1,0:T(8,128)(2,1)}, bf16[320,1728]{1,0:T(8,128)(2,1)}, u32[]{:S(2)}, u32[]{:S(2)}) collective-permute-start(bf16[320,1728]{1,0:T(8,128)(2,1)} %copy.165), channel_id=1, source_target_pairs={{0,4},{2,6},{4,0},{6,2},{1,5},{3,7},{5,1},{7,3},{8,12},{10,14},{12... | collective-permute-start | bytes 3317768 | tf_op jit(solution)/shard_map/ppermute | solution.py:369
  192.7 108.7 %collective-permute-start.7 = (bf16[1280,960]{0,1:T(8,128)(2,1)}, bf16[1280,960]{0,1:T(8,128)(2,1)}, u32[]{:S(2)}, u32[]{:S(2)}) collective-permute-start(bf16[1280,960]{0,1:T(8,128)(2,1)} %concatenate.293), channel_id=1, source_target_pairs={{0,8},{8,0},{16,24},{24,16},{1,9},{9,1},{17,25},{25,17},{2,10},{10... | collective-permute-start | bytes 7372808 | tf_op jit(solution)/shard_map/ppermute | solution.py:357
  201.3 94.3 %collective-permute-start.30 = (bf16[320,1728]{1,0:T(8,128)(2,1)}, bf16[320,1728]{1,0:T(8,128)(2,1)}, u32[]{:S(2)}, u32[]{:S(2)}) collective-permute-start(bf16[320,1728]{1,0:T(8,128)(2,1)} %copy.172), channel_id=1, source_target_pairs={{0,4},{2,6},{4,0},{6,2},{1,5},{3,7},{5,1},{7,3},{8,12},{10,14},{12... | collective-permute-start | bytes 3317768 | tf_op jit(solution)/shard_map/ppermute | solution.py:369
  251.3 94.5 %collective-permute-start.14 = (bf16[1280,640]{0,1:T(8,128)(2,1)}, bf16[1280,640]{0,1:T(8,128)(2,1)}, u32[]{:S(2)}, u32[]{:S(2)}) collective-permute-start(bf16[1280,640]{0,1:T(8,128)(2,1)} %concatenate.307), channel_id=1, source_target_pairs={{0,8},{8,0},{16,24},{24,16},{1,9},{9,1},{17,25},{25,17},{2,10},{10... | collective-permute-start | bytes 4915208 | tf_op jit(solution)/shard_map/ppermute | solution.py:357
  275.9 83.8 %collective-permute-start.21 = (bf16[640,1728]{0,1:T(8,128)(2,1)}, bf16[640,1728]{0,1:T(8,128)(2,1)}, u32[]{:S(2)}, u32[]{:S(2)}) collective-permute-start(bf16[640,1728]{0,1:T(8,128)(2,1)} %pad_maximum_fusion), channel_id=1, source_target_pairs={{0,16},{8,24},{16,0},{24,8},{1,17},{9,25},{17,1},{25,9},{2,18},{10... | collective-permute-start | bytes 6635528 | tf_op jit(solution)/shard_map/ppermute | solution.py:361
  295.6 79.0 %collective-permute-start.27 = (bf16[640,1728]{0,1:T(8,128)(2,1)}, bf16[640,1728]{0,1:T(8,128)(2,1)}, u32[]{:S(2)}, u32[]{:S(2)}) collective-permute-start(bf16[640,1728]{0,1:T(8,128)(2,1)} %pad_maximum_fusion.1), channel_id=1, source_target_pairs={{0,16},{8,24},{16,0},{24,8},{1,17},{9,25},{17,1},{25,9},{2,18},{10... | collective-permute-start | bytes 6635528 | tf_op jit(solution)/shard_map/ppermute | solution.py:361
  317.2 94.1 %collective-permute-start.31 = (bf16[640,1728]{0,1:T(8,128)(2,1)}, bf16[640,1728]{0,1:T(8,128)(2,1)}, u32[]{:S(2)}, u32[]{:S(2)}) collective-permute-start(bf16[640,1728]{0,1:T(8,128)(2,1)} %pad_maximum_fusion.2), channel_id=1, source_target_pairs={{0,16},{8,24},{16,0},{24,8},{1,17},{9,25},{17,1},{25,9},{2,18},{10... | collective-permute-start | bytes 6635528 | tf_op jit(solution)/shard_map/ppermute | solution.py:361
  345.8 73.6 %collective-permute-start.12 = (bf16[256,1280]{1,0:T(8,128)(2,1)}, bf16[256,1280]{1,0:T(8,128)(2,1)}, u32[]{:S(2)}, u32[]{:S(2)}) collective-permute-start(bf16[256,1280]{1,0:T(8,128)(2,1)} %pad_maximum_fusion.23), channel_id=1, source_target_pairs={{0,1},{1,0},{2,3},{3,2},{4,5},{5,4},{6,7},{7,6},{8,9},{9,8},{10,11... | collective-permute-start | bytes 1966088 | tf_op jit(solution)/shard_map/ppermute | solution.py:373
  351.9 69.3 %collective-permute-start.15 = (bf16[256,1280]{1,0:T(8,128)(2,1)S(1)}, bf16[256,1280]{1,0:T(8,128)(2,1)}, u32[]{:S(2)}, u32[]{:S(2)}) collective-permute-start(bf16[256,1280]{1,0:T(8,128)(2,1)S(1)} %slice.493), channel_id=1, source_target_pairs={{0,2},{2,0},{4,6},{6,4},{1,3},{3,1},{5,7},{7,5},{8,10},{10,8},{12,... | collective-permute-start | bytes 1966088 | tf_op jit(solution)/shard_map/ppermute | solution.py:365
  359.7 84.0 %collective-permute-start.39 = (bf16[128,1280]{1,0:T(8,128)(2,1)}, bf16[128,1280]{1,0:T(8,128)(2,1)}, u32[]{:S(2)}, u32[]{:S(2)}) collective-permute-start(bf16[128,1280]{1,0:T(8,128)(2,1)} %pad_maximum_fusion.46), channel_id=1, source_target_pairs={{0,1},{1,0},{2,3},{3,2},{4,5},{5,4},{6,7},{7,6},{8,9},{9,8},{10,11... | collective-permute-start | bytes 983048 | tf_op jit(solution)/shard_map/ppermute | solution.py:373
  374.6 80.8 %collective-permute-start.38 = (bf16[256,1280]{1,0:T(8,128)(2,1)}, bf16[256,1280]{1,0:T(8,128)(2,1)}, u32[]{:S(2)}, u32[]{:S(2)}) collective-permute-start(bf16[256,1280]{1,0:T(8,128)(2,1)} %pad_maximum_fusion.28), channel_id=1, source_target_pairs={{0,1},{1,0},{2,3},{3,2},{4,5},{5,4},{6,7},{7,6},{8,9},{9,8},{10,11... | collective-permute-start | bytes 1966088 | tf_op jit(solution)/shard_map/ppermute | solution.py:373
  411.4 67.7 %collective-permute-start.24 = (bf16[1280,1728]{0,1:T(8,128)(2,1)}, bf16[1280,1728]{0,1:T(8,128)(2,1)}, u32[]{:S(2)}, u32[]{:S(2)}) collective-permute-start(bf16[1280,1728]{0,1:T(8,128)(2,1)} %concatenate.314), channel_id=1, source_target_pairs={{0,8},{8,0},{16,24},{24,16},{1,9},{9,1},{17,25},{25,17},{2,10},{10... | collective-permute-start | bytes 13271048 | tf_op jit(solution)/shard_map/ppermute | solution.py:357
  419.4 66.2 %collective-permute-start.28 = (bf16[1280,1728]{0,1:T(8,128)(2,1)}, bf16[1280,1728]{0,1:T(8,128)(2,1)}, u32[]{:S(2)}, u32[]{:S(2)}) collective-permute-start(bf16[1280,1728]{0,1:T(8,128)(2,1)} %concatenate.319), channel_id=1, source_target_pairs={{0,8},{8,0},{16,24},{24,16},{1,9},{9,1},{17,25},{25,17},{2,10},{10... | collective-permute-start | bytes 13271048 | tf_op jit(solution)/shard_map/ppermute | solution.py:357
  547.1 240.7 %collective-permute-start.66 = (bf16[1280,1728]{0,1:T(8,128)(2,1)}, bf16[1280,1728]{0,1:T(8,128)(2,1)}, u32[]{:S(2)}, u32[]{:S(2)}) collective-permute-start(bf16[1280,1728]{0,1:T(8,128)(2,1)} %convolution_convert_fusion.2), channel_id=1, source_target_pairs={{0,8},{8,0},{16,24},{24,16},{1,9},{9,1},{17,25},{25,17},{2,10},{10... | collective-permute-start | bytes 13271048 | tf_op jit(solution)/shard_map/ppermute | solution.py:357
  567.5 242.7 %collective-permute-start.70 = (bf16[1280,1728]{0,1:T(8,128)(2,1)}, bf16[1280,1728]{0,1:T(8,128)(2,1)}, u32[]{:S(2)}, u32[]{:S(2)}) collective-permute-start(bf16[1280,1728]{0,1:T(8,128)(2,1)} %convolution_convert_fusion), channel_id=1, source_target_pairs={{0,8},{8,0},{16,24},{24,16},{1,9},{9,1},{17,25},{25,17},{2,10},{10... | collective-permute-start | bytes 13271048 | tf_op jit(solution)/shard_map/ppermute | solution.py:357
  568.1 316.3 %collective-permute-start.62 = (bf16[1280,1728]{0,1:T(8,128)(2,1)}, bf16[1280,1728]{0,1:T(8,128)(2,1)}, u32[]{:S(2)}, u32[]{:S(2)}) collective-permute-start(bf16[1280,1728]{0,1:T(8,128)(2,1)} %convolution_convert_fusion.4), channel_id=1, source_target_pairs={{0,8},{8,0},{16,24},{24,16},{1,9},{9,1},{17,25},{25,17},{2,10},{10... | collective-permute-start | bytes 13271048 | tf_op jit(solution)/shard_map/ppermute | solution.py:357
  694.7 67.6 %collective-permute-start.50 = (bf16[256,1280]{1,0:T(8,128)(2,1)}, bf16[256,1280]{1,0:T(8,128)(2,1)}, u32[]{:S(2)}, u32[]{:S(2)}) collective-permute-start(bf16[256,1280]{1,0:T(8,128)(2,1)} %pad_maximum_fusion.34), channel_id=1, source_target_pairs={{0,1},{1,0},{2,3},{3,2},{4,5},{5,4},{6,7},{7,6},{8,9},{9,8},{10,11... | collective-permute-start | bytes 1966088 | tf_op jit(solution)/shard_map/ppermute | solution.py:373
  791.5 126.1 %collective-permute-start.67 = (bf16[640,1728]{0,1:T(8,128)(2,1)}, bf16[640,1728]{0,1:T(8,128)(2,1)}, u32[]{:S(2)}, u32[]{:S(2)}) collective-permute-start(bf16[640,1728]{0,1:T(8,128)(2,1)} %add_convert_fusion.3), channel_id=1, source_target_pairs={{0,16},{8,24},{16,0},{24,8},{1,17},{9,25},{17,1},{25,9},{2,18},{10... | collective-permute-start | bytes 6635528 | tf_op jit(solution)/shard_map/ppermute | solution.py:361
  793.3 88.7 %collective-permute-start.55 = (bf16[640,960]{0,1:T(8,128)(2,1)S(1)}, bf16[640,960]{0,1:T(8,128)(2,1)S(1)}, u32[]{:S(2)}, u32[]{:S(2)}) collective-permute-start(bf16[640,960]{0,1:T(8,128)(2,1)S(1)} %add_convert_fusion.10), channel_id=1, source_target_pairs={{0,16},{8,24},{16,0},{24,8},{1,17},{9,25},{17,1},{25,9},{2,18},{10... | collective-permute-start | bytes 3686408 | tf_op jit(solution)/shard_map/ppermute | solution.py:361
  813.8 115.7 %collective-permute-start.71 = (bf16[640,1728]{0,1:T(8,128)(2,1)}, bf16[640,1728]{0,1:T(8,128)(2,1)}, u32[]{:S(2)}, u32[]{:S(2)}) collective-permute-start(bf16[640,1728]{0,1:T(8,128)(2,1)} %add_convert_fusion.1), channel_id=1, source_target_pairs={{0,16},{8,24},{16,0},{24,8},{1,17},{9,25},{17,1},{25,9},{2,18},{10... | collective-permute-start | bytes 6635528 | tf_op jit(solution)/shard_map/ppermute | solution.py:361
  888.7 87.9 %collective-permute-start.63 = (bf16[640,1728]{0,1:T(8,128)(2,1)}, bf16[640,1728]{0,1:T(8,128)(2,1)}, u32[]{:S(2)}, u32[]{:S(2)}) collective-permute-start(bf16[640,1728]{0,1:T(8,128)(2,1)} %add_convert_fusion.5), channel_id=1, source_target_pairs={{0,16},{8,24},{16,0},{24,8},{1,17},{9,25},{17,1},{25,9},{2,18},{10... | collective-permute-start | bytes 6635528 | tf_op jit(solution)/shard_map/ppermute | solution.py:361
  914.9 69.7 %collective-permute-start.57 = (bf16[160,960]{0,1:T(8,128)(2,1)}, bf16[160,960]{0,1:T(8,128)(2,1)}, u32[]{:S(2)}, u32[]{:S(2)}) collective-permute-start(bf16[160,960]{0,1:T(8,128)(2,1)} %constant_dynamic-slice_fusion.8), channel_id=1, source_target_pairs={{0,2},{2,0},{4,6},{6,4},{1,3},{3,1},{5,7},{7,5},{8,10},{10,8},{12,... | collective-permute-start | bytes 921608 | tf_op jit(solution)/shard_map/ppermute | solution.py:365
  926.2 99.8 %collective-permute-start.68 = (bf16[320,1728]{1,0:T(8,128)(2,1)}, bf16[320,1728]{1,0:T(8,128)(2,1)}, u32[]{:S(2)}, u32[]{:S(2)}) collective-permute-start(bf16[320,1728]{1,0:T(8,128)(2,1)} %copy.188), channel_id=1, source_target_pairs={{0,4},{2,6},{4,0},{6,2},{1,5},{3,7},{5,1},{7,3},{8,12},{10,14},{12... | collective-permute-start | bytes 3317768 | tf_op jit(solution)/shard_map/ppermute | solution.py:369
  937.7 113.0 %collective-permute-start.72 = (bf16[320,1728]{1,0:T(8,128)(2,1)}, bf16[320,1728]{1,0:T(8,128)(2,1)}, u32[]{:S(2)}, u32[]{:S(2)}) collective-permute-start(bf16[320,1728]{1,0:T(8,128)(2,1)} %copy.193), channel_id=1, source_target_pairs={{0,4},{2,6},{4,0},{6,2},{1,5},{3,7},{5,1},{7,3},{8,12},{10,14},{12... | collective-permute-start | bytes 3317768 | tf_op jit(solution)/shard_map/ppermute | solution.py:369
  983.3 90.7 %collective-permute-start.64 = (bf16[320,1728]{1,0:T(8,128)(2,1)}, bf16[320,1728]{1,0:T(8,128)(2,1)}, u32[]{:S(2)}, u32[]{:S(2)}) collective-permute-start(bf16[320,1728]{1,0:T(8,128)(2,1)} %copy.183), channel_id=1, source_target_pairs={{0,4},{2,6},{4,0},{6,2},{1,5},{3,7},{5,1},{7,3},{8,12},{10,14},{12... | collective-permute-start | bytes 3317768 | tf_op jit(solution)/shard_map/ppermute | solution.py:369
  (188 other events, 3735.7 us)
Sparse Core Ops, SparseCore 0:
  698.0 57.5 reduce-scatter.3

commit v2 on v0

--- a/solution.py
+++ b/solution.py
@@ -1,8 +1,11 @@
+import functools
 import math
 
 import jax
 import jax.numpy as jnp
 from jax import lax
+from jax.experimental import pallas as pl
+from jax.experimental.pallas import tpu as pltpu
 from jax.sharding import PartitionSpec as P
 
 D = 2560
@@ -353,7 +356,684 @@
     )
 
 
+def to_core(value):
+    return lax.ppermute(value, "fsdp", [(i, i ^ 1) for i in range(4)])
+
+
+def to_x(value):
+    return lax.ppermute(value, "fsdp", [(i, i ^ 2) for i in range(4)])
+
+
+def to_z(value, step):
+    return lax.ppermute(value, "seq", [(i, i ^ step) for i in range(4)])
+
+
+def to_tp(value):
+    return lax.ppermute(value, "tp", [(0, 1), (1, 0)])
+
+
+def hold(value, *events):
+    return lax.optimization_barrier((value, events))[0]
+
+
+def float_of(value):
+    return value.astype(jnp.float32)
+
+
+def low_of(value):
+    return value.astype(jnp.bfloat16)
+
+
+def rows_dot(left, right):
+    return lax.dot_general(left, right, (((0,), (0,)), ((), ())), preferred_element_type=jnp.float32)
+
+
+def cols_dot(left, right):
+    return lax.dot_general(left, right, (((1,), (1,)), ((), ())), preferred_element_type=jnp.float32)
+
+
+def wide_dot(left, pieces):
+    depth = pieces[0].shape[0]
+    return sum(
+        jnp.dot(left[:, i * depth : (i + 1) * depth], piece, preferred_element_type=jnp.float32)
+        for i, piece in enumerate(pieces)
+    )
+
+
+def place_kernel(rows, place, one, two, three, four, plane, mine, held, read_sems, sems):
+    reads = [
+        pltpu.make_async_copy(piece, held.at[k], read_sems.at[k])
+        for k, piece in enumerate((one, two, three, four))
+    ]
+    for copy in reads:
+        copy.start()
+    writes = []
+    for k, read in enumerate(reads):
+        read.wait()
+        start = pl.multiple_of((place[0] ^ k) * rows, 16)
+        for i, target in enumerate((plane, mine)):
+            write = pltpu.make_async_copy(
+                held.at[k], target.at[pl.ds(start, rows), :], sems.at[2 * k + i]
+            )
+            write.start()
+            writes.append(write)
+    for write in writes:
+        write.wait()
+
+
+def place_rows(pieces, place):
+    rows, columns = pieces[0].shape
+    anywhere = pl.BlockSpec(memory_space=pl.ANY)
+    return pl.pallas_call(
+        lambda *refs: place_kernel(rows, *refs),
+        out_shape=(
+            jax.ShapeDtypeStruct((4 * rows, columns), jnp.bfloat16),
+            jax.ShapeDtypeStruct((8 * rows, columns), jnp.bfloat16),
+        ),
+        in_specs=[pl.BlockSpec(memory_space=pltpu.SMEM)] + [anywhere] * 4,
+        out_specs=(anywhere, anywhere),
+        scratch_shapes=[
+            pltpu.VMEM((4, rows, columns), jnp.bfloat16),
+            pltpu.SemaphoreType.DMA((4,)),
+            pltpu.SemaphoreType.DMA((8,)),
+        ],
+        cost_estimate=pl.CostEstimate(
+            flops=0, bytes_accessed=24 * rows * columns, transcendentals=0
+        ),
+        name="place_rows",
+    )(place.reshape(1), *pieces)
+
+
+def fill_kernel(rows, across, first, mine, held, read_sems, sems):
+    part = rows // 4
+    reads = [
+        pltpu.make_async_copy(across.at[pl.ds(k * part, part), :], held.at[k], read_sems.at[k])
+        for k in range(4)
+    ]
+    for copy in reads:
+        copy.start()
+    writes = []
+    for k, read in enumerate(reads):
+        read.wait()
+        write = pltpu.make_async_copy(
+            held.at[k], mine.at[pl.ds(rows + k * part, part), :], sems.at[k]
+        )
+        write.start()
+        writes.append(write)
+    for write in writes:
+        write.wait()
+
+
+def fill_rows(mine, across):
+    rows, columns = across.shape
+    anywhere = pl.BlockSpec(memory_space=pl.ANY)
+    return pl.pallas_call(
+        lambda *refs: fill_kernel(rows, *refs),
+        out_shape=jax.ShapeDtypeStruct(mine.shape, mine.dtype),
+        in_specs=[anywhere] * 2,
+        out_specs=anywhere,
+        scratch_shapes=[
+            pltpu.VMEM((4, rows // 4, columns), jnp.bfloat16),
+            pltpu.SemaphoreType.DMA((4,)),
+            pltpu.SemaphoreType.DMA((4,)),
+        ],
+        input_output_aliases={1: 0},
+        cost_estimate=pl.CostEstimate(flops=0, bytes_accessed=4 * rows * columns, transcendentals=0),
+        name="fill_rows",
+    )(across, mine)
+
+
+VMEM_BYTES = 40 * 1024 * 1024
+
+
+def take_rows_kernel(own, one_near, one_far, two_tp, two_far, out, sems):
+    n = own.shape[0]
+    half = own.shape[1] // 2
+    left, right = pl.ds(0, half), pl.ds(half, half)
+    moves = [
+        (own, pl.ds(0, n), pl.ds(0, 2 * half)),
+        (one_near, pl.ds(2 * n, n), left),
+        (one_far.at[pl.ds(0, n), :], pl.ds(n, n), left),
+        (one_far.at[pl.ds(n, n), :], pl.ds(3 * n, n), left),
+        (two_tp, pl.ds(n, n), right),
+        (two_far, pl.ds(2 * n, 2 * n), right),
+    ]
+    copies = [
+        pltpu.make_async_copy(source, out.at[rows, columns], sems.at[k])
+        for k, (source, rows, columns) in enumerate(moves)
+    ]
+    for copy in copies:
+        copy.start()
+    for copy in copies:
+        copy.wait()
+
+
+def take_rows(own, *received):
+    shape = (4 * own.shape[0], own.shape[1])
+    return pl.pallas_call(
+        take_rows_kernel,
+        out_shape=jax.ShapeDtypeStruct(shape, own.dtype),
+        in_specs=[pl.BlockSpec(memory_space=pl.ANY)] * 5,
+        out_specs=pl.BlockSpec(memory_space=pltpu.VMEM),
+        scratch_shapes=[pltpu.SemaphoreType.DMA((6,))],
+        compiler_params=pltpu.CompilerParams(vmem_limit_bytes=VMEM_BYTES),
+        cost_estimate=pl.CostEstimate(flops=0, bytes_accessed=4096, transcendentals=0),
+        name="take_rows",
+    )(own, *received)
+
+
+def dense_call(kernel, name, outs, scratch, args):
+    whole = pl.BlockSpec(memory_space=pltpu.VMEM)
+    return pl.pallas_call(
+        kernel,
+        out_shape=[jax.ShapeDtypeStruct(shape, kind) for shape, kind in outs],
+        in_specs=[whole] * len(args),
+        out_specs=[whole] * len(outs),
+        scratch_shapes=scratch,
+        compiler_params=pltpu.CompilerParams(vmem_limit_bytes=VMEM_BYTES),
+        cost_estimate=pl.CostEstimate(flops=1024, bytes_accessed=4096, transcendentals=0),
+        name=name,
+    )(*args)
+
+
+def turned(value, cos_wide, sin_wide):
+    half = HEAD_DIM // 2
+    swapped = jnp.concatenate([value[:, half:], value[:, :half]], axis=1)
+    return value * cos_wide + swapped * sin_wide
+
+
+def rope_kernel(raw, cos_wide, sin_wide, query, kv):
+    cos, sin = cos_wide[...], sin_wide[...]
+    query_width, kv_width = query.shape[1], kv.shape[1] // 2
+    for start in range(0, query_width, HEAD_DIM):
+        columns = slice(start, start + HEAD_DIM)
+        query[:, columns] = turned(raw[:, columns], cos, sin).astype(jnp.bfloat16)
+    for start in range(0, kv_width, HEAD_DIM):
+        columns = slice(query_width + start, query_width + start + HEAD_DIM)
+        kv[:, start : start + HEAD_DIM] = turned(raw[:, columns], cos, sin).astype(jnp.bfloat16)
+    values = raw[:, query_width + kv_width : query_width + 2 * kv_width]
+    kv[:, kv_width:] = values.astype(jnp.bfloat16)
+
+
+def pair_of(early, own, index):
+    columns = slice(index * HEAD_DIM, (index + 1) * HEAD_DIM)
+    return jnp.concatenate([early[:, columns], own[:, columns]], axis=0)
+
+
+def attend_kernel(scale, query, early, own, query_ids, key_ids, attended, log_total, fill):
+    kv_local = own.shape[1] // HEAD_DIM // 2
+    rows_total = query.shape[0]
+    half_rows = rows_total // 2
+    for part in range(2):
+        rows = slice(part * half_rows, (part + 1) * half_rows)
+        allowed = (key_ids[:, 0:1] == query_ids[0:1, rows]) & (
+            key_ids[:, 1:2] <= query_ids[1:2, rows]
+        )
+        fill[...] = jnp.where(allowed, 0.0, mask_fill)
+        for kv in range(kv_local):
+            keys = pair_of(early, own, kv)
+            values = pair_of(early, own, kv_local + kv)
+            for member in range(GROUP):
+                head = kv * GROUP + member
+                columns = slice(head * HEAD_DIM, (head + 1) * HEAD_DIM)
+                scores = cols_dot(keys, query[rows, columns]) + fill[...]
+                top = jnp.max(scores, axis=0, keepdims=True)
+                weights = jnp.exp((scores - top) * scale)
+                total = jnp.sum(weights, axis=0, keepdims=True)
+                probs = (weights * (1.0 / total)).astype(jnp.bfloat16)
+                attended[rows, columns] = rows_dot(values, probs).T.astype(jnp.bfloat16)
+                log_total[head : head + 1, rows] = top * scale + jnp.log(total)
+
+
+def attend_back_kernel(
+    scale,
+    query,
+    early,
+    own,
+    query_ids,
+    key_ids,
+    log_total,
+    grad_attended,
+    cos_wide,
+    sin_wide,
+    grad_query,
+    grad_early,
+    grad_own,
+    fill,
+    all_probs,
+    all_grads,
+):
+    kv_local = own.shape[1] // HEAD_DIM // 2
+    rows_total = query.shape[0]
+    half_rows = rows_total // 2
+    for part in range(2):
+        rows = slice(part * half_rows, (part + 1) * half_rows)
+        allowed = (key_ids[:, 0:1] == query_ids[0:1, rows]) & (
+            key_ids[:, 1:2] <= query_ids[1:2, rows]
+        )
+        fill[:, rows] = jnp.where(allowed, 0.0, mask_fill)
+    for kv in range(kv_local):
+        keys = pair_of(early, own, kv)
+        values = pair_of(early, own, kv_local + kv)
+        queries, outs = [], []
+        for part in range(2):
+            rows = slice(part * half_rows, (part + 1) * half_rows)
+            cos, sin = cos_wide[rows, :], -sin_wide[rows, :]
+            for member in range(GROUP):
+                head = kv * GROUP + member
+                columns = slice(head * HEAD_DIM, (head + 1) * HEAD_DIM)
+                place = (part * GROUP + member) * half_rows
+                where = slice(place, place + half_rows)
+                one_query, one_out = query[rows, columns], grad_attended[rows, columns]
+                queries.append(one_query)
+                outs.append(one_out)
+                scores = cols_dot(keys, one_query) + fill[:, rows]
+                probs = jnp.exp(scores * scale - log_total[head : head + 1, rows])
+                grad_probs = cols_dot(values, one_out)
+                delta = jnp.sum(probs * grad_probs, axis=0, keepdims=True)
+                grads = (probs * (grad_probs - delta)).astype(jnp.bfloat16)
+                all_probs[:, where] = probs.astype(jnp.bfloat16)
+                all_grads[:, where] = grads
+                turned_grad = rows_dot(keys, grads).T * scale
+                grad_query[rows, columns] = turned(turned_grad, cos, sin).astype(jnp.bfloat16)
+        grad_keys = (
+            jnp.dot(
+                all_grads[...], jnp.concatenate(queries, axis=0), preferred_element_type=jnp.float32
+            )
+            * scale
+        )
+        grad_values = jnp.dot(
+            all_probs[...], jnp.concatenate(outs, axis=0), preferred_element_type=jnp.float32
+        )
+        for start, grad in ((kv, grad_keys), (kv_local + kv, grad_values)):
+            columns = slice(start * HEAD_DIM, (start + 1) * HEAD_DIM)
+            grad_early[:, columns] = grad[:rows_total].astype(jnp.bfloat16)
+            grad_own[:, columns] = grad[rows_total:]
+
+
+def join_kernel(grad_query, grad_own, late, cos_wide, sin_wide, grad_raw):
+    cos, sin = cos_wide[...], -sin_wide[...]
+    query_width, kv_width = grad_query.shape[1], grad_own.shape[1] // 2
+    grad_raw[:, :query_width] = grad_query[...]
+    for start in range(0, kv_width, HEAD_DIM):
+        columns = slice(start, start + HEAD_DIM)
+        grad = grad_own[:, columns] + late[:, columns].astype(jnp.float32)
+        grad_raw[:, query_width + start : query_width + start + HEAD_DIM] = turned(
+            grad, cos, sin
+        ).astype(jnp.bfloat16)
+    values = grad_own[:, kv_width:] + late[:, kv_width:].astype(jnp.float32)
+    used = query_width + 2 * kv_width
+    grad_raw[:, query_width + kv_width : used] = values.astype(jnp.bfloat16)
+    spare = grad_raw.shape[1] - used
+    grad_raw[:, used:] = jnp.zeros((grad_raw.shape[0], spare), jnp.bfloat16)
+
+
+def half_plan(
+    tokens, doc_lengths, w_query, w_key, w_value, w_out, w_gate, w_up, w_down, norm_gains, cotangent
+):
+    fsdp_index = lax.axis_index("fsdp")
+    seq_index = lax.axis_index("seq")
+    tp_index = lax.axis_index("tp")
+    near = seq_index % 2
+    far = seq_index // 2
+    local_rows = tokens.shape[0]
+    group_rows = 4 * local_rows
+    middle = D // 2
+    quarter = D // 4
+    block_rows = D // 16
+    score_scale = 1.0 / math.sqrt(HEAD_DIM)
+
+    def columns_in(value):
+        return jnp.concatenate(
+            [
+                lax.dynamic_slice_in_dim(value, (fsdp_index ^ k) * quarter, quarter, 1)
+                for k in (0, 2, 1, 3)
+            ],
+            axis=1,
+        )
+
+    def columns_out(value):
+        pieces = []
+        for block in range(4):
+            k = fsdp_index ^ block
+            place = (k // 2) + (k % 2) * 2
+            pieces.append(lax.dynamic_slice_in_dim(value, place * quarter, quarter, 1))
+        return jnp.concatenate(pieces, axis=1)
+
+    def both_halves(array, size):
+        low_part = array[:, :size]
+        high_part = array[:, size:]
+        high_part = jnp.pad(high_part, ((0, 0), (0, size - high_part.shape[1])))
+        first = near == 0
+        return jnp.where(first, low_part, high_part), jnp.where(first, high_part, low_part)
+
+    def z_stage(halves):
+        own, other = halves
+        return own, to_z(other, 1), to_z(own, 2), to_z(other, 3)
+
+    def joined(own, received, width):
+        first = near == 0
+        size = own.shape[1]
+        low_part = jnp.where(first, own, received)
+        high_part = jnp.where(first, received, own)[:, : width - size]
+        return jnp.concatenate([low_part, high_part], axis=1)
+
+    def gather_rows(value):
+        half = value.shape[1] // 2
+        one, two = value[:, :half], value[:, half:]
+        one_near, two_tp = to_z(one, 1), to_tp(two)
+        one_far = to_tp(jnp.concatenate([one, one_near], axis=0))
+        two_far = to_z(jnp.concatenate([two, two_tp], axis=0), 1)
+        return value, one_near, one_far, two_tp, two_far
+
+    def scatter_start(one, two):
+        n = local_rows
+        send_one = jnp.concatenate([one[n : 2 * n], one[3 * n :]], axis=0)
+        return one, two, to_tp(send_one), to_z(two[2 * n :], 1)
+
+    def scatter_end(one, two, got_one, got_two):
+        n = local_rows
+        next_one = low_of(float_of(one[2 * n : 3 * n]) + float_of(got_one[n:]))
+        next_two = low_of(float_of(two[n : 2 * n]) + float_of(got_two[n:]))
+        last_one = to_z(next_one, 1)
+        last_two = to_tp(next_two)
+        sum_one = float_of(one[:n]) + float_of(got_one[:n]) + float_of(last_one)
+        sum_two = float_of(two[:n]) + float_of(got_two[:n]) + float_of(last_two)
+        return jnp.concatenate([sum_one, sum_two], axis=1)
+
+    def grad_pair(left, right):
+        other = low_of(rows_dot(left[:, middle:], right))
+        from_core = to_core(other)
+        return low_of(rows_dot(left[:, :middle], right)), from_core
+
+    def x_send(mine, from_core):
+        return low_of(float_of(mine[quarter:]) + float_of(from_core[quarter:]))
+
+    def z_pieces(mine, from_core, from_x):
+        total = low_of(
+            float_of(mine[:quarter]) + float_of(from_core[:quarter]) + float_of(from_x)
+        )
+        return [
+            lax.dynamic_slice_in_dim(total, (seq_index ^ k) * block_rows, block_rows, 0)
+            for k in range(4)
+        ]
+
+    def z_send(pieces):
+        return pieces[0], to_z(pieces[1], 1), to_z(pieces[2], 2), to_z(pieces[3], 3)
+
+    def z_sum(own, from_near, from_far, from_last, width):
+        return joined(
+            float_of(own) + float_of(from_far), float_of(from_near) + float_of(from_last), width
+        )
+
+    query_width = w_query.shape[1] // 2
+    key_width = w_key.shape[1] // 2
+    kv_local = key_width // HEAD_DIM
+    query_heads = query_width // HEAD_DIM
+    heads_width = -(-(query_width + 2 * key_width) // 128) * 128
+    hidden_width = -(-(w_gate.shape[1] // 2) // 128) * 128
+    heads_parts = [
+        both_halves(w_query, query_width),
+        both_halves(w_key, key_width),
+        both_halves(w_value, key_width),
+    ]
+    spare = heads_width - query_width - 2 * key_width
+    heads_halves = [
+        jnp.pad(jnp.concatenate([part[i] for part in heads_parts], axis=1), ((0, 0), (0, spare)))
+        for i in range(2)
+    ]
+    gain_stack = norm_gains[None]
+    for step in (1, 2):
+        gain_stack = jnp.concatenate([gain_stack, to_z(gain_stack, step)], axis=0)
+    gain_plane = jnp.concatenate(
+        [
+            lax.dynamic_index_in_dim(gain_stack, seq_index ^ k, 0, keepdims=False)
+            for k in range(4)
+        ],
+        axis=1,
+    )
+    gain_mine = jnp.concatenate([gain_plane, to_x(gain_plane)], axis=1)
+    gains = float_of(jnp.concatenate([gain_mine, to_core(gain_mine)], axis=1))
+    gain_one = gains[0]
+    gain_two = gains[1]
+    heads_z = z_stage(heads_halves)
+    tokens_in = columns_in(tokens)
+    token_rows = float_of(tokens_in)
+    inv_one = rms_scale(token_rows)
+    heads_plane, heads_mine = place_rows(hold(heads_z, gain_stack), seq_index)
+    heads_x = to_x(heads_plane)
+    normed_rows = low_of(token_rows * inv_one * gain_one)
+    normed_wait = gather_rows(hold(normed_rows, heads_plane))
+    out_z = z_stage(hold(both_halves(w_out.T, query_width), heads_z[1]))
+    gate_z = z_stage(hold(both_halves(w_gate, hidden_width), heads_z[2:]))
+    up_z = z_stage(hold(both_halves(w_up, hidden_width), out_z[2:]))
+    down_z = z_stage(hold(both_halves(w_down.T, hidden_width), gate_z[2:]))
+    out_plane, out_mine = place_rows(hold(out_z, normed_rows), seq_index)
+
+    row_ids = jnp.arange(local_rows, dtype=jnp.int32)
+    own_positions = jnp.concatenate(
+        [
+            far * (2 * 2 * local_rows)
+            + (near ^ i) * (2 * local_rows)
+            + (tp_index ^ j) * local_rows
+            + row_ids
+            for i in range(2)
+            for j in range(2)
+        ]
+    )
+    cos_tab, sin_tab = rope_tables(own_positions)
+    cos_wide = jnp.concatenate([cos_tab, cos_tab], axis=1)
+    sin_wide = jnp.concatenate([-sin_tab, sin_tab], axis=1)
+    key_positions = jnp.concatenate([own_positions - group_rows, own_positions])
+    doc_ends = jnp.cumsum(doc_lengths[0])[: DOCS - 1]
+
+    def doc_of(positions):
+        return jnp.sum((positions[:, None] >= doc_ends[None, :]).astype(jnp.int32), axis=1)
+
+    key_docs = jnp.where(key_positions >= 0, doc_of(key_positions), -1)
+    query_ids = jnp.stack([doc_of(own_positions), own_positions // BLOCK])
+    key_ids = jnp.stack([key_docs, key_positions // BLOCK], axis=1)
+
+    heads_mine = fill_rows(*hold((heads_mine, heads_x), out_plane))
+    heads_weights = heads_mine, to_core(heads_mine)
+    out_x = to_x(out_plane)
+    normed_one = take_rows(*hold(normed_wait, heads_mine))
+    cot_in = columns_in(cotangent)
+    cot_wait = gather_rows(hold(cot_in, normed_one))
+    gate_plane, gate_mine = place_rows(hold(gate_z, heads_mine), seq_index)
+    gate_x = to_x(gate_plane)
+    raw = wide_dot(hold(normed_one, gate_plane), heads_weights)
+    query_rot, own_kv = dense_call(
+        rope_kernel,
+        "rope",
+        [
+            ((group_rows, query_width), jnp.bfloat16),
+            ((group_rows, 2 * key_width), jnp.bfloat16),
+        ],
+        [],
+        (raw, cos_wide, sin_wide),
+    )
+    early_kv = lax.ppermute(own_kv, "seq", [(0, 2), (1, 3)])
+    out_mine = fill_rows(*hold((out_mine, out_x), own_kv))
+    out_weights = out_mine, to_core(out_mine)
+    cot_span = take_rows(*hold(cot_wait, out_mine))
+    query_rot = hold(query_rot, cot_span)
+    attended_low, log_total = dense_call(
+        functools.partial(attend_kernel, score_scale),
+        "attend",
+        [
+            ((group_rows, query_width), jnp.bfloat16),
+            ((query_heads, group_rows), jnp.float32),
+        ],
+        [pltpu.VMEM((2 * group_rows, group_rows // 2), jnp.float32)],
+        (query_rot, early_kv, own_kv, query_ids, key_ids),
+    )
+    up_plane, up_mine = place_rows(hold(up_z, log_total), seq_index)
+    up_x = to_x(up_plane)
+    branch = scatter_start(
+        *[low_of(cols_dot(hold(attended_low, up_plane), w)) for w in out_weights]
+    )
+    gate_mine = fill_rows(*hold((gate_mine, gate_x), branch[:2]))
+    gate_weights = gate_mine, to_core(gate_mine)
+    attn_branch = scatter_end(*hold(branch, gate_mine))
+    residual = token_rows + attn_branch
+    inv_two = rms_scale(residual)
+    normed_two = low_of(residual * inv_two * gain_two)
+    two_wait = gather_rows(normed_two)
+    down_plane, down_mine = place_rows(hold(down_z, normed_two), seq_index)
+    down_x = to_x(down_plane)
+    up_mine = fill_rows(*hold((up_mine, up_x), down_plane))
+    up_weights = up_mine, to_core(up_mine)
+    span_two = take_rows(*hold(two_wait, up_mine))
+    gate_pre = wide_dot(span_two, gate_weights)
+    up_pre = wide_dot(span_two, up_weights)
+    sig_gate = jax.nn.sigmoid(gate_pre)
+    silu_gate = gate_pre * sig_gate
+    hidden_low = low_of(silu_gate * up_pre)
+    down_pair = grad_pair(cot_span, hidden_low)
+    down_send = x_send(*down_pair)
+    down_back = to_x(down_send)
+    down_mine = fill_rows(*hold((down_mine, down_x), down_send))
+    down_weights = down_mine, to_core(down_mine)
+    grad_hidden = wide_dot(cot_span, down_weights)
+    grad_gate_pre = low_of(grad_hidden * up_pre * (sig_gate * (1.0 + gate_pre * (1.0 - sig_gate))))
+    grad_up_pre = low_of(grad_hidden * silu_gate)
+    normed_back = scatter_start(
+        *[
+            low_of(cols_dot(grad_gate_pre, gate_w) + cols_dot(grad_up_pre, up_w))
+            for gate_w, up_w in zip(gate_weights, up_weights)
+        ]
+    )
+    gate_pair = grad_pair(hold(span_two, normed_back[:2]), grad_gate_pre)
+    up_pair = grad_pair(hold(span_two, gate_pair[0]), grad_up_pre)
+    gate_send = x_send(*hold(gate_pair, up_pair[0]))
+    gate_back = to_x(gate_send)
+    down_pieces = z_pieces(*hold((*down_pair, down_back), gate_send))
+    down_done = z_send(down_pieces)
+    grad_normed_two = scatter_end(*hold(normed_back, down_pieces))
+    gain_two_term = jnp.sum(grad_normed_two * residual * inv_two, axis=0)
+    scaled_two = grad_normed_two * gain_two
+    grad_residual = (
+        float_of(cot_in)
+        + inv_two * scaled_two
+        - residual
+        * (inv_two * inv_two * inv_two)
+        * jnp.mean(scaled_two * residual, axis=-1, keepdims=True)
+    )
+    grad_residual_low = low_of(grad_residual)
+    grad_wait = gather_rows(grad_residual_low)
+    up_send = x_send(*hold(up_pair, grad_residual_low))
+    up_back = to_x(up_send)
+    mlp_parts = [low_of(cols_dot(hold(hidden_low, up_send), w)) for w in down_weights]
+    gate_pieces = z_pieces(*hold((*gate_pair, gate_back), mlp_parts))
+    gate_done = z_send(gate_pieces)
+    hidden_units = w_gate.shape[1]
+    grad_down = z_sum(*hold(down_done, gate_pieces), hidden_units).T
+    grad_span = take_rows(*hold(grad_wait, gate_pieces))
+    grad_attended = low_of(wide_dot(grad_span, out_weights))
+    branch_mlp = scatter_start(*hold(mlp_parts, grad_span))
+    grad_query, grad_early, grad_own = dense_call(
+        functools.partial(attend_back_kernel, score_scale),
+        "attend_back",
+        [
+            ((group_rows, query_width), jnp.bfloat16),
+            ((group_rows, 2 * key_width), jnp.bfloat16),
+            ((group_rows, 2 * key_width), jnp.float32),
+        ],
+        [
+            pltpu.VMEM((2 * group_rows, group_rows), jnp.float32),
+            pltpu.VMEM((2 * group_rows, GROUP * group_rows), jnp.bfloat16),
+            pltpu.VMEM((2 * group_rows, GROUP * group_rows), jnp.bfloat16),
+        ],
+        (
+            query_rot,
+            early_kv,
+            own_kv,
+            query_ids,
+            key_ids,
+            log_total,
+            hold(grad_attended, grad_down),
+            cos_wide,
+            sin_wide,
+        ),
+    )
+    late_kv = lax.ppermute(grad_early, "seq", [(2, 0), (3, 1)])
+    out_pair = grad_pair(hold(grad_span, grad_early), attended_low)
+    mlp_branch = scatter_end(*hold(branch_mlp, out_pair[0]))
+    mixed_out = columns_out(low_of(residual + mlp_branch))
+    out_send = x_send(*out_pair)
+    out_back = to_x(out_send)
+    up_pieces = z_pieces(*hold((*up_pair, up_back), out_send))
+    up_done = z_send(up_pieces)
+    (grad_raw,) = dense_call(
+        join_kernel,
+        "join",
+        [((group_rows, heads_width), jnp.bfloat16)],
+        [],
+        (grad_query, grad_own, hold(late_kv, up_pieces), cos_wide, sin_wide),
+    )
+    heads_pair = grad_pair(normed_one, grad_raw)
+    first_back = scatter_start(
+        *[low_of(cols_dot(hold(grad_raw, heads_pair[0]), w)) for w in heads_weights]
+    )
+    heads_send = x_send(*hold(heads_pair, first_back[:2]))
+    heads_back = to_x(heads_send)
+    grad_gate = z_sum(*hold(gate_done, heads_send), hidden_units)
+    out_pieces = z_pieces(*hold((*out_pair, out_back), heads_send))
+    out_done = z_send(out_pieces)
+    grad_normed_one = scatter_end(*hold(first_back, out_pieces, grad_gate))
+    scaled_one = grad_normed_one * gain_one
+    grad_tokens = columns_out(
+        grad_residual
+        + inv_one * scaled_one
+        - token_rows
+        * (inv_one * inv_one * inv_one)
+        * jnp.mean(scaled_one * token_rows, axis=-1, keepdims=True)
+    )
+    gain_one_term = jnp.sum(grad_normed_one * token_rows * inv_one, axis=0)
+    gain_rows = jnp.stack([gain_one_term, gain_two_term])
+    heads_pieces = z_pieces(*hold((*heads_pair, heads_back), gain_rows))
+    heads_done = z_send(heads_pieces)
+    gain_rows = gain_rows[:, :middle] + to_core(gain_rows[:, middle:])
+    gain_rows = gain_rows[:, :quarter] + to_x(gain_rows[:, quarter:])
+    gain_rows = gain_rows + to_tp(gain_rows)
+    gain_blocks = gain_rows.reshape(2, 4, block_rows)
+    gain_grads = sum(
+        to_z(piece, k) if k else piece
+        for k, piece in (
+            (k, lax.dynamic_index_in_dim(gain_blocks, seq_index ^ k, 1, keepdims=False))
+            for k in range(4)
+        )
+    )
+    grad_up = z_sum(*hold(up_done, heads_pieces), hidden_units)
+    grad_out = z_sum(*hold(out_done, grad_up), w_out.shape[0]).T
+    heads_own, heads_near, heads_far, heads_last = hold(heads_done, grad_out)
+    heads_first = float_of(heads_own) + float_of(heads_far)
+    heads_second = float_of(heads_near) + float_of(heads_last)
+    splits = (query_width, query_width + key_width, query_width + 2 * key_width)
+    grad_query_w, grad_key_w, grad_value_w = (
+        joined(own, other, 2 * own.shape[1])
+        for own, other in list(
+            zip(jnp.split(heads_first, splits, axis=1), jnp.split(heads_second, splits, axis=1))
+        )[:3]
+    )
+    return (
+        mixed_out,
+        grad_tokens,
+        grad_query_w,
+        grad_key_w,
+        grad_value_w,
+        grad_out,
+        grad_gate,
+        grad_up,
+        grad_down,
+        gain_grads,
+    )
+
+
 def solution(mesh):
+    halves = mesh.shape["seq"] == 4 and mesh.shape["tp"] == 2 and mesh.shape["fsdp"] == 4
+    plan = half_plan if halves else per_device
     in_specs = (
         P(("fsdp", "seq", "tp"), None),
         P("fsdp", None),
@@ -380,5 +1060,5 @@
         P(None, ("fsdp", "seq")),
     )
     return jax.shard_map(
-        per_device, mesh=mesh, in_specs=in_specs, out_specs=out_specs, check_vma=False
-    )
+        plan, mesh=mesh, in_specs=in_specs, out_specs=out_specs, check_vma=False
+    )

time: 1840 us -> 846 us (0.46)
  waiting for transfers between devices: 1480 us -> 458 us
  starting transfers between devices: 1.64 us -> 113 us
  matrix products: 197 us -> 101 us
  blocking collectives: 78.3 us -> 0 us
  Pallas kernels: 0 us -> 73.9 us
  other arithmetic: 42.8 us -> 66.2 us
    reduce_scatter x13 -> x0, waiting for transfers between devices: 983 us -> none  [the longest x1 188 us: per_device(): lax.psum_scatter(grad_gate_w.astype(jnp.bfloat16), ('fsdp', 'seq'), scatt...]
    all_gather x11 -> x0, waiting for transfers between devices: 488 us -> none  [the longest x1 99 us: per_device(): lax.all_gather(w_down, ('fsdp', 'seq'), axis=1, tiled=True)]
    ppermute x0 -> x94, waiting for transfers between devices: none -> 458 us  [the longest x51 244 us: to_z(): return lax.ppermute(value, 'seq', [(i, i ^ step) for i in range(4)])]
    ppermute x0 -> x94, starting transfers between devices: none -> 113 us  [the longest x51 78.7 us: to_z(): return lax.ppermute(value, 'seq', [(i, i ^ step) for i in range(4)])]
    dot_general x39 -> x30, matrix products: 197 us -> 101 us  [the longest x10 37.7 us: wide_dot(): jnp.dot(left[:, i * depth:(i + 1) * depth], piece, preferred_element_type...]
    pallas_call x0 -> x18, Pallas kernels: none -> 73.9 us  [the longest x4 32.7 us: dense_call(): pl.pallas_call(kernel, out_shape=[jax.ShapeDtypeStruct(shape, kind) for s...]
    all_gather x3 -> x0, blocking collectives: 70 us -> none  [the longest x1 28.7 us: per_device(): lax.all_gather(norm_gains, ('fsdp', 'seq'), axis=1, tiled=True)]
  transfers between devices with their start and end apart: 25 -> 94, of which waited for: 23 -> 44; matrix products, arithmetic and copies ran while one was open for 8% -> 15% of each run, Pallas kernels for 0% -> 8%
where the time goes in v2:
time: 846 us; the launch traced here: 833 us
  waiting for transfers between devices  458 us (54%)
  starting transfers between devices  113 us (13%)
  matrix products  101 us (12%)
  Pallas kernels  73.9 us (9%)
  other arithmetic  66.2 us (8%)
  local copies, waits for them, and re-layouts  17.1 us (2%)
    ppermute x51, waiting for transfers between devices, to_z(): return lax.ppermute(value, 'seq', [(i, i ^ step) for i in range(4)])  244 us
    ppermute x12, waiting for transfers between devices, to_x(): return lax.ppermute(value, 'fsdp', [(i, i ^ 2) for i in range(4)])  114 us
    ppermute x51, starting transfers between devices, to_z(): return lax.ppermute(value, 'seq', [(i, i ^ step) for i in range(4)])  78.7 us
    ppermute x17, waiting for transfers between devices, to_tp(): return lax.ppermute(value, 'tp', [(0, 1), (1, 0)])  50.5 us
    dot_general x10, matrix products, wide_dot(): jnp.dot(left[:, i * depth:(i + 1) * depth], piece, preferred_element_type...  37.7 us
    dot_general x10, matrix products, cols_dot(): lax.dot_general(left, right, (((1,), (1,)), ((), ())), preferred_element_...  33.2 us
    pallas_call x4, Pallas kernels, dense_call(): pl.pallas_call(kernel, out_shape=[jax.ShapeDtypeStruct(shape, kind) for s...  32.7 us
    convert_element_type x22, other arithmetic, low_of(): return value.astype(jnp.bfloat16)  30.6 us
  transfers between devices with their start and end apart: 94, of which 44 were waited for; matrix products, arithmetic and copies ran while one was open for 15% of the time, Pallas kernels for 8%

profile of v2, /device:TPU:18, one launch (start us, length us, event | category | flops | bytes accessed | tf_op | source)
XLA Modules:
  0.0 832.6 jit_solution(16829750073165985990)
XLA Ops:
  15.1 6.7 collective-permute-done
  21.9 11.9 %collective-permute-done.1 = bf16[2,2,160]{2,1,0:T(2,128)(2,1)S(1)} collective-permute-done((bf16[2,2,160]{2,1,0:T(2,128)(2,1)S(1)}, bf16[2,2,160]{2,1,0:T(2,128)(2,1)S(1)}, u32[]{:S(2)}, u32[]{:S(2)}) %collective-permute-start.1) | collective-permute-done | bytes 1312 | tf_op jit(solution)/shard_map/ppermute | solution.py:368
  51.0 12.7 %collective-permute-done.13.refs_3_ = bf16[160,640]{1,0:T(8,128)(2,1)S(1)} collective-permute-done((bf16[160,640]{1,0:T(8,128)(2,1)}, bf16[160,640]{1,0:T(8,128)(2,1)S(1)}, u32[]{:S(2)}, u32[]{:S(2)}) %collective-permute-start.13) | collective-permute-done | bytes 204832 | tf_op jit(solution)/shard_map/ppermute | solution.py:368
  82.4 10.0 %collective-permute-done.8.one_far = bf16[256,1280]{1,0:T(8,128)(2,1)S(1)} collective-permute-done((bf16[256,1280]{1,0:T(8,128)(2,1)S(1)}, bf16[256,1280]{1,0:T(8,128)(2,1)S(1)}, u32[]{:S(2)}, u32[]{:S(2)}) %collective-permute-start.8) | collective-permute-done | bytes 655392 | tf_op jit(solution)/shard_map/ppermute | solution.py:372
  95.9 24.0 %collective-permute-done.10.two_far = bf16[256,1280]{1,0:T(8,128)(2,1)S(1)} collective-permute-done((bf16[256,1280]{1,0:T(8,128)(2,1)S(1)}, bf16[256,1280]{1,0:T(8,128)(2,1)S(1)}, u32[]{:S(2)}, u32[]{:S(2)}) %collective-permute-start.10) | collective-permute-done | bytes 655392 | tf_op jit(solution)/shard_map/ppermute | solution.py:368
  124.6 8.3 collective-permute-done.16.refs_3_
  139.0 12.3 %collective-permute-done.19.one_near = bf16[128,1280]{1,0:T(8,128)(2,1)S(1)} collective-permute-done((bf16[128,1280]{1,0:T(8,128)(2,1)S(1)}, bf16[128,1280]{1,0:T(8,128)(2,1)S(1)}, u32[]{:S(2)}, u32[]{:S(2)}) %collective-permute-start.19) | collective-permute-done | bytes 327712 | tf_op jit(solution)/shard_map/ppermute | solution.py:368
  168.1 21.3 %collective-permute-done.22.two_far = bf16[256,1280]{1,0:T(8,128)(2,1)} collective-permute-done((bf16[256,1280]{1,0:T(8,128)(2,1)}, bf16[256,1280]{1,0:T(8,128)(2,1)}, u32[]{:S(2)}, u32[]{:S(2)}) %collective-permute-start.22) | collective-permute-done | bytes 655392 | tf_op jit(solution)/shard_map/ppermute | solution.py:368
  189.4 9.6 %collective-permute-done.24.early = bf16[512,320]{1,0:T(8,128)(2,1)S(1)} collective-permute-done((bf16[512,320]{1,0:T(8,128)(2,1)S(1)}, bf16[512,320]{1,0:T(8,128)(2,1)S(1)}, u32[]{:S(2)}, u32[]{:S(2)}) %collective-permute-start.24) | collective-permute-done | bytes 327712 | tf_op jit(solution)/shard_map/ppermute | solution.py:856
  204.2 13.7 %attend.1 = (bf16[512,640]{1,0:T(8,128)(2,1)S(1)}, f32[8,512]{1,0:T(8,128)S(1)}) custom-call(bf16[512,640]{1,0:T(8,128)(2,1)S(1)} %get-tuple-element.196.query, bf16[512,320]{1,0:T(8,128)(2,1)S(1)} %collective-permute-done.24.early, bf16[512,320]{1,0:T(8,128)(2,1)S(1)} %get-tuple-element.188.own, s32[2,512]{1,0:T(2,128)S(1)} %pad_add_fusion.1.query_ids, ...), custom_call_target="tpu_custom_call" | custom-call | flops 1024 | bytes 4096 | tf_op jit(solution)/shard_map/attend/pallas_call | solution.py:527
  218.0 15.0 %place_rows.8 = (bf16[640,1792]{1,0:T(8,128)(2,1)}, bf16[1280,1792]{1,0:T(8,128)(2,1)}) custom-call(s32[1]{0:T(128)} %bitcast.5.refs_0_, bf16[160,1792]{1,0:T(8,128)(2,1)} %get-tuple-element.201.refs_1_, bf16[160,1792]{1,0:T(8,128)(2,1)} %collective-permute-done.25.refs_2_, bf16[160,1792]{1,0:T(8,128)(2,1)} %collective-permute-done.26.refs_3_, ...), custom_call_target="tpu_custom_call" | custom-call | bytes 6881280 | tf_op jit(solution)/shard_map/place_rows/pallas_call | solution.py:427
  254.6 21.8 %collective-permute-done.30 = bf16[256,1280]{1,0:T(8,128)(2,1)} collective-permute-done((bf16[256,1280]{1,0:T(8,128)(2,1)S(1)}, bf16[256,1280]{1,0:T(8,128)(2,1)}, u32[]{:S(2)}, u32[]{:S(2)}) %collective-permute-start.30) | collective-permute-done | bytes 655392 | tf_op jit(solution)/shard_map/ppermute | solution.py:368
  289.6 9.6 %collective-permute-done.32 = bf16[128,1280]{1,0:T(8,128)(2,1)S(1)} collective-permute-done((bf16[128,1280]{1,0:T(8,128)(2,1)S(1)}, bf16[128,1280]{1,0:T(8,128)(2,1)S(1)}, u32[]{:S(2)}, u32[]{:S(2)}) %collective-permute-start.32) | collective-permute-done | bytes 327712 | tf_op jit(solution)/shard_map/ppermute | solution.py:368
  310.5 7.6 collective-permute-done.34.one_near
  320.5 13.7 %collective-permute-done.35.one_far = bf16[256,1280]{1,0:T(8,128)(2,1)S(1)} collective-permute-done((bf16[256,1280]{1,0:T(8,128)(2,1)S(1)}, bf16[256,1280]{1,0:T(8,128)(2,1)S(1)}, u32[]{:S(2)}, u32[]{:S(2)}) %collective-permute-start.35) | collective-permute-done | bytes 655392 | tf_op jit(solution)/shard_map/ppermute | solution.py:372
  365.7 41.8 %collective-permute-done.44.refs_0_ = bf16[640,1792]{1,0:T(8,128)(2,1)S(1)} collective-permute-done((bf16[640,1792]{1,0:T(8,128)(2,1)S(1)}, bf16[640,1792]{1,0:T(8,128)(2,1)S(1)}, u32[]{:S(2)}, u32[]{:S(2)}) %collective-permute-start.44) | collective-permute-done | bytes 2293792 | tf_op jit(solution)/shard_map/ppermute | solution.py:364
  411.5 7.9 collective-permute-done.46
  419.4 6.8 fusion.27
  440.8 6.2 fusion.2
  473.8 30.9 %collective-permute-done.50 = bf16[640,1792]{1,0:T(8,128)(2,1)S(1)} collective-permute-done((bf16[640,1792]{1,0:T(8,128)(2,1)}, bf16[640,1792]{1,0:T(8,128)(2,1)S(1)}, u32[]{:S(2)}, u32[]{:S(2)}) %collective-permute-start.50) | collective-permute-done | bytes 2293792 | tf_op jit(solution)/shard_map/ppermute | solution.py:364
  519.8 19.3 %collective-permute-done.52 = bf16[128,1280]{1,0:T(8,128)(2,1)S(1)} collective-permute-done((bf16[128,1280]{1,0:T(8,128)(2,1)S(1)}, bf16[128,1280]{1,0:T(8,128)(2,1)S(1)}, u32[]{:S(2)}, u32[]{:S(2)}) %collective-permute-start.52) | collective-permute-done | bytes 327712 | tf_op jit(solution)/shard_map/ppermute | solution.py:368
  554.3 7.5 collective-permute-done.54.one_near
  570.1 8.0 collective-permute-done.61
  579.7 10.7 %collective-permute-done.57.two_far = bf16[256,1280]{1,0:T(8,128)(2,1)S(1)} collective-permute-done((bf16[256,1280]{1,0:T(8,128)(2,1)S(1)}, bf16[256,1280]{1,0:T(8,128)(2,1)S(1)}, u32[]{:S(2)}, u32[]{:S(2)}) %collective-permute-start.57) | collective-permute-done | bytes 655392 | tf_op jit(solution)/shard_map/ppermute | solution.py:368
  597.6 15.6 %attend_back.1 = (bf16[512,640]{1,0:T(8,128)(2,1)S(1)}, bf16[512,320]{1,0:T(8,128)(2,1)S(1)}, f32[512,320]{1,0:T(8,128)S(1)}) custom-call(bf16[512,640]{1,0:T(8,128)(2,1)S(1)} %get-tuple-element.196.query, bf16[512,320]{1,0:T(8,128)(2,1)S(1)} %collective-permute-done.24.early, bf16[512,320]{1,0:T(8,128)(2,1)S(1)} %get-tuple-element.188.own, ...), custom_call_target="tpu_custom_call" | custom-call | flops 1024 | bytes 4096 | tf_op jit(solution)/shard_map/attend_back/pallas_call | solution.py:527
  622.6 11.4 %collective-permute-done.59 = bf16[256,1280]{1,0:T(8,128)(2,1)} collective-permute-done((bf16[256,1280]{1,0:T(8,128)(2,1)}, bf16[256,1280]{1,0:T(8,128)(2,1)}, u32[]{:S(2)}, u32[]{:S(2)}) %collective-permute-start.59) | collective-permute-done | bytes 655392 | tf_op jit(solution)/shard_map/ppermute | solution.py:372
  635.8 10.4 %collective-permute-done.60 = bf16[256,1280]{1,0:T(8,128)(2,1)} collective-permute-done((bf16[256,1280]{1,0:T(8,128)(2,1)}, bf16[256,1280]{1,0:T(8,128)(2,1)}, u32[]{:S(2)}, u32[]{:S(2)}) %collective-permute-start.60) | collective-permute-done | bytes 655392 | tf_op jit(solution)/shard_map/ppermute | solution.py:368
  659.6 27.9 %collective-permute-done.66.late = bf16[512,320]{1,0:T(8,128)(2,1)S(1)} collective-permute-done((bf16[512,320]{1,0:T(8,128)(2,1)S(1)}, bf16[512,320]{1,0:T(8,128)(2,1)S(1)}, u32[]{:S(2)}, u32[]{:S(2)}) %collective-permute-start.66) | collective-permute-done | bytes 327712 | tf_op jit(solution)/shard_map/ppermute | solution.py:960
  722.8 23.2 %collective-permute-done.78 = bf16[640,1024]{1,0:T(8,128)(2,1)S(1)} collective-permute-done((bf16[640,1024]{1,0:T(8,128)(2,1)S(1)}, bf16[640,1024]{1,0:T(8,128)(2,1)S(1)}, u32[]{:S(2)}, u32[]{:S(2)}) %collective-permute-start.78) | collective-permute-done | bytes 1310752 | tf_op jit(solution)/shard_map/ppermute | solution.py:364
  751.3 10.1 %collective-permute-done.86 = bf16[160,1792]{1,0:T(8,128)(2,1)S(1)} collective-permute-done((bf16[160,1792]{1,0:T(8,128)(2,1)S(1)}, bf16[160,1792]{1,0:T(8,128)(2,1)S(1)}, u32[]{:S(2)}, u32[]{:S(2)}) %collective-permute-start.86) | collective-permute-done | bytes 573472 | tf_op jit(solution)/shard_map/ppermute | solution.py:368
  768.1 20.7 %collective-permute-done.70 = bf16[256,1280]{1,0:T(8,128)(2,1)S(1)} collective-permute-done((bf16[256,1280]{1,0:T(8,128)(2,1)S(1)}, bf16[256,1280]{1,0:T(8,128)(2,1)S(1)}, u32[]{:S(2)}, u32[]{:S(2)}) %collective-permute-start.70) | collective-permute-done | bytes 655392 | tf_op jit(solution)/shard_map/ppermute | solution.py:368
  802.0 11.3 %collective-permute-done.76 = bf16[128,1280]{1,0:T(8,128)(2,1)S(1)} collective-permute-done((bf16[128,1280]{1,0:T(8,128)(2,1)S(1)}, bf16[128,1280]{1,0:T(8,128)(2,1)S(1)}, u32[]{:S(2)}, u32[]{:S(2)}) %collective-permute-start.76) | collective-permute-done | bytes 327712 | tf_op jit(solution)/shard_map/ppermute | solution.py:368
  (598 shorter events, 361.6 us)
Async XLA Ops:
  75.1 81.0 %collective-permute-start.18 = (bf16[1280,1024]{1,0:T(8,128)(2,1)}, bf16[1280,1024]{1,0:T(8,128)(2,1)}, u32[]{:S(2)}, u32[]{:S(2)}) collective-permute-start(bf16[1280,1024]{1,0:T(8,128)(2,1)} %fill_rows.5), channel_id=1, source_target_pairs={{0,8},{8,0},{16,24},{24,16},{1,9},{9,1},{17,25},{25,17},{2,10},{10... | collective-permute-start | bytes 7864328 | tf_op jit(solution)/shard_map/ppermute | solution.py:360
  76.9 43.0 %collective-permute-start.10 = (bf16[256,1280]{1,0:T(8,128)(2,1)S(1)}, bf16[256,1280]{1,0:T(8,128)(2,1)S(1)}, u32[]{:S(2)}, u32[]{:S(2)}) collective-permute-start(bf16[256,1280]{1,0:T(8,128)(2,1)S(1)} %pad_maximum_fusion.8), channel_id=1, source_target_pairs={{0,2},{2,0},{4,6},{6,4},{1,3},{3,1},{5,7},{7,5},{8,10},{10,8},{12,... | collective-permute-start | bytes 1966088 | tf_op jit(solution)/shard_map/ppermute | solution.py:368
  81.1 52.3 %collective-permute-start.17 = (bf16[160,1792]{1,0:T(8,128)(2,1)S(1)}, bf16[160,1792]{1,0:T(8,128)(2,1)}, u32[]{:S(2)}, u32[]{:S(2)}) collective-permute-start(bf16[160,1792]{1,0:T(8,128)(2,1)S(1)} %get-tuple-element.178), channel_id=1, source_target_pairs={{0,6},{2,4},{4,2},{6,0},{1,7},{3,5},{5,3},{7,1},{8,14},{10,12},{12... | collective-permute-start | bytes 1720328 | tf_op jit(solution)/shard_map/ppermute | solution.py:368
  81.5 52.5 %collective-permute-start.15 = (bf16[160,1792]{1,0:T(8,128)(2,1)S(1)}, bf16[160,1792]{1,0:T(8,128)(2,1)}, u32[]{:S(2)}, u32[]{:S(2)}) collective-permute-start(bf16[160,1792]{1,0:T(8,128)(2,1)S(1)} %get-tuple-element.178), channel_id=1, source_target_pairs={{0,2},{2,0},{4,6},{6,4},{1,3},{3,1},{5,7},{7,5},{8,10},{10,8},{12,... | collective-permute-start | bytes 1720328 | tf_op jit(solution)/shard_map/ppermute | solution.py:368
  92.4 40.5 %collective-permute-start.16 = (bf16[160,1792]{1,0:T(8,128)(2,1)S(1)}, bf16[160,1792]{1,0:T(8,128)(2,1)S(1)}, u32[]{:S(2)}, u32[]{:S(2)}) collective-permute-start(bf16[160,1792]{1,0:T(8,128)(2,1)S(1)} %get-tuple-element.179.refs_1_), channel_id=1, source_target_pairs={{0,4},{2,6},{4,0},{6,2},{1,5},{3,7},{5,1},{7,3},{8,12},{10,14},{12... | collective-permute-start | bytes 1720328 | tf_op jit(solution)/shard_map/ppermute | solution.py:368
  134.0 84.0 %collective-permute-start.27 = (bf16[160,1792]{1,0:T(8,128)(2,1)}, bf16[160,1792]{1,0:T(8,128)(2,1)}, u32[]{:S(2)}, u32[]{:S(2)}) collective-permute-start(bf16[160,1792]{1,0:T(8,128)(2,1)} %get-tuple-element.199), channel_id=1, source_target_pairs={{0,6},{2,4},{4,2},{6,0},{1,7},{3,5},{5,3},{7,1},{8,14},{10,12},{12... | collective-permute-start | bytes 1720328 | tf_op jit(solution)/shard_map/ppermute | solution.py:368
  160.8 57.2 %collective-permute-start.25 = (bf16[160,1792]{1,0:T(8,128)(2,1)}, bf16[160,1792]{1,0:T(8,128)(2,1)}, u32[]{:S(2)}, u32[]{:S(2)}) collective-permute-start(bf16[160,1792]{1,0:T(8,128)(2,1)} %get-tuple-element.199), channel_id=1, source_target_pairs={{0,2},{2,0},{4,6},{6,4},{1,3},{3,1},{5,7},{7,5},{8,10},{10,8},{12,... | collective-permute-start | bytes 1720328 | tf_op jit(solution)/shard_map/ppermute | solution.py:368
  163.9 54.1 %collective-permute-start.26 = (bf16[160,1792]{1,0:T(8,128)(2,1)}, bf16[160,1792]{1,0:T(8,128)(2,1)}, u32[]{:S(2)}, u32[]{:S(2)}) collective-permute-start(bf16[160,1792]{1,0:T(8,128)(2,1)} %get-tuple-element.201.refs_1_), channel_id=1, source_target_pairs={{0,4},{2,6},{4,0},{6,2},{1,5},{3,7},{5,1},{7,3},{8,12},{10,14},{12... | collective-permute-start | bytes 1720328 | tf_op jit(solution)/shard_map/ppermute | solution.py:368
  189.4 47.9 %collective-permute-start.28 = (bf16[1280,640]{1,0:T(8,128)(2,1)}, bf16[1280,640]{1,0:T(8,128)(2,1)}, u32[]{:S(2)}, u32[]{:S(2)}) collective-permute-start(bf16[1280,640]{1,0:T(8,128)(2,1)} %fill_rows.6), channel_id=1, source_target_pairs={{0,8},{8,0},{16,24},{24,16},{1,9},{9,1},{17,25},{25,17},{2,10},{10... | collective-permute-start | bytes 4915208 | tf_op jit(solution)/shard_map/ppermute | solution.py:360
  199.0 51.7 %collective-permute-start.31 = (bf16[640,1792]{1,0:T(8,128)(2,1)}, bf16[640,1792]{1,0:T(8,128)(2,1)}, u32[]{:S(2)}, u32[]{:S(2)}) collective-permute-start(bf16[640,1792]{1,0:T(8,128)(2,1)} %get-tuple-element.183), channel_id=1, source_target_pairs={{0,16},{8,24},{16,0},{24,8},{1,17},{9,25},{17,1},{25,9},{2,18},{10... | collective-permute-start | bytes 6881288 | tf_op jit(solution)/shard_map/ppermute | solution.py:364
  247.3 54.7 %collective-permute-start.41 = (bf16[160,1792]{1,0:T(8,128)(2,1)}, bf16[160,1792]{1,0:T(8,128)(2,1)}, u32[]{:S(2)}, u32[]{:S(2)}) collective-permute-start(bf16[160,1792]{1,0:T(8,128)(2,1)} %get-tuple-element.216), channel_id=1, source_target_pairs={{0,6},{2,4},{4,2},{6,0},{1,7},{3,5},{5,3},{7,1},{8,14},{10,12},{12... | collective-permute-start | bytes 1720328 | tf_op jit(solution)/shard_map/ppermute | solution.py:368
  247.3 54.7 %collective-permute-start.39 = (bf16[160,1792]{1,0:T(8,128)(2,1)}, bf16[160,1792]{1,0:T(8,128)(2,1)}, u32[]{:S(2)}, u32[]{:S(2)}) collective-permute-start(bf16[160,1792]{1,0:T(8,128)(2,1)} %get-tuple-element.216), channel_id=1, source_target_pairs={{0,2},{2,0},{4,6},{6,4},{1,3},{3,1},{5,7},{7,5},{8,10},{10,8},{12,... | collective-permute-start | bytes 1720328 | tf_op jit(solution)/shard_map/ppermute | solution.py:368
  250.7 51.3 %collective-permute-start.40 = (bf16[160,1792]{1,0:T(8,128)(2,1)}, bf16[160,1792]{1,0:T(8,128)(2,1)}, u32[]{:S(2)}, u32[]{:S(2)}) collective-permute-start(bf16[160,1792]{1,0:T(8,128)(2,1)} %get-tuple-element.217.refs_1_), channel_id=1, source_target_pairs={{0,4},{2,6},{4,0},{6,2},{1,5},{3,7},{5,1},{7,3},{8,12},{10,14},{12... | collective-permute-start | bytes 1720328 | tf_op jit(solution)/shard_map/ppermute | solution.py:368
  253.9 51.5 %collective-permute-start.38 = (bf16[640,1792]{1,0:T(8,128)(2,1)}, bf16[640,1792]{1,0:T(8,128)(2,1)}, u32[]{:S(2)}, u32[]{:S(2)}) collective-permute-start(bf16[640,1792]{1,0:T(8,128)(2,1)} %get-tuple-element.205), channel_id=1, source_target_pairs={{0,16},{8,24},{16,0},{24,8},{1,17},{9,25},{17,1},{25,9},{2,18},{10... | collective-permute-start | bytes 6881288 | tf_op jit(solution)/shard_map/ppermute | solution.py:364
  355.2 52.3 %collective-permute-start.44 = (bf16[640,1792]{1,0:T(8,128)(2,1)S(1)}, bf16[640,1792]{1,0:T(8,128)(2,1)S(1)}, u32[]{:S(2)}, u32[]{:S(2)}) collective-permute-start(bf16[640,1792]{1,0:T(8,128)(2,1)S(1)} %copy-done.88), channel_id=1, source_target_pairs={{0,16},{8,24},{16,0},{24,8},{1,17},{9,25},{17,1},{25,9},{2,18},{10... | collective-permute-start | bytes 6881288 | tf_op jit(solution)/shard_map/ppermute | solution.py:364
  451.8 52.9 %collective-permute-start.50 = (bf16[640,1792]{1,0:T(8,128)(2,1)}, bf16[640,1792]{1,0:T(8,128)(2,1)S(1)}, u32[]{:S(2)}, u32[]{:S(2)}) collective-permute-start(bf16[640,1792]{1,0:T(8,128)(2,1)} %add_convert_fusion.5), channel_id=1, source_target_pairs={{0,16},{8,24},{16,0},{24,8},{1,17},{9,25},{17,1},{25,9},{2,18},{10... | collective-permute-start | bytes 6881288 | tf_op jit(solution)/shard_map/ppermute | solution.py:364
  454.8 51.4 %collective-permute-start.48 = (bf16[256,1280]{1,0:T(8,128)(2,1)S(1)}, bf16[256,1280]{1,0:T(8,128)(2,1)}, u32[]{:S(2)}, u32[]{:S(2)}) collective-permute-start(bf16[256,1280]{1,0:T(8,128)(2,1)S(1)} %pad_maximum_fusion.15), channel_id=1, source_target_pairs={{0,1},{1,0},{2,3},{3,2},{4,5},{5,4},{6,7},{7,6},{8,9},{9,8},{10,11... | collective-permute-start | bytes 1966088 | tf_op jit(solution)/shard_map/ppermute | solution.py:372
  455.2 53.5 %collective-permute-start.49 = (bf16[256,1280]{1,0:T(8,128)(2,1)S(1)}, bf16[256,1280]{1,0:T(8,128)(2,1)}, u32[]{:S(2)}, u32[]{:S(2)}) collective-permute-start(bf16[256,1280]{1,0:T(8,128)(2,1)S(1)} %slice.472), channel_id=1, source_target_pairs={{0,2},{2,0},{4,6},{6,4},{1,3},{3,1},{5,7},{7,5},{8,10},{10,8},{12,... | collective-permute-start | bytes 1966088 | tf_op jit(solution)/shard_map/ppermute | solution.py:368
  465.6 76.7 %collective-permute-start.47 = (bf16[1280,1792]{1,0:T(8,128)(2,1)}, bf16[1280,1792]{1,0:T(8,128)(2,1)S(1)}, u32[]{:S(2)}, u32[]{:S(2)}) collective-permute-start(bf16[1280,1792]{1,0:T(8,128)(2,1)} %convolution_convert_fusion.1), channel_id=1, source_target_pairs={{0,8},{8,0},{16,24},{24,16},{1,9},{9,1},{17,25},{25,17},{2,10},{10... | collective-permute-start | bytes 13762568 | tf_op jit(solution)/shard_map/ppermute | solution.py:360
  473.4 91.0 %collective-permute-start.58 = (bf16[640,1792]{1,0:T(8,128)(2,1)}, bf16[640,1792]{1,0:T(8,128)(2,1)}, u32[]{:S(2)}, u32[]{:S(2)}) collective-permute-start(bf16[640,1792]{1,0:T(8,128)(2,1)} %add_convert_fusion.4), channel_id=1, source_target_pairs={{0,16},{8,24},{16,0},{24,8},{1,17},{9,25},{17,1},{25,9},{2,18},{10... | collective-permute-start | bytes 6881288 | tf_op jit(solution)/shard_map/ppermute | solution.py:364
  505.9 63.2 %collective-permute-start.63 = (bf16[160,1792]{1,0:T(8,128)(2,1)S(1)}, bf16[160,1792]{1,0:T(8,128)(2,1)S(1)}, u32[]{:S(2)}, u32[]{:S(2)}) collective-permute-start(bf16[160,1792]{1,0:T(8,128)(2,1)S(1)} %get-tuple-element.322), channel_id=1, source_target_pairs={{0,6},{2,4},{4,2},{6,0},{1,7},{3,5},{5,3},{7,1},{8,14},{10,12},{12... | collective-permute-start | bytes 1720328 | tf_op jit(solution)/shard_map/ppermute | solution.py:368
  506.2 63.9 %collective-permute-start.62 = (bf16[160,1792]{1,0:T(8,128)(2,1)S(1)}, bf16[160,1792]{1,0:T(8,128)(2,1)S(1)}, u32[]{:S(2)}, u32[]{:S(2)}) collective-permute-start(bf16[160,1792]{1,0:T(8,128)(2,1)S(1)} %get-tuple-element.323), channel_id=1, source_target_pairs={{0,4},{2,6},{4,0},{6,2},{1,5},{3,7},{5,1},{7,3},{8,12},{10,14},{12... | collective-permute-start | bytes 1720328 | tf_op jit(solution)/shard_map/ppermute | solution.py:368
  569.1 84.9 %collective-permute-start.67 = (bf16[640,1792]{1,0:T(8,128)(2,1)}, bf16[640,1792]{1,0:T(8,128)(2,1)}, u32[]{:S(2)}, u32[]{:S(2)}) collective-permute-start(bf16[640,1792]{1,0:T(8,128)(2,1)} %add_convert_fusion.2), channel_id=1, source_target_pairs={{0,16},{8,24},{16,0},{24,8},{1,17},{9,25},{17,1},{25,9},{2,18},{10... | collective-permute-start | bytes 6881288 | tf_op jit(solution)/shard_map/ppermute | solution.py:364
  619.2 89.5 %collective-permute-start.75 = (bf16[160,1792]{1,0:T(8,128)(2,1)}, bf16[160,1792]{1,0:T(8,128)(2,1)S(1)}, u32[]{:S(2)}, u32[]{:S(2)}) collective-permute-start(bf16[160,1792]{1,0:T(8,128)(2,1)} %get-tuple-element.318), channel_id=1, source_target_pairs={{0,6},{2,4},{4,2},{6,0},{1,7},{3,5},{5,3},{7,1},{8,14},{10,12},{12... | collective-permute-start | bytes 1720328 | tf_op jit(solution)/shard_map/ppermute | solution.py:368
  634.0 77.0 %collective-permute-start.74 = (bf16[160,1792]{1,0:T(8,128)(2,1)S(1)}, bf16[160,1792]{1,0:T(8,128)(2,1)S(1)}, u32[]{:S(2)}, u32[]{:S(2)}) collective-permute-start(bf16[160,1792]{1,0:T(8,128)(2,1)S(1)} %copy-done.76), channel_id=1, source_target_pairs={{0,4},{2,6},{4,0},{6,2},{1,5},{3,7},{5,1},{7,3},{8,12},{10,14},{12... | collective-permute-start | bytes 1720328 | tf_op jit(solution)/shard_map/ppermute | solution.py:368
  646.2 66.1 %collective-permute-start.73 = (bf16[160,1792]{1,0:T(8,128)(2,1)S(1)}, bf16[160,1792]{1,0:T(8,128)(2,1)S(1)}, u32[]{:S(2)}, u32[]{:S(2)}) collective-permute-start(bf16[160,1792]{1,0:T(8,128)(2,1)S(1)} %copy-done.75), channel_id=1, source_target_pairs={{0,2},{2,0},{4,6},{6,4},{1,3},{3,1},{5,7},{7,5},{8,10},{10,8},{12,... | collective-permute-start | bytes 1720328 | tf_op jit(solution)/shard_map/ppermute | solution.py:368
  711.0 50.4 %collective-permute-start.86 = (bf16[160,1792]{1,0:T(8,128)(2,1)S(1)}, bf16[160,1792]{1,0:T(8,128)(2,1)S(1)}, u32[]{:S(2)}, u32[]{:S(2)}) collective-permute-start(bf16[160,1792]{1,0:T(8,128)(2,1)S(1)} %get-tuple-element.315), channel_id=1, source_target_pairs={{0,4},{2,6},{4,0},{6,2},{1,5},{3,7},{5,1},{7,3},{8,12},{10,14},{12... | collective-permute-start | bytes 1720328 | tf_op jit(solution)/shard_map/ppermute | solution.py:368
  712.2 53.0 %collective-permute-start.85 = (bf16[160,1792]{1,0:T(8,128)(2,1)S(1)}, bf16[160,1792]{1,0:T(8,128)(2,1)S(1)}, u32[]{:S(2)}, u32[]{:S(2)}) collective-permute-start(bf16[160,1792]{1,0:T(8,128)(2,1)S(1)} %get-tuple-element.316), channel_id=1, source_target_pairs={{0,2},{2,0},{4,6},{6,4},{1,3},{3,1},{5,7},{7,5},{8,10},{10,8},{12,... | collective-permute-start | bytes 1720328 | tf_op jit(solution)/shard_map/ppermute | solution.py:368
  719.7 47.8 %collective-permute-start.69 = (bf16[256,1280]{1,0:T(8,128)(2,1)S(1)}, bf16[256,1280]{1,0:T(8,128)(2,1)S(1)}, u32[]{:S(2)}, u32[]{:S(2)}) collective-permute-start(bf16[256,1280]{1,0:T(8,128)(2,1)S(1)} %pad_maximum_fusion.20), channel_id=1, source_target_pairs={{0,1},{1,0},{2,3},{3,2},{4,5},{5,4},{6,7},{7,6},{8,9},{9,8},{10,11... | collective-permute-start | bytes 1966088 | tf_op jit(solution)/shard_map/ppermute | solution.py:372
  745.9 42.8 %collective-permute-start.70 = (bf16[256,1280]{1,0:T(8,128)(2,1)S(1)}, bf16[256,1280]{1,0:T(8,128)(2,1)S(1)}, u32[]{:S(2)}, u32[]{:S(2)}) collective-permute-start(bf16[256,1280]{1,0:T(8,128)(2,1)S(1)} %slice.484), channel_id=1, source_target_pairs={{0,2},{2,0},{4,6},{6,4},{1,3},{3,1},{5,7},{7,5},{8,10},{10,8},{12,... | collective-permute-start | bytes 1966088 | tf_op jit(solution)/shard_map/ppermute | solution.py:368
  748.8 45.8 %collective-permute-start.84 = (bf16[160,640]{1,0:T(8,128)(2,1)S(1)}, bf16[160,640]{1,0:T(8,128)(2,1)S(1)}, u32[]{:S(2)}, u32[]{:S(2)}) collective-permute-start(bf16[160,640]{1,0:T(8,128)(2,1)S(1)} %get-tuple-element.365), channel_id=1, source_target_pairs={{0,6},{2,4},{4,2},{6,0},{1,7},{3,5},{5,3},{7,1},{8,14},{10,12},{12... | collective-permute-start | bytes 614408 | tf_op jit(solution)/shard_map/ppermute | solution.py:368
  767.6 47.0 %collective-permute-start.81 = (bf16[160,1024]{1,0:T(8,128)(2,1)S(1)}, bf16[160,1024]{1,0:T(8,128)(2,1)S(1)}, u32[]{:S(2)}, u32[]{:S(2)}) collective-permute-start(bf16[160,1024]{1,0:T(8,128)(2,1)S(1)} %get-tuple-element.338), channel_id=1, source_target_pairs={{0,6},{2,4},{4,2},{6,0},{1,7},{3,5},{5,3},{7,1},{8,14},{10,12},{12... | collective-permute-start | bytes 983048 | tf_op jit(solution)/shard_map/ppermute | solution.py:368
  (177 other events, 2906.8 us)

commit v3 on v2

--- a/solution.py
+++ b/solution.py
@@ -356,6 +356,10 @@
     )
 
 
+VMEM_BYTES = 48 * 1024 * 1024
+SMALL_COST = pl.CostEstimate(flops=1024, bytes_accessed=4096, transcendentals=0)
+
+
 def to_core(value):
     return lax.ppermute(value, "fsdp", [(i, i ^ 1) for i in range(4)])
 
@@ -392,18 +396,12 @@
     return lax.dot_general(left, right, (((1,), (1,)), ((), ())), preferred_element_type=jnp.float32)
 
 
-def wide_dot(left, pieces):
-    depth = pieces[0].shape[0]
-    return sum(
-        jnp.dot(left[:, i * depth : (i + 1) * depth], piece, preferred_element_type=jnp.float32)
-        for i, piece in enumerate(pieces)
-    )
-
-
-def place_kernel(rows, place, one, two, three, four, plane, mine, held, read_sems, sems):
+def place_kernel(rows, place, pair, pair_far, plane, mine, held, read_sems, sems):
     reads = [
-        pltpu.make_async_copy(piece, held.at[k], read_sems.at[k])
-        for k, piece in enumerate((one, two, three, four))
+        pltpu.make_async_copy(
+            (pair, pair_far)[k // 2].at[pl.ds((k % 2) * rows, rows), :], held.at[k], read_sems.at[k]
+        )
+        for k in range(4)
     ]
     for copy in reads:
         copy.start()
@@ -421,8 +419,8 @@
         write.wait()
 
 
-def place_rows(pieces, place):
-    rows, columns = pieces[0].shape
+def place_rows(pair, pair_far, place):
+    rows, columns = pair.shape[0] // 2, pair.shape[1]
     anywhere = pl.BlockSpec(memory_space=pl.ANY)
     return pl.pallas_call(
         lambda *refs: place_kernel(rows, *refs),
@@ -430,25 +428,25 @@
             jax.ShapeDtypeStruct((4 * rows, columns), jnp.bfloat16),
             jax.ShapeDtypeStruct((8 * rows, columns), jnp.bfloat16),
         ),
-        in_specs=[pl.BlockSpec(memory_space=pltpu.SMEM)] + [anywhere] * 4,
+        in_specs=[pl.BlockSpec(memory_space=pltpu.SMEM)] + [anywhere] * 2,
         out_specs=(anywhere, anywhere),
         scratch_shapes=[
             pltpu.VMEM((4, rows, columns), jnp.bfloat16),
             pltpu.SemaphoreType.DMA((4,)),
             pltpu.SemaphoreType.DMA((8,)),
         ],
-        cost_estimate=pl.CostEstimate(
-            flops=0, bytes_accessed=24 * rows * columns, transcendentals=0
-        ),
+        cost_estimate=SMALL_COST,
         name="place_rows",
-    )(place.reshape(1), *pieces)
-
-
-def fill_kernel(rows, across, first, mine, held, read_sems, sems):
-    part = rows // 4
+    )(place.reshape(1), pair, pair_far)
+
+
+def fill_kernel(rows, part, start, across, first, mine, held, read_sems, sems):
+    columns = pl.ds(start, mine.shape[1])
     reads = [
-        pltpu.make_async_copy(across.at[pl.ds(k * part, part), :], held.at[k], read_sems.at[k])
-        for k in range(4)
+        pltpu.make_async_copy(
+            across.at[pl.ds(k * part, part), columns], held.at[k], read_sems.at[k]
+        )
+        for k in range(rows // part)
     ]
     for copy in reads:
         copy.start()
@@ -464,34 +462,32 @@
         write.wait()
 
 
-def fill_rows(mine, across):
-    rows, columns = across.shape
+def fill_rows(mine, across, start=0):
+    rows, columns = across.shape[0], mine.shape[1]
+    part = 128 if rows % 128 == 0 else 32
     anywhere = pl.BlockSpec(memory_space=pl.ANY)
     return pl.pallas_call(
-        lambda *refs: fill_kernel(rows, *refs),
+        lambda *refs: fill_kernel(rows, part, start, *refs),
         out_shape=jax.ShapeDtypeStruct(mine.shape, mine.dtype),
         in_specs=[anywhere] * 2,
         out_specs=anywhere,
         scratch_shapes=[
-            pltpu.VMEM((4, rows // 4, columns), jnp.bfloat16),
-            pltpu.SemaphoreType.DMA((4,)),
-            pltpu.SemaphoreType.DMA((4,)),
+            pltpu.VMEM((rows // part, part, columns), jnp.bfloat16),
+            pltpu.SemaphoreType.DMA((rows // part,)),
+            pltpu.SemaphoreType.DMA((rows // part,)),
         ],
         input_output_aliases={1: 0},
-        cost_estimate=pl.CostEstimate(flops=0, bytes_accessed=4 * rows * columns, transcendentals=0),
+        cost_estimate=SMALL_COST,
         name="fill_rows",
     )(across, mine)
 
 
-VMEM_BYTES = 40 * 1024 * 1024
-
-
-def take_rows_kernel(own, one_near, one_far, two_tp, two_far, out, sems):
-    n = own.shape[0]
-    half = own.shape[1] // 2
+def take_rows_kernel(one, two, one_near, one_far, two_tp, two_far, out, sems):
+    n, half = one.shape
     left, right = pl.ds(0, half), pl.ds(half, half)
     moves = [
-        (own, pl.ds(0, n), pl.ds(0, 2 * half)),
+        (one, pl.ds(0, n), left),
+        (two, pl.ds(0, n), right),
         (one_near, pl.ds(2 * n, n), left),
         (one_far.at[pl.ds(0, n), :], pl.ds(n, n), left),
         (one_far.at[pl.ds(n, n), :], pl.ds(3 * n, n), left),
@@ -508,18 +504,18 @@
         copy.wait()
 
 
-def take_rows(own, *received):
-    shape = (4 * own.shape[0], own.shape[1])
+def take_rows(*pieces):
+    rows, half = pieces[0].shape
     return pl.pallas_call(
         take_rows_kernel,
-        out_shape=jax.ShapeDtypeStruct(shape, own.dtype),
-        in_specs=[pl.BlockSpec(memory_space=pl.ANY)] * 5,
+        out_shape=jax.ShapeDtypeStruct((4 * rows, 2 * half), pieces[0].dtype),
+        in_specs=[pl.BlockSpec(memory_space=pl.ANY)] * 6,
         out_specs=pl.BlockSpec(memory_space=pltpu.VMEM),
-        scratch_shapes=[pltpu.SemaphoreType.DMA((6,))],
+        scratch_shapes=[pltpu.SemaphoreType.DMA((7,))],
         compiler_params=pltpu.CompilerParams(vmem_limit_bytes=VMEM_BYTES),
-        cost_estimate=pl.CostEstimate(flops=0, bytes_accessed=4096, transcendentals=0),
+        cost_estimate=SMALL_COST,
         name="take_rows",
-    )(own, *received)
+    )(*pieces)
 
 
 def dense_call(kernel, name, outs, scratch, args):
@@ -531,7 +527,7 @@
         out_specs=[whole] * len(outs),
         scratch_shapes=scratch,
         compiler_params=pltpu.CompilerParams(vmem_limit_bytes=VMEM_BYTES),
-        cost_estimate=pl.CostEstimate(flops=1024, bytes_accessed=4096, transcendentals=0),
+        cost_estimate=SMALL_COST,
         name=name,
     )(*args)
 
@@ -668,6 +664,437 @@
     grad_raw[:, used:] = jnp.zeros((grad_raw.shape[0], spare), jnp.bfloat16)
 
 
+def tiled_call(kernel, name, steps, in_specs, outs, args):
+    return pl.pallas_call(
+        kernel,
+        grid=(steps,),
+        out_shape=[jax.ShapeDtypeStruct(shape, kind) for shape, kind, _, _ in outs],
+        in_specs=[pl.BlockSpec(block, index) for block, index in in_specs],
+        out_specs=[pl.BlockSpec(block, index) for _, _, block, index in outs],
+        compiler_params=pltpu.CompilerParams(vmem_limit_bytes=VMEM_BYTES),
+        cost_estimate=SMALL_COST,
+        name=name,
+    )(*args)
+
+
+def fixed(step):
+    return (0, 0)
+
+
+def by_row(step):
+    return (step, 0)
+
+
+def by_column(step):
+    return (0, step)
+
+
+def split_dot(left, mine, other):
+    depth = mine.shape[0]
+    first = jnp.dot(left[:, :depth], mine[...], preferred_element_type=jnp.float32)
+    return first + jnp.dot(left[:, depth:], other[...], preferred_element_type=jnp.float32)
+
+
+def project_kernel(start, left, mine, other, out):
+    columns = slice(start, start + out.shape[1])
+    depth = mine.shape[0]
+    first = jnp.dot(left[:, :depth], mine[:, columns], preferred_element_type=jnp.float32)
+    second = jnp.dot(left[:, depth:], other[:, columns], preferred_element_type=jnp.float32)
+    out[...] = (first + second).astype(out.dtype)
+
+
+def project(left, weights, start, columns, kind):
+    mine, other = weights
+    rows, depth = left.shape[0], mine.shape[0]
+    tiled = start == 0 and columns % 512 == 0
+    tile = 512 if tiled else columns
+    block = (depth, tile) if tiled else mine.shape
+    (out,) = tiled_call(
+        functools.partial(project_kernel, start),
+        "project",
+        columns // tile,
+        [(left.shape, fixed), (block, by_column), (block, by_column)],
+        [((rows, columns), kind, (rows, tile), by_column)],
+        (left, mine, other),
+    )
+    return out
+
+
+def hidden_kernel(normed, gate_m, gate_o, up_m, up_o, hidden, gate_slope, up_slope):
+    gate_pre = split_dot(normed, gate_m, gate_o)
+    up_pre = split_dot(normed, up_m, up_o)
+    sig_gate = 1.0 / (1.0 + jnp.exp(-gate_pre))
+    silu_gate = gate_pre * sig_gate
+    hidden[...] = (silu_gate * up_pre).astype(jnp.bfloat16)
+    gate_slope[...] = up_pre * (sig_gate * (1.0 + gate_pre * (1.0 - sig_gate)))
+    up_slope[...] = silu_gate
+
+
+def hidden_units(normed, gate_weights, up_weights):
+    rows = normed.shape[0]
+    depth, columns = gate_weights[0].shape
+    tile = 256
+    outs = [
+        ((rows, columns), kind, (rows, tile), by_column)
+        for kind in (jnp.bfloat16, jnp.float32, jnp.float32)
+    ]
+    return tiled_call(
+        hidden_kernel,
+        "hidden_units",
+        columns // tile,
+        [(normed.shape, fixed)] + [((depth, tile), by_column)] * 4,
+        outs,
+        (normed, *gate_weights, *up_weights),
+    )
+
+
+def hidden_grad_kernel(cot, down_m, down_o, gate_slope, up_slope, gate_grad, up_grad):
+    grad_hidden = split_dot(cot, down_m, down_o)
+    gate_grad[...] = (grad_hidden * gate_slope[...]).astype(jnp.bfloat16)
+    up_grad[...] = (grad_hidden * up_slope[...]).astype(jnp.bfloat16)
+
+
+def hidden_grads(cot, down_weights, gate_slope, up_slope):
+    rows = cot.shape[0]
+    depth, columns = down_weights[0].shape
+    tile = 256
+    out = ((rows, columns), jnp.bfloat16, (rows, tile), by_column)
+    return tiled_call(
+        hidden_grad_kernel,
+        "hidden_grads",
+        columns // tile,
+        [(cot.shape, fixed)]
+        + [((depth, tile), by_column)] * 2
+        + [((rows, tile), by_column)] * 2,
+        [out] * 2,
+        (cot, *down_weights, gate_slope, up_slope),
+    )
+
+
+def back_kernel(count, start, *refs):
+    lefts, weights, outs = refs[:count], refs[count : 3 * count], refs[3 * count :]
+    columns = slice(start, start + lefts[0].shape[1])
+    sums = []
+    for half in range(2):
+        terms = [
+            cols_dot(left[...], weights[2 * i + half][:, columns]) for i, left in enumerate(lefts)
+        ]
+        sums.append(sum(terms).astype(jnp.bfloat16))
+    one, two = sums
+    one_keep, one_send, two_keep, two_send = outs
+    n = one.shape[0] // 4
+    one_keep[:n, :], one_send[:n, :] = one[:n], one[n : 2 * n]
+    one_keep[n:, :], one_send[n:, :] = one[2 * n : 3 * n], one[3 * n :]
+    two_keep[...], two_send[...] = two[: 2 * n], two[2 * n :]
+
+
+def project_back(lefts, weights, start=0):
+    rows, width = lefts[0].shape
+    depth = weights[0][0].shape[0]
+    tile = 256
+    flat = [half for pair in weights for half in pair]
+    return tiled_call(
+        functools.partial(back_kernel, len(lefts), start),
+        "project_back",
+        depth // tile,
+        [((rows, width), fixed)] * len(lefts) + [((tile, flat[0].shape[1]), by_row)] * len(flat),
+        [((rows // 2, depth), jnp.bfloat16, (rows // 2, tile), by_column)] * 4,
+        (*lefts, *flat),
+    )
+
+
+def outer_kernel(left, left_other, right, right_other, out):
+    first = rows_dot(left[...], right[...])
+    out[...] = (first + rows_dot(left_other[...], right_other[...])).astype(jnp.bfloat16)
+
+
+def outer(left, left_other, right, right_other, index):
+    rows, width = left.shape[0], right.shape[1]
+    depth = left_other.shape[1] // 2
+    tile = 256 if width % 256 == 0 else width
+    (out,) = tiled_call(
+        outer_kernel,
+        "outer",
+        width // tile,
+        [((rows, depth), lambda step: (0, index))] * 2 + [((rows, tile), by_column)] * 2,
+        [((depth, width), jnp.bfloat16, (depth, tile), by_column)],
+        (left, left_other, right, right_other),
+    )
+    return out
+
+
+def norm_kernel(rows, gain, out):
+    value = rows[...].astype(jnp.float32)
+    scale = lax.rsqrt(jnp.mean(value * value, axis=1, keepdims=True) + norm_eps)
+    out[...] = (value * scale * gain[...]).astype(jnp.bfloat16)
+
+
+def norm_rows(rows, gain):
+    count, width = rows.shape
+    tile = count // 4
+    (out,) = tiled_call(
+        norm_kernel,
+        "norm_rows",
+        4,
+        [((tile, width), by_row), ((1, width), fixed)],
+        [((count, width), jnp.bfloat16, (tile, width), by_row)],
+        (rows, gain.reshape(1, width)),
+    )
+    return out
+
+
+def take_wide_kernel(own, from_near, from_tp, out, sems):
+    n = own.shape[0]
+    moves = [
+        (own, pl.ds(0, n)),
+        (from_tp.at[pl.ds(0, n), :], pl.ds(n, n)),
+        (from_near, pl.ds(2 * n, n)),
+        (from_tp.at[pl.ds(n, n), :], pl.ds(3 * n, n)),
+    ]
+    copies = [
+        pltpu.make_async_copy(source, out.at[rows, :], sems.at[k])
+        for k, (source, rows) in enumerate(moves)
+    ]
+    for copy in copies:
+        copy.start()
+    for copy in copies:
+        copy.wait()
+
+
+def take_wide(own, from_near, from_tp):
+    return pl.pallas_call(
+        take_wide_kernel,
+        out_shape=jax.ShapeDtypeStruct((4 * own.shape[0], own.shape[1]), own.dtype),
+        in_specs=[pl.BlockSpec(memory_space=pl.ANY)] * 3,
+        out_specs=pl.BlockSpec(memory_space=pltpu.VMEM),
+        scratch_shapes=[pltpu.SemaphoreType.DMA((4,))],
+        compiler_params=pltpu.CompilerParams(vmem_limit_bytes=VMEM_BYTES),
+        cost_estimate=SMALL_COST,
+        name="take_wide",
+    )(own, from_near, from_tp)
+
+
+def rows_call(fn, name, where, steps, ins, outs):
+    def kernel(where_ref, *refs):
+        values = [ref[...].astype(jnp.float32) for ref in refs[: len(ins)]]
+        for ref, value in zip(refs[len(ins) :], fn(*values)):
+            ref[...] = value.astype(ref.dtype)
+
+    def spec(rows, columns, place):
+        return pl.BlockSpec((rows, columns), lambda step, ref: (place(step, ref), 0))
+
+    return pl.pallas_call(
+        kernel,
+        grid_spec=pltpu.PrefetchScalarGridSpec(
+            num_scalar_prefetch=1,
+            grid=(steps,),
+            in_specs=[spec(rows, array.shape[1], place) for array, rows, place in ins],
+            out_specs=[spec(rows, shape[1], place) for shape, _, rows, place in outs],
+        ),
+        out_shape=[jax.ShapeDtypeStruct(shape, kind) for shape, kind, _, _ in outs],
+        compiler_params=pltpu.CompilerParams(vmem_limit_bytes=VMEM_BYTES),
+        cost_estimate=SMALL_COST,
+        name=name,
+    )(where, *[array for array, _, _ in ins])
+
+
+def far_halves(where, own, from_x):
+    rows, columns = own.shape[0] // 4, own.shape[1]
+    keep, give = (lambda step, ref: 2 * ref[0] + step), (lambda step, ref: 2 - 2 * ref[0] + step)
+    out = ((2 * rows, columns), jnp.bfloat16, rows, lambda step, ref: step)
+    return rows_call(
+        lambda a, b, c, d: (a + b, c + d),
+        "far_halves",
+        where,
+        2,
+        [(array, rows, place) for place in (keep, give) for array in (own, from_x)],
+        [out, out],
+    )
+
+
+def near_halves(where, pair, from_far):
+    rows, columns = pair.shape[0] // 2, pair.shape[1]
+    keep, give = (lambda step, ref: ref[1]), (lambda step, ref: 1 - ref[1])
+    out = ((rows, columns), jnp.bfloat16, rows, lambda step, ref: 0)
+    return rows_call(
+        lambda a, b, c, d: (a + b, c + d),
+        "near_halves",
+        where,
+        1,
+        [(array, rows, place) for place in (keep, give) for array in (pair, from_far)],
+        [out, out],
+    )
+
+
+def join_halves_kernel(turn, where, own, received, *outs):
+    first = where[1] == 0
+    low_part = jnp.where(first, own[...], received[...]).astype(jnp.float32)
+    high_part = jnp.where(first, received[...], own[...]).astype(jnp.float32)
+    start = 0
+    for out in outs:
+        width = out.shape[0] if turn else out.shape[1]
+        if len(outs) == 1:
+            size = own.shape[1]
+            rest = width - size
+        else:
+            size = rest = width // 2
+        left, right = low_part[:, start : start + size], high_part[:, start : start + rest]
+        if turn:
+            out[:size, :] = left.T
+            out[size:, :] = right.T
+        else:
+            out[:, :size] = left
+            out[:, size:] = right
+        start += size
+
+
+def join_halves(where, own, received, widths, turn=False):
+    rows = own.shape[0]
+    shapes = [(width, rows) if turn else (rows, width) for width in widths]
+    whole = pl.BlockSpec(memory_space=pltpu.VMEM)
+    return pl.pallas_call(
+        functools.partial(join_halves_kernel, turn),
+        out_shape=[jax.ShapeDtypeStruct(shape, jnp.float32) for shape in shapes],
+        in_specs=[pl.BlockSpec(memory_space=pltpu.SMEM), whole, whole],
+        out_specs=[whole] * len(shapes),
+        compiler_params=pltpu.CompilerParams(vmem_limit_bytes=VMEM_BYTES),
+        cost_estimate=SMALL_COST,
+        name="join_halves",
+    )(where, own, received)
+
+
+def split_halves_kernel(plan, where, *refs):
+    arrays, pairs, other = refs[: len(plan)], refs[len(plan) : -1], refs[-1]
+    rows = other.shape[0]
+    first = where[1] == 0
+    offset = 0
+    filled = [0] * len(pairs)
+    for index, (array, (target, size, turn)) in enumerate(zip(arrays, plan)):
+        value = array[...]
+        if turn:
+            value = value.astype(jnp.float32).T.astype(jnp.bfloat16)
+        low_part, high_part = value[:, :size], value[:, size:]
+        missing = size - high_part.shape[1]
+        if missing:
+            high_part = jnp.concatenate(
+                [high_part, jnp.zeros((rows, missing), jnp.bfloat16)], axis=1
+            )
+        start = filled[target]
+        pair = pairs[target]
+        pair[:rows, start : start + size] = jnp.where(first, low_part, high_part)
+        other[:, offset + start : offset + start + size] = jnp.where(first, high_part, low_part)
+        filled[target] = start + size
+        if index + 1 == len(plan) or plan[index + 1][0] != target:
+            spare = pair.shape[1] - filled[target]
+            if spare:
+                pair[:rows, filled[target] :] = jnp.zeros((rows, spare), jnp.bfloat16)
+                end = offset + pair.shape[1]
+                other[:, end - spare : end] = jnp.zeros((rows, spare), jnp.bfloat16)
+            offset += pair.shape[1]
+
+
+def split_halves(where, arrays, plan, widths):
+    rows = D // 16
+    whole = pl.BlockSpec(memory_space=pltpu.VMEM)
+    return pl.pallas_call(
+        functools.partial(split_halves_kernel, plan),
+        out_shape=[jax.ShapeDtypeStruct((2 * rows, width), jnp.bfloat16) for width in widths]
+        + [jax.ShapeDtypeStruct((rows, sum(widths)), jnp.bfloat16)],
+        in_specs=[pl.BlockSpec(memory_space=pltpu.SMEM)] + [whole] * len(arrays),
+        out_specs=[whole] * (len(widths) + 1),
+        compiler_params=pltpu.CompilerParams(vmem_limit_bytes=VMEM_BYTES),
+        cost_estimate=SMALL_COST,
+        name="split_halves",
+    )(where, *arrays)
+
+
+def pair_kernel(first, second, out):
+    n = first.shape[0]
+    out[:n, :] = first[...]
+    out[n:, :] = second[...]
+
+
+def pair_rows(first, second):
+    rows, columns = first.shape
+    (out,) = dense_call(
+        pair_kernel, "pair_rows", [((2 * rows, columns), first.dtype)], [], (first, second)
+    )
+    return out
+
+
+def middle_kernel(one, got_one, two, got_two, next_one, next_two, sum_one, sum_two):
+    n = sum_one.shape[0]
+    for keep, got, later, total in (
+        (one, got_one, next_one, sum_one),
+        (two, got_two, next_two, sum_two),
+    ):
+        both = keep[...].astype(jnp.float32) + got[...].astype(jnp.float32)
+        total[...] = both[:n]
+        later[...] = both[n:].astype(jnp.bfloat16)
+
+
+def scatter_middle(one, got_one, two, got_two):
+    rows, columns = one.shape[0] // 2, one.shape[1]
+    return dense_call(
+        middle_kernel,
+        "scatter_middle",
+        [((rows, columns), jnp.bfloat16)] * 2 + [((rows, columns), jnp.float32)] * 2,
+        [],
+        (one, got_one, two, got_two),
+    )
+
+
+def summed(sum_one, sum_two, last_one, last_two):
+    one = sum_one[...] + last_one[...].astype(jnp.float32)
+    two = sum_two[...] + last_two[...].astype(jnp.float32)
+    return jnp.concatenate([one, two], axis=1)
+
+
+def store_halves(value, one, two):
+    half = one.shape[1]
+    one[...] = value[:, :half].astype(one.dtype)
+    two[...] = value[:, half:].astype(two.dtype)
+
+
+def residual_kernel(sum_one, sum_two, last_one, last_two, rows, gain, residual, one, two):
+    value = rows[...].astype(jnp.float32) + summed(sum_one, sum_two, last_one, last_two)
+    residual[...] = value
+    scale = lax.rsqrt(jnp.mean(value * value, axis=1, keepdims=True) + norm_eps)
+    store_halves(value * scale * gain[...], one, two)
+
+
+def norm_grad(grad, value, gain):
+    scale = lax.rsqrt(jnp.mean(value * value, axis=1, keepdims=True) + norm_eps)
+    scaled = grad * gain
+    inner = jnp.mean(scaled * value, axis=1, keepdims=True)
+    gain_term = jnp.sum(grad * value * scale, axis=0, keepdims=True)
+    return scale * scaled - value * (scale * scale * scale) * inner, gain_term
+
+
+def residual_grad_kernel(
+    sum_one, sum_two, last_one, last_two, residual, gain, cot, grad, gain_term, one, two
+):
+    back, term = norm_grad(summed(sum_one, sum_two, last_one, last_two), residual[...], gain[...])
+    value = cot[...].astype(jnp.float32) + back
+    grad[...] = value
+    gain_term[...] = term
+    store_halves(value, one, two)
+
+
+def token_grad_kernel(
+    sum_one, sum_two, last_one, last_two, rows, gain, grad_residual, grad, gain_term
+):
+    value = rows[...].astype(jnp.float32)
+    back, term = norm_grad(summed(sum_one, sum_two, last_one, last_two), value, gain[...])
+    grad[...] = grad_residual[...] + back
+    gain_term[...] = term
+
+
+def mixed_kernel(sum_one, sum_two, last_one, last_two, residual, mixed):
+    total = residual[...] + summed(sum_one, sum_two, last_one, last_two)
+    mixed[...] = total.astype(jnp.bfloat16)
+
+
 def half_plan(
     tokens, doc_lengths, w_query, w_key, w_value, w_out, w_gate, w_up, w_down, norm_gains, cotangent
 ):
@@ -700,91 +1127,58 @@
             pieces.append(lax.dynamic_slice_in_dim(value, place * quarter, quarter, 1))
         return jnp.concatenate(pieces, axis=1)
 
-    def both_halves(array, size):
-        low_part = array[:, :size]
-        high_part = array[:, size:]
-        high_part = jnp.pad(high_part, ((0, 0), (0, size - high_part.shape[1])))
-        first = near == 0
-        return jnp.where(first, low_part, high_part), jnp.where(first, high_part, low_part)
-
-    def z_stage(halves):
-        own, other = halves
-        return own, to_z(other, 1), to_z(own, 2), to_z(other, 3)
-
-    def joined(own, received, width):
-        first = near == 0
-        size = own.shape[1]
-        low_part = jnp.where(first, own, received)
-        high_part = jnp.where(first, received, own)[:, : width - size]
-        return jnp.concatenate([low_part, high_part], axis=1)
-
-    def gather_rows(value):
-        half = value.shape[1] // 2
-        one, two = value[:, :half], value[:, half:]
-        one_near, two_tp = to_z(one, 1), to_tp(two)
-        one_far = to_tp(jnp.concatenate([one, one_near], axis=0))
-        two_far = to_z(jnp.concatenate([two, two_tp], axis=0), 1)
-        return value, one_near, one_far, two_tp, two_far
-
-    def scatter_start(one, two):
-        n = local_rows
-        send_one = jnp.concatenate([one[n : 2 * n], one[3 * n :]], axis=0)
-        return one, two, to_tp(send_one), to_z(two[2 * n :], 1)
-
-    def scatter_end(one, two, got_one, got_two):
-        n = local_rows
-        next_one = low_of(float_of(one[2 * n : 3 * n]) + float_of(got_one[n:]))
-        next_two = low_of(float_of(two[n : 2 * n]) + float_of(got_two[n:]))
-        last_one = to_z(next_one, 1)
-        last_two = to_tp(next_two)
-        sum_one = float_of(one[:n]) + float_of(got_one[:n]) + float_of(last_one)
-        sum_two = float_of(two[:n]) + float_of(got_two[:n]) + float_of(last_two)
-        return jnp.concatenate([sum_one, sum_two], axis=1)
-
-    def grad_pair(left, right):
-        other = low_of(rows_dot(left[:, middle:], right))
-        from_core = to_core(other)
-        return low_of(rows_dot(left[:, :middle], right)), from_core
-
-    def x_send(mine, from_core):
-        return low_of(float_of(mine[quarter:]) + float_of(from_core[quarter:]))
-
-    def z_pieces(mine, from_core, from_x):
-        total = low_of(
-            float_of(mine[:quarter]) + float_of(from_core[:quarter]) + float_of(from_x)
-        )
-        return [
-            lax.dynamic_slice_in_dim(total, (seq_index ^ k) * block_rows, block_rows, 0)
-            for k in range(4)
-        ]
-
-    def z_send(pieces):
-        return pieces[0], to_z(pieces[1], 1), to_z(pieces[2], 2), to_z(pieces[3], 3)
-
-    def z_sum(own, from_near, from_far, from_last, width):
-        return joined(
-            float_of(own) + float_of(from_far), float_of(from_near) + float_of(from_last), width
-        )
-
+    def gather_first(one, two):
+        return one, two, to_z(one, 1), to_tp(two)
+
+    def gather_second(one, two, one_near, two_tp):
+        one_far = to_tp(pair_rows(one, one_near))
+        two_far = to_z(pair_rows(two, two_tp), 1)
+        return one, two, one_near, one_far, two_tp, two_far
+
+    def scatter_first(one_keep, one_send, two_keep, two_send):
+        return one_keep, to_tp(one_send), two_keep, to_z(two_send, 1)
+
+    def scatter_second(next_one, next_two, sum_one, sum_two):
+        return sum_one, sum_two, to_z(next_one, 1), to_tp(next_two)
+
+    where = jnp.stack([far, near]).astype(jnp.int32)
     query_width = w_query.shape[1] // 2
     key_width = w_key.shape[1] // 2
-    kv_local = key_width // HEAD_DIM
     query_heads = query_width // HEAD_DIM
     heads_width = -(-(query_width + 2 * key_width) // 128) * 128
     hidden_width = -(-(w_gate.shape[1] // 2) // 128) * 128
-    heads_parts = [
-        both_halves(w_query, query_width),
-        both_halves(w_key, key_width),
-        both_halves(w_value, key_width),
-    ]
+    row_shape = (local_rows, D)
+    half_shape = (local_rows, middle)
+
+    tokens_in = columns_in(tokens)
+    cot_in = columns_in(cotangent)
+    first_width = heads_width + query_width
+    plan = ((0, query_width, False), (0, key_width, False), (0, key_width, False))
     spare = heads_width - query_width - 2 * key_width
-    heads_halves = [
-        jnp.pad(jnp.concatenate([part[i] for part in heads_parts], axis=1), ((0, 0), (0, spare)))
-        for i in range(2)
-    ]
+    first_pair, first_other = split_halves(
+        where,
+        (w_query, w_key, w_value, jnp.zeros((block_rows, 2 * spare), jnp.bfloat16), w_out),
+        (*plan, (0, spare, False), (0, query_width, True)),
+        (first_width,),
+    )
     gain_stack = norm_gains[None]
-    for step in (1, 2):
-        gain_stack = jnp.concatenate([gain_stack, to_z(gain_stack, step)], axis=0)
+    gain_stack = jnp.concatenate([gain_stack, to_z(gain_stack, 1)], axis=0)
+    first_near = to_z(first_other, 1)
+    token_wait = gather_first(tokens_in[:, :middle], tokens_in[:, middle:])
+    gain_far = to_z(hold(gain_stack, token_wait[2:]), 2)
+    gain_stack = jnp.concatenate([gain_stack, gain_far], axis=0)
+    first_pair = fill_rows(*hold((first_pair, first_near), gain_stack))
+    first_far = to_z(first_pair, 2)
+    token_wait = gather_second(*hold(token_wait, first_pair))
+    gate_pair, gate_other = split_halves(
+        where, (w_gate,), ((0, hidden_width, False),), (hidden_width,)
+    )
+    up_pair, up_other = split_halves(where, (w_up,), ((0, hidden_width, False),), (hidden_width,))
+    down_pair, down_other = split_halves(
+        where, (w_down,), ((0, hidden_width, True),), (hidden_width,)
+    )
+    gate_near = to_z(hold(gate_other, first_pair), 1)
+    token_wait = hold(token_wait, gate_other, up_other, down_other)
     gain_plane = jnp.concatenate(
         [
             lax.dynamic_index_in_dim(gain_stack, seq_index ^ k, 0, keepdims=False)
@@ -794,21 +1188,9 @@
     )
     gain_mine = jnp.concatenate([gain_plane, to_x(gain_plane)], axis=1)
     gains = float_of(jnp.concatenate([gain_mine, to_core(gain_mine)], axis=1))
-    gain_one = gains[0]
-    gain_two = gains[1]
-    heads_z = z_stage(heads_halves)
-    tokens_in = columns_in(tokens)
-    token_rows = float_of(tokens_in)
-    inv_one = rms_scale(token_rows)
-    heads_plane, heads_mine = place_rows(hold(heads_z, gain_stack), seq_index)
-    heads_x = to_x(heads_plane)
-    normed_rows = low_of(token_rows * inv_one * gain_one)
-    normed_wait = gather_rows(hold(normed_rows, heads_plane))
-    out_z = z_stage(hold(both_halves(w_out.T, query_width), heads_z[1]))
-    gate_z = z_stage(hold(both_halves(w_gate, hidden_width), heads_z[2:]))
-    up_z = z_stage(hold(both_halves(w_up, hidden_width), out_z[2:]))
-    down_z = z_stage(hold(both_halves(w_down.T, hidden_width), gate_z[2:]))
-    out_plane, out_mine = place_rows(hold(out_z, normed_rows), seq_index)
+    gain_one = gains[0:1]
+    gain_two = gains[1:2]
+    token_span = take_rows(*hold(token_wait, gains))
 
     row_ids = jnp.arange(local_rows, dtype=jnp.int32)
     own_positions = jnp.concatenate(
@@ -834,15 +1216,24 @@
     query_ids = jnp.stack([doc_of(own_positions), own_positions // BLOCK])
     key_ids = jnp.stack([key_docs, key_positions // BLOCK], axis=1)
 
-    heads_mine = fill_rows(*hold((heads_mine, heads_x), out_plane))
-    heads_weights = heads_mine, to_core(heads_mine)
-    out_x = to_x(out_plane)
-    normed_one = take_rows(*hold(normed_wait, heads_mine))
-    cot_in = columns_in(cotangent)
-    cot_wait = gather_rows(hold(cot_in, normed_one))
-    gate_plane, gate_mine = place_rows(hold(gate_z, heads_mine), seq_index)
-    gate_x = to_x(gate_plane)
-    raw = wide_dot(hold(normed_one, gate_plane), heads_weights)
+    gate_pair = fill_rows(*hold((gate_pair, gate_near), token_span))
+    first_plane, first_mine = place_rows(*hold((first_pair, first_far), gate_pair), seq_index)
+    first_x = to_x(first_plane)
+    gate_far = to_z(hold(gate_pair, first_plane), 2)
+    normed_one = norm_rows(hold(token_span, first_plane), gain_one)
+    normed_other = to_core(normed_one[:, middle:])
+    up_pair = fill_rows(up_pair, to_z(hold(up_other, first_plane), 1))
+    down_pair = fill_rows(down_pair, to_z(hold(down_other, first_plane), 1))
+    cot_first = gather_first(*hold((cot_in[:, :middle], cot_in[:, middle:]), up_pair))
+    gate_plane, gate_mine = place_rows(
+        *hold((gate_pair, gate_far), cot_first[2:], down_pair, normed_one), seq_index
+    )
+    first_mine = fill_rows(*hold((first_mine, first_x), gate_plane))
+    first_weights = first_mine, to_core(first_mine)
+    gate_x = to_x(hold(gate_plane, first_mine))
+    up_far = to_z(hold(up_pair, gate_plane), 2)
+    cot_wait = gather_second(*hold(cot_first, first_mine))
+    raw = project(normed_one, first_weights, 0, heads_width, jnp.float32)
     query_rot, own_kv = dense_call(
         rope_kernel,
         "rope",
@@ -853,11 +1244,12 @@
         [],
         (raw, cos_wide, sin_wide),
     )
-    early_kv = lax.ppermute(own_kv, "seq", [(0, 2), (1, 3)])
-    out_mine = fill_rows(*hold((out_mine, out_x), own_kv))
-    out_weights = out_mine, to_core(out_mine)
-    cot_span = take_rows(*hold(cot_wait, out_mine))
-    query_rot = hold(query_rot, cot_span)
+    cot_span = take_rows(*hold(cot_wait, own_kv))
+    up_plane, up_mine = place_rows(*hold((up_pair, up_far), cot_span), seq_index)
+    early_kv = lax.ppermute(hold(own_kv, up_plane), "seq", [(0, 2), (1, 3)])
+    gate_mine = fill_rows(*hold((gate_mine, gate_x), up_plane))
+    gate_weights = gate_mine, to_core(gate_mine)
+    up_x = to_x(hold(up_plane, gate_mine))
     attended_low, log_total = dense_call(
         functools.partial(attend_kernel, score_scale),
         "attend",
@@ -868,70 +1260,80 @@
         [pltpu.VMEM((2 * group_rows, group_rows // 2), jnp.float32)],
         (query_rot, early_kv, own_kv, query_ids, key_ids),
     )
-    up_plane, up_mine = place_rows(hold(up_z, log_total), seq_index)
-    up_x = to_x(up_plane)
-    branch = scatter_start(
-        *[low_of(cols_dot(hold(attended_low, up_plane), w)) for w in out_weights]
-    )
-    gate_mine = fill_rows(*hold((gate_mine, gate_x), branch[:2]))
-    gate_weights = gate_mine, to_core(gate_mine)
-    attn_branch = scatter_end(*hold(branch, gate_mine))
-    residual = token_rows + attn_branch
-    inv_two = rms_scale(residual)
-    normed_two = low_of(residual * inv_two * gain_two)
-    two_wait = gather_rows(normed_two)
-    down_plane, down_mine = place_rows(hold(down_z, normed_two), seq_index)
-    down_x = to_x(down_plane)
+    attended_other = to_core(attended_low)
+    down_far = to_z(hold(down_pair, log_total), 2)
+    branch = scatter_first(
+        *project_back([attended_low], [first_weights], heads_width)
+    )
+    branch = scatter_middle(*branch)
+    branch = scatter_second(*branch)
+    down_plane, down_mine = place_rows(*hold((down_pair, down_far), branch[:2]), seq_index)
     up_mine = fill_rows(*hold((up_mine, up_x), down_plane))
     up_weights = up_mine, to_core(up_mine)
-    span_two = take_rows(*hold(two_wait, up_mine))
-    gate_pre = wide_dot(span_two, gate_weights)
-    up_pre = wide_dot(span_two, up_weights)
-    sig_gate = jax.nn.sigmoid(gate_pre)
-    silu_gate = gate_pre * sig_gate
-    hidden_low = low_of(silu_gate * up_pre)
-    down_pair = grad_pair(cot_span, hidden_low)
-    down_send = x_send(*down_pair)
-    down_back = to_x(down_send)
-    down_mine = fill_rows(*hold((down_mine, down_x), down_send))
+    down_x = to_x(hold(down_plane, up_mine))
+    residual, two_one, two_two = dense_call(
+        residual_kernel,
+        "residual",
+        [(row_shape, jnp.float32)] + [(half_shape, jnp.bfloat16)] * 2,
+        [],
+        (*hold(branch, up_mine), tokens_in, gain_two),
+    )
+    two_wait = gather_second(*gather_first(two_one, two_two))
+    span_two = take_rows(*two_wait)
+    span_other = to_core(span_two[:, middle:])
+    cot_other = to_core(hold(cot_span[:, middle:], log_total))
+    hidden_low, gate_slope, up_slope = hidden_units(span_two, gate_weights, up_weights)
+    hidden_other = to_core(hidden_low)
+    down_mine = fill_rows(*hold((down_mine, down_x), hidden_low))
     down_weights = down_mine, to_core(down_mine)
-    grad_hidden = wide_dot(cot_span, down_weights)
-    grad_gate_pre = low_of(grad_hidden * up_pre * (sig_gate * (1.0 + gate_pre * (1.0 - sig_gate))))
-    grad_up_pre = low_of(grad_hidden * silu_gate)
-    normed_back = scatter_start(
-        *[
-            low_of(cols_dot(grad_gate_pre, gate_w) + cols_dot(grad_up_pre, up_w))
-            for gate_w, up_w in zip(gate_weights, up_weights)
-        ]
-    )
-    gate_pair = grad_pair(hold(span_two, normed_back[:2]), grad_gate_pre)
-    up_pair = grad_pair(hold(span_two, gate_pair[0]), grad_up_pre)
-    gate_send = x_send(*hold(gate_pair, up_pair[0]))
-    gate_back = to_x(gate_send)
-    down_pieces = z_pieces(*hold((*down_pair, down_back), gate_send))
-    down_done = z_send(down_pieces)
-    grad_normed_two = scatter_end(*hold(normed_back, down_pieces))
-    gain_two_term = jnp.sum(grad_normed_two * residual * inv_two, axis=0)
-    scaled_two = grad_normed_two * gain_two
-    grad_residual = (
-        float_of(cot_in)
-        + inv_two * scaled_two
-        - residual
-        * (inv_two * inv_two * inv_two)
-        * jnp.mean(scaled_two * residual, axis=-1, keepdims=True)
-    )
-    grad_residual_low = low_of(grad_residual)
-    grad_wait = gather_rows(grad_residual_low)
-    up_send = x_send(*hold(up_pair, grad_residual_low))
-    up_back = to_x(up_send)
-    mlp_parts = [low_of(cols_dot(hold(hidden_low, up_send), w)) for w in down_weights]
-    gate_pieces = z_pieces(*hold((*gate_pair, gate_back), mlp_parts))
-    gate_done = z_send(gate_pieces)
-    hidden_units = w_gate.shape[1]
-    grad_down = z_sum(*hold(down_done, gate_pieces), hidden_units).T
-    grad_span = take_rows(*hold(grad_wait, gate_pieces))
-    grad_attended = low_of(wide_dot(grad_span, out_weights))
-    branch_mlp = scatter_start(*hold(mlp_parts, grad_span))
+
+    down_parts = hold((cot_span, cot_other, hidden_low, hidden_other), down_mine)
+    down_give = outer(*down_parts, 1)
+    down_back = to_x(down_give)
+    mlp_parts = project_back([hold(hidden_low, down_give)], [down_weights])
+    grad_gate_pre, grad_up_pre = hidden_grads(
+        hold(cot_span, mlp_parts), down_weights, gate_slope, up_slope
+    )
+    gate_other = to_core(grad_gate_pre)
+    up_other = to_core(grad_up_pre)
+    branch_mlp = scatter_first(*mlp_parts)
+    back_parts = project_back(
+        [grad_gate_pre, grad_up_pre], [gate_weights, up_weights]
+    )
+    branch_mlp = scatter_middle(*hold(branch_mlp, back_parts))
+    normed_back = scatter_first(*hold(back_parts, branch_mlp))
+    down_keep = outer(*hold(down_parts, branch_mlp), 0)
+    gate_parts = hold((span_two, span_other, grad_gate_pre, gate_other), down_keep)
+    gate_give = outer(*gate_parts, 1)
+    down_keep, down_give = far_halves(where, *hold((down_keep, down_back), gate_give))
+    down_far = to_z(down_give, 2)
+    gate_back = to_x(hold(gate_give, down_give))
+    normed_back = scatter_second(*scatter_middle(*hold(normed_back, down_give)))
+    gate_keep = outer(*hold(gate_parts, normed_back[:2]), 0)
+    up_parts = hold((span_two, span_other, grad_up_pre, up_other), gate_keep)
+    up_give = outer(*up_parts, 1)
+    up_keep = outer(*hold(up_parts, up_give), 0)
+    grad_residual, gain_two_term, grad_one, grad_two = dense_call(
+        residual_grad_kernel,
+        "residual_grad",
+        [(row_shape, jnp.float32), ((1, D), jnp.float32)] + [(half_shape, jnp.bfloat16)] * 2,
+        [],
+        (*hold(normed_back, up_keep), residual, gain_two, cot_in),
+    )
+    grad_wait = gather_first(grad_one, grad_two)
+    down_own, down_other = near_halves(where, *hold((down_keep, down_far), grad_one))
+    gate_keep, gate_give = far_halves(where, *hold((gate_keep, gate_back), down_other))
+    gate_far = to_z(gate_give, 2)
+    up_back = to_x(hold(up_give, gate_give))
+    grad_wait = gather_second(*hold(grad_wait, gate_give))
+    gate_own, gate_other = near_halves(where, *hold((gate_keep, gate_far), grad_wait[2::2]))
+    up_keep, up_give = far_halves(where, *hold((up_keep, up_back), gate_other))
+    up_far = to_z(up_give, 2)
+    grad_span = take_rows(*hold(grad_wait, up_give))
+    down_near = to_z(hold(down_other, grad_span), 1)
+    gate_near = to_z(hold(gate_other, grad_span), 1)
+    span_grad_other = to_core(grad_span[:, middle:])
+    grad_attended = project(grad_span, first_weights, heads_width, query_width, jnp.bfloat16)
     grad_query, grad_early, grad_own = dense_call(
         functools.partial(attend_back_kernel, score_scale),
         "attend_back",
@@ -952,70 +1354,81 @@
             query_ids,
             key_ids,
             log_total,
-            hold(grad_attended, grad_down),
+            grad_attended,
             cos_wide,
             sin_wide,
         ),
     )
-    late_kv = lax.ppermute(grad_early, "seq", [(2, 0), (3, 1)])
-    out_pair = grad_pair(hold(grad_span, grad_early), attended_low)
-    mlp_branch = scatter_end(*hold(branch_mlp, out_pair[0]))
-    mixed_out = columns_out(low_of(residual + mlp_branch))
-    out_send = x_send(*out_pair)
-    out_back = to_x(out_send)
-    up_pieces = z_pieces(*hold((*up_pair, up_back), out_send))
-    up_done = z_send(up_pieces)
+    up_own, up_other = near_halves(where, *hold((up_keep, up_far), grad_early))
+    late_kv = lax.ppermute(hold(grad_early, up_other), "seq", [(2, 0), (3, 1)])
+    out_parts = hold((grad_span, span_grad_other, attended_low, attended_other), up_other)
+    up_near = to_z(hold(up_other, late_kv), 1)
+    out_give = outer(*out_parts, 1)
+    out_back = to_x(out_give)
+    out_keep = outer(*out_parts, 0)
     (grad_raw,) = dense_call(
         join_kernel,
         "join",
         [((group_rows, heads_width), jnp.bfloat16)],
         [],
-        (grad_query, grad_own, hold(late_kv, up_pieces), cos_wide, sin_wide),
-    )
-    heads_pair = grad_pair(normed_one, grad_raw)
-    first_back = scatter_start(
-        *[low_of(cols_dot(hold(grad_raw, heads_pair[0]), w)) for w in heads_weights]
-    )
-    heads_send = x_send(*hold(heads_pair, first_back[:2]))
-    heads_back = to_x(heads_send)
-    grad_gate = z_sum(*hold(gate_done, heads_send), hidden_units)
-    out_pieces = z_pieces(*hold((*out_pair, out_back), heads_send))
-    out_done = z_send(out_pieces)
-    grad_normed_one = scatter_end(*hold(first_back, out_pieces, grad_gate))
-    scaled_one = grad_normed_one * gain_one
-    grad_tokens = columns_out(
-        grad_residual
-        + inv_one * scaled_one
-        - token_rows
-        * (inv_one * inv_one * inv_one)
-        * jnp.mean(scaled_one * token_rows, axis=-1, keepdims=True)
-    )
-    gain_one_term = jnp.sum(grad_normed_one * token_rows * inv_one, axis=0)
-    gain_rows = jnp.stack([gain_one_term, gain_two_term])
-    heads_pieces = z_pieces(*hold((*heads_pair, heads_back), gain_rows))
-    heads_done = z_send(heads_pieces)
+        (grad_query, grad_own, hold(late_kv, out_give, out_keep, down_near, gate_near), cos_wide, sin_wide),
+    )
+    raw_other = to_core(grad_raw)
+    first_parts = project_back([grad_raw], [first_weights])
+    first_back = scatter_first(*first_parts)
+    heads_parts = hold((normed_one, normed_other, grad_raw, raw_other), first_parts, up_near)
+    heads_give = outer(*heads_parts, 1)
+    heads_back = to_x(heads_give)
+    out_keep, out_give = far_halves(where, *hold((out_keep, out_back), heads_give))
+    out_far = to_z(out_give, 2)
+    heads_keep = outer(*hold(heads_parts, out_give), 0)
+    units = w_gate.shape[1]
+    first_back = scatter_middle(*hold(first_back, heads_keep, heads_give))
+    heads_keep, heads_give = far_halves(where, *hold((heads_keep, heads_back), first_back))
+    heads_far = to_z(heads_give, 2)
+    first_back = scatter_second(*hold(first_back, heads_give))
+    out_own, out_other = near_halves(where, *hold((out_keep, out_far), first_back[:2]))
+    out_near = to_z(out_other, 1)
+    grad_rows, gain_one_term = dense_call(
+        token_grad_kernel,
+        "token_grad",
+        [(row_shape, jnp.float32), ((1, D), jnp.float32)],
+        [],
+        (*hold(first_back, out_other), tokens_in, gain_one, grad_residual),
+    )
+    gain_rows = jnp.concatenate([gain_one_term, gain_two_term], axis=0)
+    (grad_down,) = join_halves(where, *hold((down_own, down_near), grad_rows), (units,), True)
+    (grad_gate,) = join_halves(where, *hold((gate_own, gate_near), grad_down), (units,))
+    (grad_up,) = join_halves(where, *hold((up_own, up_near), grad_gate), (units,))
+    heads_own, heads_other = near_halves(where, *hold((heads_keep, heads_far), grad_up))
+    heads_near = to_z(heads_other, 1)
+    gain_rows = hold(gain_rows, heads_other)
     gain_rows = gain_rows[:, :middle] + to_core(gain_rows[:, middle:])
     gain_rows = gain_rows[:, :quarter] + to_x(gain_rows[:, quarter:])
     gain_rows = gain_rows + to_tp(gain_rows)
+    branch_mlp = scatter_second(*hold(branch_mlp, heads_other))
+    (grad_out,) = join_halves(
+        where, *hold((out_own, out_near), gain_rows), (w_out.shape[0],), True
+    )
+    (mixed,) = dense_call(
+        mixed_kernel,
+        "mixed",
+        [(row_shape, jnp.bfloat16)],
+        [],
+        (*hold(branch_mlp, grad_out), residual),
+    )
+    mixed_out = columns_out(mixed)
+    grad_tokens = columns_out(grad_rows)
     gain_blocks = gain_rows.reshape(2, 4, block_rows)
-    gain_grads = sum(
-        to_z(piece, k) if k else piece
-        for k, piece in (
-            (k, lax.dynamic_index_in_dim(gain_blocks, seq_index ^ k, 1, keepdims=False))
-            for k in range(4)
-        )
-    )
-    grad_up = z_sum(*hold(up_done, heads_pieces), hidden_units)
-    grad_out = z_sum(*hold(out_done, grad_up), w_out.shape[0]).T
-    heads_own, heads_near, heads_far, heads_last = hold(heads_done, grad_out)
-    heads_first = float_of(heads_own) + float_of(heads_far)
-    heads_second = float_of(heads_near) + float_of(heads_last)
-    splits = (query_width, query_width + key_width, query_width + 2 * key_width)
-    grad_query_w, grad_key_w, grad_value_w = (
-        joined(own, other, 2 * own.shape[1])
-        for own, other in list(
-            zip(jnp.split(heads_first, splits, axis=1), jnp.split(heads_second, splits, axis=1))
-        )[:3]
+    gain_pair = [
+        lax.dynamic_index_in_dim(gain_blocks, seq_index ^ k, 1, keepdims=False) for k in range(4)
+    ]
+    gain_half = jnp.stack(gain_pair[:2]) + to_z(jnp.stack(gain_pair[2:]), 2)
+    gain_grads = gain_half[0] + to_z(gain_half[1], 1)
+    grad_query_w, grad_key_w, grad_value_w = join_halves(
+        where,
+        *(heads_own, heads_near),
+        (2 * query_width, 2 * key_width, 2 * key_width),
     )
     return (
         mixed_out,

time: 846 us -> 828 us (0.979)
  Pallas kernels: 73.9 us -> 234 us
  matrix products: 101 us -> 0 us
  other arithmetic: 66.2 us -> 10.9 us
  local copies, waits for them, and re-layouts: 17.1 us -> 56.8 us
  waiting for transfers between devices: 458 us -> 420 us
  starting transfers between devices: 113 us -> 90.4 us
    pallas_call x9 -> x50, Pallas kernels: 14.8 us -> 177 us  [the longest x19 124 us: tiled_call(): pl.pallas_call(kernel, grid=(steps,), out_shape=[jax.ShapeDtypeStruct(sha...]
    dot_general x30 -> x0, matrix products: 101 us -> none  [the longest x10 37.7 us: wide_dot(): jnp.dot(left[:, i * depth:(i + 1) * depth], piece, preferred_element_type...]
    ppermute x12 -> x11, waiting for transfers between devices: 114 us -> 49.9 us  [to_x(): return lax.ppermute(value, 'fsdp', [(i, i ^ 2) for i in range(4)])]
    ppermute x51 -> x38, waiting for transfers between devices: 244 us -> 306 us  [to_z(): return lax.ppermute(value, 'seq', [(i, i ^ step) for i in range(4)])]
    unnamed x230 -> x241, local copies, waits for them, and re-layouts: 11.7 us -> 46.3 us
    convert_element_type x23 -> x0, other arithmetic: 30.6 us -> none  [the longest x22 30.6 us: low_of(): return value.astype(jnp.bfloat16)]
    ppermute x51 -> x38, starting transfers between devices: 78.7 us -> 53 us  [to_z(): return lax.ppermute(value, 'seq', [(i, i ^ step) for i in range(4)])]
    ppermute x17, waiting for transfers between devices: 50.5 us -> 30.1 us  [to_tp(): return lax.ppermute(value, 'tp', [(0, 1), (1, 0)])]
  transfers between devices with their start and end apart: 94 -> 83, of which waited for: 44 -> 35; matrix products, arithmetic and copies ran while one was open for 15% -> 3% of each run, Pallas kernels for 8% -> 26%
where the time goes in v3:
time: 828 us; the launch traced here: 814 us
  waiting for transfers between devices  420 us (51%)
  Pallas kernels  234 us (28%)
  starting transfers between devices  90.4 us (11%)
  local copies, waits for them, and re-layouts  56.8 us (7%)
  other arithmetic  10.9 us (1%)
    ppermute x38, waiting for transfers between devices, to_z(): return lax.ppermute(value, 'seq', [(i, i ^ step) for i in range(4)])  306 us
    pallas_call x19, Pallas kernels, tiled_call(): pl.pallas_call(kernel, grid=(steps,), out_shape=[jax.ShapeDtypeStruct(sha...  124 us
    ppermute x38, starting transfers between devices, to_z(): return lax.ppermute(value, 'seq', [(i, i ^ step) for i in range(4)])  53 us
    ppermute x11, waiting for transfers between devices, to_x(): return lax.ppermute(value, 'fsdp', [(i, i ^ 2) for i in range(4)])  49.9 us
    unnamed x241, local copies, waits for them, and re-layouts  46.3 us
    pallas_call x20, Pallas kernels, dense_call(): pl.pallas_call(kernel, out_shape=[jax.ShapeDtypeStruct(shape, kind) for s...  43.2 us
    ppermute x17, waiting for transfers between devices, to_tp(): return lax.ppermute(value, 'tp', [(0, 1), (1, 0)])  30.1 us
    pallas_call x8, Pallas kernels, fill_rows(): pl.pallas_call(lambda *refs: fill_kernel(rows, part, start, *refs), out_s...  17.5 us
  transfers between devices with their start and end apart: 83, of which 35 were waited for; matrix products, arithmetic and copies ran while one was open for 3% of the time, Pallas kernels for 26%

profile of v3, /device:TPU:18, one launch (start us, length us, event | category | flops | bytes accessed | tf_op | source)
XLA Modules:
  0.0 814.2 jit_solution(5794686079402103919)
XLA Ops:
  11.9 16.9 %collective-permute-done.3 = bf16[1,2,160]{2,1,0:T(2,128)(2,1)S(1)} collective-permute-done((bf16[1,2,160]{2,1,0:T(2,128)(2,1)S(1)}, bf16[1,2,160]{2,1,0:T(2,128)(2,1)S(1)}, u32[]{:S(2)}, u32[]{:S(2)}) %collective-permute-start.3) | collective-permute-done | bytes 672 | tf_op jit(solution)/shard_map/ppermute | solution.py:372
  53.5 23.3 %collective-permute-done.6.two_far = bf16[256,1280]{1,0:T(8,128)(2,1)} collective-permute-done((bf16[256,1280]{1,0:T(8,128)(2,1)}, bf16[256,1280]{1,0:T(8,128)(2,1)}, u32[]{:S(2)}, u32[]{:S(2)}) %collective-permute-start.6) | collective-permute-done | bytes 655392 | tf_op jit(solution)/shard_map/ppermute | solution.py:372
  96.0 19.0 %collective-permute-done.13.refs_0_ = bf16[160,1792]{1,0:T(8,128)(2,1)S(1)} collective-permute-done((bf16[160,1792]{1,0:T(8,128)(2,1)S(1)}, bf16[160,1792]{1,0:T(8,128)(2,1)S(1)}, u32[]{:S(2)}, u32[]{:S(2)}) %collective-permute-start.13) | collective-permute-done | bytes 573472 | tf_op jit(solution)/shard_map/ppermute | solution.py:372
  125.1 17.9 %collective-permute-done.16.refs_0_ = bf16[160,1792]{1,0:T(8,128)(2,1)} collective-permute-done((bf16[160,1792]{1,0:T(8,128)(2,1)}, bf16[160,1792]{1,0:T(8,128)(2,1)}, u32[]{:S(2)}, u32[]{:S(2)}) %collective-permute-start.16) | collective-permute-done | bytes 573472 | tf_op jit(solution)/shard_map/ppermute | solution.py:372
  173.2 24.8 %collective-permute-done.20.two_far = bf16[256,1280]{1,0:T(8,128)(2,1)S(1)} collective-permute-done((bf16[256,1280]{1,0:T(8,128)(2,1)S(1)}, bf16[256,1280]{1,0:T(8,128)(2,1)S(1)}, u32[]{:S(2)}, u32[]{:S(2)}) %collective-permute-start.20) | collective-permute-done | bytes 655392 | tf_op jit(solution)/shard_map/ppermute | solution.py:372
  200.7 6.5 collective-permute-done.18.refs_2_
  217.9 11.5 %collective-permute-done.21.early = bf16[512,320]{1,0:T(8,128)(2,1)S(1)} collective-permute-done((bf16[512,320]{1,0:T(8,128)(2,1)S(1)}, bf16[512,320]{1,0:T(8,128)(2,1)S(1)}, u32[]{:S(2)}, u32[]{:S(2)}) %collective-permute-start.21) | collective-permute-done | bytes 327712 | tf_op jit(solution)/shard_map/ppermute | solution.py:1249
  230.6 13.7 %attend.1 = (bf16[512,640]{1,0:T(8,128)(2,1)S(1)}, f32[8,512]{1,0:T(8,128)S(1)}) custom-call(bf16[512,640]{1,0:T(8,128)(2,1)S(1)} %copy-done.33, bf16[512,320]{1,0:T(8,128)(2,1)S(1)} %collective-permute-done.21.early, bf16[512,320]{1,0:T(8,128)(2,1)S(1)} %copy-done.36, s32[2,512]{1,0:T(2,128)S(1)} %pad_add_fusion.1.query_ids, s32[1024,2]{1,0:T(8,128)S(1)} %copy.62.key_ids), custom_call_target="tpu_custom_call" | custom-call | flops 1024 | bytes 4096 | tf_op jit(solution)/shard_map/attend/pallas_call | solution.py:523
  252.2 9.8 %collective-permute-start.23 = (bf16[256,1280]{1,0:T(8,128)(2,1)S(1)}, bf16[256,1280]{1,0:T(8,128)(2,1)S(1)}, u32[]{:S(2)}, u32[]{:S(2)}) collective-permute-start(bf16[256,1280]{1,0:T(8,128)(2,1)S(1)} %get-tuple-element.353), channel_id=1, source_target_pairs={{0,2},{2,0},{4,6},{6,4},{1,3},{3,1},{5,7},{7,5},{8,10},{10,8},{12,... | collective-permute-start | bytes 1966088 | tf_op jit(solution)/shard_map/ppermute | solution.py:372
  266.1 34.3 %collective-permute-done.23.got_two = bf16[256,1280]{1,0:T(8,128)(2,1)S(1)} collective-permute-done((bf16[256,1280]{1,0:T(8,128)(2,1)S(1)}, bf16[256,1280]{1,0:T(8,128)(2,1)S(1)}, u32[]{:S(2)}, u32[]{:S(2)}) %collective-permute-start.23) | collective-permute-done | bytes 655392 | tf_op jit(solution)/shard_map/ppermute | solution.py:372
  314.7 7.3 collective-permute-done.24.last_one
  326.1 7.8 collective-permute-done.31.second.two_tp
  335.8 13.2 %collective-permute-done.32.two_far = bf16[256,1280]{1,0:T(8,128)(2,1)S(1)} collective-permute-done((bf16[256,1280]{1,0:T(8,128)(2,1)S(1)}, bf16[256,1280]{1,0:T(8,128)(2,1)S(1)}, u32[]{:S(2)}, u32[]{:S(2)}) %collective-permute-start.32) | collective-permute-done | bytes 655392 | tf_op jit(solution)/shard_map/ppermute | solution.py:372
  352.2 15.9 %hidden_units.1 = (bf16[512,1792]{1,0:T(8,128)(2,1)S(1)}, f32[512,1792]{1,0:T(8,128)}, f32[512,1792]{1,0:T(8,128)}) custom-call(bf16[512,2560]{1,0:T(8,128)(2,1)S(1)} %take_rows.6.normed.left, bf16[1280,1792]{1,0:T(8,128)(2,1)} %fill_rows.13.gate_m.refs_2_, bf16[1280,1792]{1,0:T(8,128)(2,1)} %collective-permute-done.33.gate_o.refs_3_, ...), custom_call_target="tpu_custom_call" | custom-call | flops 1024 | bytes 4096 | tf_op jit(solution)/shard_map/hidden_units/pallas_call | solution.py:668
  373.9 9.8 %collective-permute-done.35.left_other = bf16[512,1280]{1,0:T(8,128)(2,1)S(1)} collective-permute-done((bf16[512,1280]{1,0:T(8,128)(2,1)S(1)}, bf16[512,1280]{1,0:T(8,128)(2,1)S(1)}, u32[]{:S(2)}, u32[]{:S(2)}) %collective-permute-start.35) | collective-permute-done | bytes 1310752 | tf_op jit(solution)/shard_map/ppermute | solution.py:364
  383.7 7.0 outer.10
  391.5 7.9 project_back.5
  401.1 11.5 %hidden_grads.1 = (bf16[512,1792]{1,0:T(8,128)(2,1)S(1)}, bf16[512,1792]{1,0:T(8,128)(2,1)S(1)}) custom-call(bf16[512,2560]{1,0:T(8,128)(2,1)} %copy-done.3, bf16[1280,1792]{1,0:T(8,128)(2,1)} %fill_rows.15.refs_1_.down_m, bf16[1280,1792]{1,0:T(8,128)(2,1)} %collective-permute-done.38.refs_2_.down_o, f32[512,1792]{1,0:T(8,128)} %get-tuple-element.393.gate_slope, ...), custom_call_target="tpu_custom_call" | custom-call | flops 1024 | bytes 4096 | tf_op jit(solution)/shard_map/hidden_grads/pallas_call | solution.py:668
  416.0 14.3 %project_back.6 = (bf16[256,1280]{1,0:T(8,128)(2,1)S(1)}, bf16[256,1280]{1,0:T(8,128)(2,1)S(1)}, bf16[256,1280]{1,0:T(8,128)(2,1)S(1)}, bf16[256,1280]{1,0:T(8,128)(2,1)S(1)}) custom-call(bf16[512,1792]{1,0:T(8,128)(2,1)S(1)} %get-tuple-element.434.refs_0_.right, bf16[512,1792]{1,0:T(8,128)(2,1)} %copy-done.7, bf16[1280,1792]{1,0:T(8,128)(2,1)} %fill_rows.13.gate_m.refs_2_, ...), custom_call_target="tpu_custom_call" | custom-call | flops 1024 | bytes 4096 | tf_op jit(solution)/shard_map/project_back/pallas_call | solution.py:668
  447.1 6.7 outer.12
  461.1 14.8 %collective-permute-done.42.got_one = bf16[256,1280]{1,0:T(8,128)(2,1)S(1)} collective-permute-done((bf16[256,1280]{1,0:T(8,128)(2,1)S(1)}, bf16[256,1280]{1,0:T(8,128)(2,1)S(1)}, u32[]{:S(2)}, u32[]{:S(2)}) %collective-permute-start.42) | collective-permute-done | bytes 655392 | tf_op jit(solution)/shard_map/ppermute | solution.py:376
  475.8 24.1 %collective-permute-done.43.got_two = bf16[256,1280]{1,0:T(8,128)(2,1)S(1)} collective-permute-done((bf16[256,1280]{1,0:T(8,128)(2,1)S(1)}, bf16[256,1280]{1,0:T(8,128)(2,1)S(1)}, u32[]{:S(2)}, u32[]{:S(2)}) %collective-permute-start.43) | collective-permute-done | bytes 655392 | tf_op jit(solution)/shard_map/ppermute | solution.py:372
  516.7 6.5 outer.15.refs_0_.refs_2_
  535.7 30.9 %collective-permute-done.50.second.one_near = bf16[128,1280]{1,0:T(8,128)(2,1)S(1)} collective-permute-done((bf16[128,1280]{1,0:T(8,128)(2,1)S(1)}, bf16[128,1280]{1,0:T(8,128)(2,1)S(1)}, u32[]{:S(2)}, u32[]{:S(2)}) %collective-permute-start.50) | collective-permute-done | bytes 327712 | tf_op jit(solution)/shard_map/ppermute | solution.py:372
  567.3 15.8 %collective-permute-done.57.refs_1_.refs_3_ = bf16[320,1792]{1,0:T(8,128)(2,1)S(1)} collective-permute-done((bf16[320,1792]{1,0:T(8,128)(2,1)S(1)}, bf16[320,1792]{1,0:T(8,128)(2,1)S(1)}, u32[]{:S(2)}, u32[]{:S(2)}) %collective-permute-start.57) | collective-permute-done | bytes 1146912 | tf_op jit(solution)/shard_map/ppermute | solution.py:372
  607.7 16.2 %attend_back.1 = (bf16[512,640]{1,0:T(8,128)(2,1)S(1)}, bf16[512,320]{1,0:T(8,128)(2,1)}, f32[512,320]{1,0:T(8,128)S(1)}) custom-call(bf16[512,640]{1,0:T(8,128)(2,1)S(1)} %copy-done.34, bf16[512,320]{1,0:T(8,128)(2,1)S(1)} %copy-done.39, bf16[512,320]{1,0:T(8,128)(2,1)S(1)} %copy-done.37, s32[2,512]{1,0:T(2,128)S(1)} %copy-done.79, ...), custom_call_target="tpu_custom_call" | custom-call | flops 1024 | bytes 4096 | tf_op jit(solution)/shard_map/attend_back/pallas_call | solution.py:523
  623.8 16.1 %collective-permute-done.58.refs_1_.refs_3_ = bf16[320,1792]{1,0:T(8,128)(2,1)S(1)} collective-permute-done((bf16[320,1792]{1,0:T(8,128)(2,1)}, bf16[320,1792]{1,0:T(8,128)(2,1)S(1)}, u32[]{:S(2)}, u32[]{:S(2)}) %collective-permute-start.58) | collective-permute-done | bytes 1146912 | tf_op jit(solution)/shard_map/ppermute | solution.py:372
  651.2 11.1 %collective-permute-done.59.late = bf16[512,320]{1,0:T(8,128)(2,1)S(1)} collective-permute-done((bf16[512,320]{1,0:T(8,128)(2,1)}, bf16[512,320]{1,0:T(8,128)(2,1)S(1)}, u32[]{:S(2)}, u32[]{:S(2)}) %collective-permute-start.59) | collective-permute-done | bytes 327712 | tf_op jit(solution)/shard_map/ppermute | solution.py:1363
  663.1 6.8 project_back.7
  669.9 8.5 %collective-permute-done.65.received = bf16[160,1792]{1,0:T(8,128)(2,1)S(1)} collective-permute-done((bf16[160,1792]{1,0:T(8,128)(2,1)S(1)}, bf16[160,1792]{1,0:T(8,128)(2,1)S(1)}, u32[]{:S(2)}, u32[]{:S(2)}) %collective-permute-start.65) | collective-permute-done | bytes 573472 | tf_op jit(solution)/shard_map/ppermute | solution.py:372
  686.3 44.5 %collective-permute-done.66.refs_1_.refs_3_ = bf16[640,640]{1,0:T(8,128)(2,1)S(1)} collective-permute-done((bf16[640,640]{1,0:T(8,128)(2,1)S(1)}, bf16[640,640]{1,0:T(8,128)(2,1)S(1)}, u32[]{:S(2)}, u32[]{:S(2)}) %collective-permute-start.66) | collective-permute-done | bytes 819232 | tf_op jit(solution)/shard_map/ppermute | solution.py:368
  741.6 24.2 %collective-permute-done.73.refs_1_.refs_3_ = bf16[320,640]{1,0:T(8,128)(2,1)S(1)} collective-permute-done((bf16[320,640]{1,0:T(8,128)(2,1)S(1)}, bf16[320,640]{1,0:T(8,128)(2,1)S(1)}, u32[]{:S(2)}, u32[]{:S(2)}) %collective-permute-start.73) | collective-permute-done | bytes 409632 | tf_op jit(solution)/shard_map/ppermute | solution.py:372
  (513 shorter events, 313.2 us)
Async XLA Ops:
  36.1 51.5 %collective-permute-start.9 = (bf16[320,1664]{1,0:T(8,128)(2,1)}, bf16[320,1664]{1,0:T(8,128)(2,1)}, u32[]{:S(2)}, u32[]{:S(2)}) collective-permute-start(bf16[320,1664]{1,0:T(8,128)(2,1)} %fill_rows.8.refs_1_), channel_id=1, source_target_pairs={{0,4},{2,6},{4,0},{6,2},{1,5},{3,7},{5,1},{7,3},{8,12},{10,14},{12... | collective-permute-start | bytes 3194888 | tf_op jit(solution)/shard_map/ppermute | solution.py:372
  37.4 39.5 %collective-permute-start.6 = (bf16[256,1280]{1,0:T(8,128)(2,1)}, bf16[256,1280]{1,0:T(8,128)(2,1)}, u32[]{:S(2)}, u32[]{:S(2)}) collective-permute-start(bf16[256,1280]{1,0:T(8,128)(2,1)} %pair_rows.9), channel_id=1, source_target_pairs={{0,2},{2,0},{4,6},{6,4},{1,3},{3,1},{5,7},{7,5},{8,10},{10,8},{12,... | collective-permute-start | bytes 1966088 | tf_op jit(solution)/shard_map/ppermute | solution.py:372
  42.4 43.3 %collective-permute-start.10 = (bf16[160,1792]{1,0:T(8,128)(2,1)}, bf16[160,1792]{1,0:T(8,128)(2,1)}, u32[]{:S(2)}, u32[]{:S(2)}) collective-permute-start(bf16[160,1792]{1,0:T(8,128)(2,1)} %get-tuple-element.312), channel_id=1, source_target_pairs={{0,2},{2,0},{4,6},{6,4},{1,3},{3,1},{5,7},{7,5},{8,10},{10,8},{12,... | collective-permute-start | bytes 1720328 | tf_op jit(solution)/shard_map/ppermute | solution.py:372
  90.8 59.1 %collective-permute-start.11 = (bf16[640,1664]{1,0:T(8,128)(2,1)}, bf16[640,1664]{1,0:T(8,128)(2,1)}, u32[]{:S(2)}, u32[]{:S(2)}) collective-permute-start(bf16[640,1664]{1,0:T(8,128)(2,1)} %get-tuple-element.317), channel_id=1, source_target_pairs={{0,16},{8,24},{16,0},{24,8},{1,17},{9,25},{17,1},{25,9},{2,18},{10... | collective-permute-start | bytes 6389768 | tf_op jit(solution)/shard_map/ppermute | solution.py:368
  93.9 52.6 %collective-permute-start.12 = (bf16[320,1792]{1,0:T(8,128)(2,1)}, bf16[320,1792]{1,0:T(8,128)(2,1)}, u32[]{:S(2)}, u32[]{:S(2)}) collective-permute-start(bf16[320,1792]{1,0:T(8,128)(2,1)} %fill_rows.9.refs_1_), channel_id=1, source_target_pairs={{0,4},{2,6},{4,0},{6,2},{1,5},{3,7},{5,1},{7,3},{8,12},{10,14},{12... | collective-permute-start | bytes 3440648 | tf_op jit(solution)/shard_map/ppermute | solution.py:372
  94.5 48.6 %collective-permute-start.16 = (bf16[160,1792]{1,0:T(8,128)(2,1)}, bf16[160,1792]{1,0:T(8,128)(2,1)}, u32[]{:S(2)}, u32[]{:S(2)}) collective-permute-start(bf16[160,1792]{1,0:T(8,128)(2,1)} %get-tuple-element.325), channel_id=1, source_target_pairs={{0,2},{2,0},{4,6},{6,4},{1,3},{3,1},{5,7},{7,5},{8,10},{10,8},{12,... | collective-permute-start | bytes 1720328 | tf_op jit(solution)/shard_map/ppermute | solution.py:372
  152.5 58.2 %collective-permute-start.26 = (bf16[640,1792]{1,0:T(8,128)(2,1)}, bf16[640,1792]{1,0:T(8,128)(2,1)}, u32[]{:S(2)}, u32[]{:S(2)}) collective-permute-start(bf16[640,1792]{1,0:T(8,128)(2,1)} %get-tuple-element.360), channel_id=1, source_target_pairs={{0,16},{8,24},{16,0},{24,8},{1,17},{9,25},{17,1},{25,9},{2,18},{10... | collective-permute-start | bytes 6881288 | tf_op jit(solution)/shard_map/ppermute | solution.py:368
  155.4 51.9 %collective-permute-start.18 = (bf16[320,1792]{1,0:T(8,128)(2,1)}, bf16[320,1792]{1,0:T(8,128)(2,1)}, u32[]{:S(2)}, u32[]{:S(2)}) collective-permute-start(bf16[320,1792]{1,0:T(8,128)(2,1)} %fill_rows.10.refs_1_), channel_id=1, source_target_pairs={{0,4},{2,6},{4,0},{6,2},{1,5},{3,7},{5,1},{7,3},{8,12},{10,14},{12... | collective-permute-start | bytes 3440648 | tf_op jit(solution)/shard_map/ppermute | solution.py:372
  160.1 37.9 %collective-permute-start.20 = (bf16[256,1280]{1,0:T(8,128)(2,1)S(1)}, bf16[256,1280]{1,0:T(8,128)(2,1)S(1)}, u32[]{:S(2)}, u32[]{:S(2)}) collective-permute-start(bf16[256,1280]{1,0:T(8,128)(2,1)S(1)} %pair_rows.11), channel_id=1, source_target_pairs={{0,2},{2,0},{4,6},{6,4},{1,3},{3,1},{5,7},{7,5},{8,10},{10,8},{12,... | collective-permute-start | bytes 1966088 | tf_op jit(solution)/shard_map/ppermute | solution.py:372
  213.3 94.0 %collective-permute-start.27 = (bf16[640,1792]{1,0:T(8,128)(2,1)}, bf16[640,1792]{1,0:T(8,128)(2,1)}, u32[]{:S(2)}, u32[]{:S(2)}) collective-permute-start(bf16[640,1792]{1,0:T(8,128)(2,1)} %get-tuple-element.363), channel_id=1, source_target_pairs={{0,16},{8,24},{16,0},{24,8},{1,17},{9,25},{17,1},{25,9},{2,18},{10... | collective-permute-start | bytes 6881288 | tf_op jit(solution)/shard_map/ppermute | solution.py:368
  244.3 58.7 %collective-permute-start.28 = (bf16[320,1792]{1,0:T(8,128)(2,1)S(1)}, bf16[320,1792]{1,0:T(8,128)(2,1)S(1)}, u32[]{:S(2)}, u32[]{:S(2)}) collective-permute-start(bf16[320,1792]{1,0:T(8,128)(2,1)S(1)} %copy-done.25), channel_id=1, source_target_pairs={{0,4},{2,6},{4,0},{6,2},{1,5},{3,7},{5,1},{7,3},{8,12},{10,14},{12... | collective-permute-start | bytes 3440648 | tf_op jit(solution)/shard_map/ppermute | solution.py:372
  252.2 48.2 %collective-permute-start.23 = (bf16[256,1280]{1,0:T(8,128)(2,1)S(1)}, bf16[256,1280]{1,0:T(8,128)(2,1)S(1)}, u32[]{:S(2)}, u32[]{:S(2)}) collective-permute-start(bf16[256,1280]{1,0:T(8,128)(2,1)S(1)} %get-tuple-element.353), channel_id=1, source_target_pairs={{0,2},{2,0},{4,6},{6,4},{1,3},{3,1},{5,7},{7,5},{8,10},{10,8},{12,... | collective-permute-start | bytes 1966088 | tf_op jit(solution)/shard_map/ppermute | solution.py:372
  262.0 88.0 %collective-permute-start.33 = (bf16[1280,1792]{1,0:T(8,128)(2,1)}, bf16[1280,1792]{1,0:T(8,128)(2,1)}, u32[]{:S(2)}, u32[]{:S(2)}) collective-permute-start(bf16[1280,1792]{1,0:T(8,128)(2,1)} %fill_rows.13.gate_m.refs_2_), channel_id=1, source_target_pairs={{0,8},{8,0},{16,24},{24,16},{1,9},{9,1},{17,25},{25,17},{2,10},{10... | collective-permute-start | bytes 13762568 | tf_op jit(solution)/shard_map/ppermute | solution.py:364
  310.1 40.0 %collective-permute-start.34 = (bf16[1280,1792]{1,0:T(8,128)(2,1)}, bf16[1280,1792]{1,0:T(8,128)(2,1)S(1)}, u32[]{:S(2)}, u32[]{:S(2)}) collective-permute-start(bf16[1280,1792]{1,0:T(8,128)(2,1)} %fill_rows.14.up_m.refs_4_), channel_id=1, source_target_pairs={{0,8},{8,0},{16,24},{24,16},{1,9},{9,1},{17,25},{25,17},{2,10},{10... | collective-permute-start | bytes 13762568 | tf_op jit(solution)/shard_map/ppermute | solution.py:364
  310.1 59.2 %collective-permute-start.37 = (bf16[640,1792]{1,0:T(8,128)(2,1)}, bf16[640,1792]{1,0:T(8,128)(2,1)}, u32[]{:S(2)}, u32[]{:S(2)}) collective-permute-start(bf16[640,1792]{1,0:T(8,128)(2,1)} %get-tuple-element.380), channel_id=1, source_target_pairs={{0,16},{8,24},{16,0},{24,8},{1,17},{9,25},{17,1},{25,9},{2,18},{10... | collective-permute-start | bytes 6881288 | tf_op jit(solution)/shard_map/ppermute | solution.py:368
  390.7 63.1 %collective-permute-start.44 = (bf16[640,1792]{1,0:T(8,128)(2,1)}, bf16[640,1792]{1,0:T(8,128)(2,1)}, u32[]{:S(2)}, u32[]{:S(2)}) collective-permute-start(bf16[640,1792]{1,0:T(8,128)(2,1)} %outer.10), channel_id=1, source_target_pairs={{0,16},{8,24},{16,0},{24,8},{1,17},{9,25},{17,1},{25,9},{2,18},{10... | collective-permute-start | bytes 6881288 | tf_op jit(solution)/shard_map/ppermute | solution.py:368
  457.3 71.0 %collective-permute-start.52 = (bf16[640,1792]{1,0:T(8,128)(2,1)}, bf16[640,1792]{1,0:T(8,128)(2,1)}, u32[]{:S(2)}, u32[]{:S(2)}) collective-permute-start(bf16[640,1792]{1,0:T(8,128)(2,1)} %outer.12), channel_id=1, source_target_pairs={{0,16},{8,24},{16,0},{24,8},{1,17},{9,25},{17,1},{25,9},{2,18},{10... | collective-permute-start | bytes 6881288 | tf_op jit(solution)/shard_map/ppermute | solution.py:368
  458.6 51.6 %collective-permute-start.49 = (bf16[512,1792]{1,0:T(8,128)(2,1)S(1)}, bf16[512,1792]{1,0:T(8,128)(2,1)S(1)}, u32[]{:S(2)}, u32[]{:S(2)}) collective-permute-start(bf16[512,1792]{1,0:T(8,128)(2,1)S(1)} %copy-done.8), channel_id=1, source_target_pairs={{0,8},{8,0},{16,24},{24,16},{1,9},{9,1},{17,25},{25,17},{2,10},{10... | collective-permute-start | bytes 5505032 | tf_op jit(solution)/shard_map/ppermute | solution.py:364
  458.7 65.8 %collective-permute-start.53 = (bf16[320,1792]{1,0:T(8,128)(2,1)}, bf16[320,1792]{1,0:T(8,128)(2,1)}, u32[]{:S(2)}, u32[]{:S(2)}) collective-permute-start(bf16[320,1792]{1,0:T(8,128)(2,1)} %get-tuple-element.423), channel_id=1, source_target_pairs={{0,4},{2,6},{4,0},{6,2},{1,5},{3,7},{5,1},{7,3},{8,12},{10,14},{12... | collective-permute-start | bytes 3440648 | tf_op jit(solution)/shard_map/ppermute | solution.py:372
  460.1 39.8 %collective-permute-start.43 = (bf16[256,1280]{1,0:T(8,128)(2,1)S(1)}, bf16[256,1280]{1,0:T(8,128)(2,1)S(1)}, u32[]{:S(2)}, u32[]{:S(2)}) collective-permute-start(bf16[256,1280]{1,0:T(8,128)(2,1)S(1)} %copy-done.85), channel_id=1, source_target_pairs={{0,2},{2,0},{4,6},{6,4},{1,3},{3,1},{5,7},{7,5},{8,10},{10,8},{12,... | collective-permute-start | bytes 1966088 | tf_op jit(solution)/shard_map/ppermute | solution.py:372
  530.6 54.8 %collective-permute-start.56 = (bf16[640,1792]{1,0:T(8,128)(2,1)}, bf16[640,1792]{1,0:T(8,128)(2,1)}, u32[]{:S(2)}, u32[]{:S(2)}) collective-permute-start(bf16[640,1792]{1,0:T(8,128)(2,1)} %outer.14), channel_id=1, source_target_pairs={{0,16},{8,24},{16,0},{24,8},{1,17},{9,25},{17,1},{25,9},{2,18},{10... | collective-permute-start | bytes 6881288 | tf_op jit(solution)/shard_map/ppermute | solution.py:368
  531.4 51.7 %collective-permute-start.57 = (bf16[320,1792]{1,0:T(8,128)(2,1)S(1)}, bf16[320,1792]{1,0:T(8,128)(2,1)S(1)}, u32[]{:S(2)}, u32[]{:S(2)}) collective-permute-start(bf16[320,1792]{1,0:T(8,128)(2,1)S(1)} %get-tuple-element.458), channel_id=1, source_target_pairs={{0,4},{2,6},{4,0},{6,2},{1,5},{3,7},{5,1},{7,3},{8,12},{10,14},{12... | collective-permute-start | bytes 3440648 | tf_op jit(solution)/shard_map/ppermute | solution.py:372
  588.6 51.3 %collective-permute-start.58 = (bf16[320,1792]{1,0:T(8,128)(2,1)}, bf16[320,1792]{1,0:T(8,128)(2,1)S(1)}, u32[]{:S(2)}, u32[]{:S(2)}) collective-permute-start(bf16[320,1792]{1,0:T(8,128)(2,1)} %get-tuple-element.470), channel_id=1, source_target_pairs={{0,4},{2,6},{4,0},{6,2},{1,5},{3,7},{5,1},{7,3},{8,12},{10,14},{12... | collective-permute-start | bytes 3440648 | tf_op jit(solution)/shard_map/ppermute | solution.py:372
  598.8 48.4 %collective-permute-start.60 = (bf16[512,1280]{1,0:T(8,128)(2,1)}, bf16[512,1280]{1,0:T(8,128)(2,1)S(1)}, u32[]{:S(2)}, u32[]{:S(2)}) collective-permute-start(bf16[512,1280]{1,0:T(8,128)(2,1)} %slice.66), channel_id=1, source_target_pairs={{0,8},{8,0},{16,24},{24,16},{1,9},{9,1},{17,25},{25,17},{2,10},{10... | collective-permute-start | bytes 3932168 | tf_op jit(solution)/shard_map/ppermute | solution.py:364
  598.9 48.3 %collective-permute-start.61 = (bf16[512,640]{1,0:T(8,128)(2,1)S(1)}, bf16[512,640]{1,0:T(8,128)(2,1)S(1)}, u32[]{:S(2)}, u32[]{:S(2)}) collective-permute-start(bf16[512,640]{1,0:T(8,128)(2,1)S(1)} %get-tuple-element.487.refs_0_.right), channel_id=1, source_target_pairs={{0,8},{8,0},{16,24},{24,16},{1,9},{9,1},{17,25},{25,17},{2,10},{10... | collective-permute-start | bytes 1966088 | tf_op jit(solution)/shard_map/ppermute | solution.py:364
  599.4 50.3 %collective-permute-start.63 = (bf16[160,1792]{1,0:T(8,128)(2,1)}, bf16[160,1792]{1,0:T(8,128)(2,1)}, u32[]{:S(2)}, u32[]{:S(2)}) collective-permute-start(bf16[160,1792]{1,0:T(8,128)(2,1)} %get-tuple-element.490), channel_id=1, source_target_pairs={{0,2},{2,0},{4,6},{6,4},{1,3},{3,1},{5,7},{7,5},{8,10},{10,8},{12,... | collective-permute-start | bytes 1720328 | tf_op jit(solution)/shard_map/ppermute | solution.py:372
  601.9 49.3 %collective-permute-start.62 = (bf16[160,1792]{1,0:T(8,128)(2,1)}, bf16[160,1792]{1,0:T(8,128)(2,1)}, u32[]{:S(2)}, u32[]{:S(2)}) collective-permute-start(bf16[160,1792]{1,0:T(8,128)(2,1)} %get-tuple-element.489), channel_id=1, source_target_pairs={{0,2},{2,0},{4,6},{6,4},{1,3},{3,1},{5,7},{7,5},{8,10},{10,8},{12,... | collective-permute-start | bytes 1720328 | tf_op jit(solution)/shard_map/ppermute | solution.py:372
  682.9 56.1 %collective-permute-start.67 = (bf16[640,1024]{1,0:T(8,128)(2,1)S(1)}, bf16[640,1024]{1,0:T(8,128)(2,1)S(1)}, u32[]{:S(2)}, u32[]{:S(2)}) collective-permute-start(bf16[640,1024]{1,0:T(8,128)(2,1)S(1)} %outer.18), channel_id=1, source_target_pairs={{0,16},{8,24},{16,0},{24,8},{1,17},{9,25},{17,1},{25,9},{2,18},{10... | collective-permute-start | bytes 3932168 | tf_op jit(solution)/shard_map/ppermute | solution.py:368
  684.3 46.5 %collective-permute-start.66 = (bf16[640,640]{1,0:T(8,128)(2,1)S(1)}, bf16[640,640]{1,0:T(8,128)(2,1)S(1)}, u32[]{:S(2)}, u32[]{:S(2)}) collective-permute-start(bf16[640,640]{1,0:T(8,128)(2,1)S(1)} %outer.16), channel_id=1, source_target_pairs={{0,16},{8,24},{16,0},{24,8},{1,17},{9,25},{17,1},{25,9},{2,18},{10... | collective-permute-start | bytes 2457608 | tf_op jit(solution)/shard_map/ppermute | solution.py:368
  685.0 53.7 %collective-permute-start.68 = (bf16[256,1280]{1,0:T(8,128)(2,1)S(1)}, bf16[256,1280]{1,0:T(8,128)(2,1)S(1)}, u32[]{:S(2)}, u32[]{:S(2)}) collective-permute-start(bf16[256,1280]{1,0:T(8,128)(2,1)S(1)} %get-tuple-element.493), channel_id=1, source_target_pairs={{0,1},{1,0},{2,3},{3,2},{4,5},{5,4},{6,7},{7,6},{8,9},{9,8},{10,11... | collective-permute-start | bytes 1966088 | tf_op jit(solution)/shard_map/ppermute | solution.py:376
  686.1 52.6 %collective-permute-start.69 = (bf16[256,1280]{1,0:T(8,128)(2,1)S(1)}, bf16[256,1280]{1,0:T(8,128)(2,1)S(1)}, u32[]{:S(2)}, u32[]{:S(2)}) collective-permute-start(bf16[256,1280]{1,0:T(8,128)(2,1)S(1)} %get-tuple-element.495), channel_id=1, source_target_pairs={{0,2},{2,0},{4,6},{6,4},{1,3},{3,1},{5,7},{7,5},{8,10},{10,8},{12,... | collective-permute-start | bytes 1966088 | tf_op jit(solution)/shard_map/ppermute | solution.py:372
  741.6 38.0 %collective-permute-start.70 = (bf16[320,1024]{1,0:T(8,128)(2,1)S(1)}, bf16[320,1024]{1,0:T(8,128)(2,1)S(1)}, u32[]{:S(2)}, u32[]{:S(2)}) collective-permute-start(bf16[320,1024]{1,0:T(8,128)(2,1)S(1)} %get-tuple-element.519), channel_id=1, source_target_pairs={{0,4},{2,6},{4,0},{6,2},{1,5},{3,7},{5,1},{7,3},{8,12},{10,14},{12... | collective-permute-start | bytes 1966088 | tf_op jit(solution)/shard_map/ppermute | solution.py:372
  (167 other events, 2025.6 us)

commit v4 on v3

--- a/solution.py
+++ b/solution.py
@@ -803,22 +803,29 @@
     )
 
 
-def outer_kernel(left, left_other, right, right_other, out):
-    first = rows_dot(left[...], right[...])
-    out[...] = (first + rows_dot(left_other[...], right_other[...])).astype(jnp.bfloat16)
-
-
-def outer(left, left_other, right, right_other, index):
+def outer_kernel(left, left_other, right, *refs):
+    others, out = refs[:-1], refs[-1]
+    total = rows_dot(left[...], right[...])
+    rows = left.shape[0] // len(others)
+    for i, other in enumerate(others):
+        total = total + rows_dot(left_other[i * rows : (i + 1) * rows, :], other[...])
+    out[...] = total.astype(jnp.bfloat16)
+
+
+def outer(left, left_others, right, right_others, index):
     rows, width = left.shape[0], right.shape[1]
-    depth = left_other.shape[1] // 2
+    left_other = left_others[index]
+    depth = left_other.shape[1]
     tile = 256 if width % 256 == 0 else width
     (out,) = tiled_call(
         outer_kernel,
         "outer",
         width // tile,
-        [((rows, depth), lambda step: (0, index))] * 2 + [((rows, tile), by_column)] * 2,
+        [((rows, depth), lambda step: (0, index)), ((rows, depth), fixed)]
+        + [((rows, tile), by_column)]
+        + [((other.shape[0], tile), by_column) for other in right_others],
         [((depth, width), jnp.bfloat16, (depth, tile), by_column)],
-        (left, left_other, right, right_other),
+        (left, left_other, right, *right_others),
     )
     return out
 
@@ -898,16 +905,25 @@
     )(where, *[array for array, _, _ in ins])
 
 
-def far_halves(where, own, from_x):
-    rows, columns = own.shape[0] // 4, own.shape[1]
+def far_halves(where, *terms):
+    rows = terms[0][0].shape[0] // 4
+    columns = sum(own.shape[1] for own, _ in terms)
     keep, give = (lambda step, ref: 2 * ref[0] + step), (lambda step, ref: 2 - 2 * ref[0] + step)
     out = ((2 * rows, columns), jnp.bfloat16, rows, lambda step, ref: step)
+    count = len(terms)
+
+    def sums(*values):
+        pairs = [values[2 * i] + values[2 * i + 1] for i in range(2 * count)]
+        if count == 1:
+            return pairs
+        return jnp.concatenate(pairs[:count], axis=1), jnp.concatenate(pairs[count:], axis=1)
+
     return rows_call(
-        lambda a, b, c, d: (a + b, c + d),
+        sums,
         "far_halves",
         where,
         2,
-        [(array, rows, place) for place in (keep, give) for array in (own, from_x)],
+        [(array, rows, place) for place in (keep, give) for pair in terms for array in pair],
         [out, out],
     )
 
@@ -1082,12 +1098,29 @@
 
 
 def token_grad_kernel(
-    sum_one, sum_two, last_one, last_two, rows, gain, grad_residual, grad, gain_term
+    sum_one, sum_two, last_one, last_two, rows, gain, grad_residual, grad
 ):
     value = rows[...].astype(jnp.float32)
-    back, term = norm_grad(summed(sum_one, sum_two, last_one, last_two), value, gain[...])
+    back, _ = norm_grad(summed(sum_one, sum_two, last_one, last_two), value, gain[...])
     grad[...] = grad_residual[...] + back
-    gain_term[...] = term
+
+
+def gain_kernel(one_keep, one_send, two_keep, two_send, rows, out):
+    n, half = one_keep.shape[0] // 2, one_keep.shape[1]
+    low_half, high_half = slice(0, n), slice(n, 2 * n)
+    ones = (one_keep, low_half), (one_send, low_half), (one_keep, high_half), (one_send, high_half)
+    twos = (two_keep, low_half), (two_keep, high_half), (two_send, low_half), (two_send, high_half)
+    left = right = 0.0
+    for k in range(4):
+        value = rows[k * n : (k + 1) * n, :].astype(jnp.float32)
+        scale = lax.rsqrt(jnp.mean(value * value, axis=1, keepdims=True) + norm_eps)
+        value = value * scale
+        one = ones[k][0][ones[k][1], :].astype(jnp.float32)
+        two = twos[k][0][twos[k][1], :].astype(jnp.float32)
+        left = left + jnp.sum(one * value[:, :half], axis=0, keepdims=True)
+        right = right + jnp.sum(two * value[:, half:], axis=0, keepdims=True)
+    out[:, :half] = left
+    out[:, half:] = right
 
 
 def mixed_kernel(sum_one, sum_two, last_one, last_two, residual, mixed):
@@ -1150,6 +1183,14 @@
     row_shape = (local_rows, D)
     half_shape = (local_rows, middle)
 
+    def cross_left(value, *events):
+        first, second = value[:, middle : middle + quarter], value[:, middle + quarter :]
+        return to_core(hold(first, events)), to_core(hold(second, events))
+
+    def cross_right(value, count):
+        rows = value.shape[0] // count
+        return tuple(to_core(value[i * rows : (i + 1) * rows]) for i in range(count))
+
     tokens_in = columns_in(tokens)
     cot_in = columns_in(cotangent)
     first_width = heads_width + query_width
@@ -1221,7 +1262,7 @@
     first_x = to_x(first_plane)
     gate_far = to_z(hold(gate_pair, first_plane), 2)
     normed_one = norm_rows(hold(token_span, first_plane), gain_one)
-    normed_other = to_core(normed_one[:, middle:])
+    normed_other = cross_left(normed_one)
     up_pair = fill_rows(up_pair, to_z(hold(up_other, first_plane), 1))
     down_pair = fill_rows(down_pair, to_z(hold(down_other, first_plane), 1))
     cot_first = gather_first(*hold((cot_in[:, :middle], cot_in[:, middle:]), up_pair))
@@ -1260,7 +1301,7 @@
         [pltpu.VMEM((2 * group_rows, group_rows // 2), jnp.float32)],
         (query_rot, early_kv, own_kv, query_ids, key_ids),
     )
-    attended_other = to_core(attended_low)
+    attended_other = cross_right(attended_low, 1)
     down_far = to_z(hold(down_pair, log_total), 2)
     branch = scatter_first(
         *project_back([attended_low], [first_weights], heads_width)
@@ -1280,35 +1321,35 @@
     )
     two_wait = gather_second(*gather_first(two_one, two_two))
     span_two = take_rows(*two_wait)
-    span_other = to_core(span_two[:, middle:])
-    cot_other = to_core(hold(cot_span[:, middle:], log_total))
+    span_other = cross_left(span_two)
+    cot_other = cross_left(cot_span, log_total)
     hidden_low, gate_slope, up_slope = hidden_units(span_two, gate_weights, up_weights)
-    hidden_other = to_core(hidden_low)
+    hidden_other = cross_right(hidden_low, 1)
     down_mine = fill_rows(*hold((down_mine, down_x), hidden_low))
     down_weights = down_mine, to_core(down_mine)
 
     down_parts = hold((cot_span, cot_other, hidden_low, hidden_other), down_mine)
     down_give = outer(*down_parts, 1)
     down_back = to_x(down_give)
-    mlp_parts = project_back([hold(hidden_low, down_give)], [down_weights])
+    down_keep = outer(*hold(down_parts, down_give), 0)
+    mlp_parts = project_back([hold(hidden_low, down_keep)], [down_weights])
     grad_gate_pre, grad_up_pre = hidden_grads(
         hold(cot_span, mlp_parts), down_weights, gate_slope, up_slope
     )
-    gate_other = to_core(grad_gate_pre)
-    up_other = to_core(grad_up_pre)
+    gate_other = cross_right(grad_gate_pre, 1)
+    up_other = cross_right(grad_up_pre, 1)
     branch_mlp = scatter_first(*mlp_parts)
     back_parts = project_back(
         [grad_gate_pre, grad_up_pre], [gate_weights, up_weights]
     )
     branch_mlp = scatter_middle(*hold(branch_mlp, back_parts))
     normed_back = scatter_first(*hold(back_parts, branch_mlp))
-    down_keep = outer(*hold(down_parts, branch_mlp), 0)
-    gate_parts = hold((span_two, span_other, grad_gate_pre, gate_other), down_keep)
+    down_keep, down_give = far_halves(where, hold((down_keep, down_back), branch_mlp))
+    down_far = to_z(down_give, 2)
+    gate_parts = hold((span_two, span_other, grad_gate_pre, gate_other), down_give)
     gate_give = outer(*gate_parts, 1)
-    down_keep, down_give = far_halves(where, *hold((down_keep, down_back), gate_give))
-    down_far = to_z(down_give, 2)
-    gate_back = to_x(hold(gate_give, down_give))
-    normed_back = scatter_second(*scatter_middle(*hold(normed_back, down_give)))
+    gate_back = to_x(gate_give)
+    normed_back = scatter_second(*scatter_middle(*hold(normed_back, gate_give)))
     gate_keep = outer(*hold(gate_parts, normed_back[:2]), 0)
     up_parts = hold((span_two, span_other, grad_up_pre, up_other), gate_keep)
     up_give = outer(*up_parts, 1)
@@ -1321,19 +1362,19 @@
         (*hold(normed_back, up_keep), residual, gain_two, cot_in),
     )
     grad_wait = gather_first(grad_one, grad_two)
-    down_own, down_other = near_halves(where, *hold((down_keep, down_far), grad_one))
-    gate_keep, gate_give = far_halves(where, *hold((gate_keep, gate_back), down_other))
+    down_own, down_other = near_halves(where, *hold((down_keep, down_far), grad_wait[2:]))
+    gate_keep, gate_give = far_halves(where, hold((gate_keep, gate_back), down_other))
     gate_far = to_z(gate_give, 2)
     up_back = to_x(hold(up_give, gate_give))
     grad_wait = gather_second(*hold(grad_wait, gate_give))
-    gate_own, gate_other = near_halves(where, *hold((gate_keep, gate_far), grad_wait[2::2]))
-    up_keep, up_give = far_halves(where, *hold((up_keep, up_back), gate_other))
-    up_far = to_z(up_give, 2)
-    grad_span = take_rows(*hold(grad_wait, up_give))
+    grad_span = take_rows(*grad_wait)
     down_near = to_z(hold(down_other, grad_span), 1)
-    gate_near = to_z(hold(gate_other, grad_span), 1)
-    span_grad_other = to_core(grad_span[:, middle:])
-    grad_attended = project(grad_span, first_weights, heads_width, query_width, jnp.bfloat16)
+    gate_own, gate_other = near_halves(where, *hold((gate_keep, gate_far), grad_span))
+    gate_near = to_z(gate_other, 1)
+    span_grad_other = cross_left(grad_span)
+    grad_attended = project(
+        hold(grad_span, gate_other), first_weights, heads_width, query_width, jnp.bfloat16
+    )
     grad_query, grad_early, grad_own = dense_call(
         functools.partial(attend_back_kernel, score_scale),
         "attend_back",
@@ -1359,77 +1400,90 @@
             sin_wide,
         ),
     )
-    up_own, up_other = near_halves(where, *hold((up_keep, up_far), grad_early))
-    late_kv = lax.ppermute(hold(grad_early, up_other), "seq", [(2, 0), (3, 1)])
-    out_parts = hold((grad_span, span_grad_other, attended_low, attended_other), up_other)
-    up_near = to_z(hold(up_other, late_kv), 1)
+    up_terms = hold((up_keep, up_back), grad_early, down_near, gate_near)
+    late_kv = lax.ppermute(hold(grad_early, up_terms[1]), "seq", [(2, 0), (3, 1)])
+    out_parts = hold((grad_span, span_grad_other, attended_low, attended_other), up_terms[1])
+    branch_mlp = scatter_second(*hold(branch_mlp, up_terms[1]))
     out_give = outer(*out_parts, 1)
     out_back = to_x(out_give)
     out_keep = outer(*out_parts, 0)
+    both_keep, both_give = far_halves(where, up_terms, hold((out_keep, out_back), late_kv, branch_mlp[2:]))
+    both_far = to_z(both_give, 2)
     (grad_raw,) = dense_call(
         join_kernel,
         "join",
         [((group_rows, heads_width), jnp.bfloat16)],
         [],
-        (grad_query, grad_own, hold(late_kv, out_give, out_keep, down_near, gate_near), cos_wide, sin_wide),
-    )
-    raw_other = to_core(grad_raw)
+        (grad_query, grad_own, hold(late_kv, both_give), cos_wide, sin_wide),
+    )
+    raw_other = cross_right(grad_raw, 2)
     first_parts = project_back([grad_raw], [first_weights])
     first_back = scatter_first(*first_parts)
-    heads_parts = hold((normed_one, normed_other, grad_raw, raw_other), first_parts, up_near)
+    heads_parts = hold((normed_one, normed_other, grad_raw, raw_other), first_parts)
     heads_give = outer(*heads_parts, 1)
     heads_back = to_x(heads_give)
-    out_keep, out_give = far_halves(where, *hold((out_keep, out_back), heads_give))
-    out_far = to_z(out_give, 2)
-    heads_keep = outer(*hold(heads_parts, out_give), 0)
+    heads_keep = outer(*heads_parts, 0)
     units = w_gate.shape[1]
-    first_back = scatter_middle(*hold(first_back, heads_keep, heads_give))
-    heads_keep, heads_give = far_halves(where, *hold((heads_keep, heads_back), first_back))
+    (gain_one_term,) = dense_call(
+        gain_kernel,
+        "gain",
+        [((1, D), jnp.float32)],
+        [],
+        (*hold(first_parts, heads_keep), token_span),
+    )
+    gain_rows = jnp.concatenate([gain_one_term, gain_two_term], axis=0)
+    gain_rows = gain_rows[:, :middle] + to_core(gain_rows[:, middle:])
+    gain_rows = gain_rows + to_tp(gain_rows)
+    first_back = scatter_middle(*hold(first_back, gain_rows))
+    heads_keep, heads_give = far_halves(where, hold((heads_keep, heads_back), first_back))
     heads_far = to_z(heads_give, 2)
-    first_back = scatter_second(*hold(first_back, heads_give))
-    out_own, out_other = near_halves(where, *hold((out_keep, out_far), first_back[:2]))
-    out_near = to_z(out_other, 1)
-    grad_rows, gain_one_term = dense_call(
+    gain_rows = hold(gain_rows, heads_give)
+    gain_rows = gain_rows[:, :quarter] + to_x(gain_rows[:, quarter:])
+    both_own, both_other = near_halves(where, *hold((both_keep, both_far), heads_give, gain_rows))
+    both_near = to_z(both_other, 1)
+    first_back = scatter_second(*hold(first_back, both_other))
+    (grad_rows,) = dense_call(
         token_grad_kernel,
         "token_grad",
-        [(row_shape, jnp.float32), ((1, D), jnp.float32)],
+        [(row_shape, jnp.float32)],
         [],
-        (*hold(first_back, out_other), tokens_in, gain_one, grad_residual),
-    )
-    gain_rows = jnp.concatenate([gain_one_term, gain_two_term], axis=0)
-    (grad_down,) = join_halves(where, *hold((down_own, down_near), grad_rows), (units,), True)
+        (*first_back, tokens_in, gain_one, grad_residual),
+    )
+    gain_blocks = hold(gain_rows, both_other).reshape(2, 4, block_rows)
+    gain_pair = [
+        lax.dynamic_index_in_dim(gain_blocks, seq_index ^ k, 1, keepdims=False) for k in range(4)
+    ]
+    gain_half = jnp.stack(gain_pair[:2]) + to_z(jnp.stack(gain_pair[2:]), 2)
+    gain_grads = gain_half[0] + to_z(gain_half[1], 1)
+    heads_own, heads_other = near_halves(
+        where, *hold((heads_keep, heads_far), grad_rows, both_near)
+    )
+    heads_near = to_z(heads_other, 1)
+    (grad_down,) = join_halves(where, *hold((down_own, down_near), heads_other), (units,), True)
     (grad_gate,) = join_halves(where, *hold((gate_own, gate_near), grad_down), (units,))
-    (grad_up,) = join_halves(where, *hold((up_own, up_near), grad_gate), (units,))
-    heads_own, heads_other = near_halves(where, *hold((heads_keep, heads_far), grad_up))
-    heads_near = to_z(heads_other, 1)
-    gain_rows = hold(gain_rows, heads_other)
-    gain_rows = gain_rows[:, :middle] + to_core(gain_rows[:, middle:])
-    gain_rows = gain_rows[:, :quarter] + to_x(gain_rows[:, quarter:])
-    gain_rows = gain_rows + to_tp(gain_rows)
-    branch_mlp = scatter_second(*hold(branch_mlp, heads_other))
-    (grad_out,) = join_halves(
-        where, *hold((out_own, out_near), gain_rows), (w_out.shape[0],), True
-    )
     (mixed,) = dense_call(
         mixed_kernel,
         "mixed",
         [(row_shape, jnp.bfloat16)],
         [],
-        (*hold(branch_mlp, grad_out), residual),
-    )
-    mixed_out = columns_out(mixed)
-    grad_tokens = columns_out(grad_rows)
-    gain_blocks = gain_rows.reshape(2, 4, block_rows)
-    gain_pair = [
-        lax.dynamic_index_in_dim(gain_blocks, seq_index ^ k, 1, keepdims=False) for k in range(4)
-    ]
-    gain_half = jnp.stack(gain_pair[:2]) + to_z(jnp.stack(gain_pair[2:]), 2)
-    gain_grads = gain_half[0] + to_z(gain_half[1], 1)
+        (*hold(branch_mlp, grad_gate), residual),
+    )
+    both_own, both_near = hold((both_own, both_near), grad_gate)
+    (grad_up,) = join_halves(
+        where,
+        *hold((both_own[:, :hidden_width], both_near[:, :hidden_width]), heads_other),
+        (units,),
+    )
+    (grad_out,) = join_halves(
+        where, both_own[:, hidden_width:], both_near[:, hidden_width:], (w_out.shape[0],), True
+    )
     grad_query_w, grad_key_w, grad_value_w = join_halves(
         where,
-        *(heads_own, heads_near),
+        *hold((heads_own, heads_near), grad_out, grad_up),
         (2 * query_width, 2 * key_width, 2 * key_width),
     )
+    mixed_out = columns_out(mixed)
+    grad_tokens = columns_out(hold(grad_rows, grad_out))
     return (
         mixed_out,
         grad_tokens,

time: 828 us -> 804 us (0.971)
  waiting for transfers between devices: 420 us -> 366 us
  starting transfers between devices: 90.4 us -> 108 us
  local copies, waits for them, and re-layouts: 56.8 us -> 74 us
    ppermute x11, waiting for transfers between devices: 49.9 us -> 5.47 us  [to_x(): return lax.ppermute(value, 'fsdp', [(i, i ^ 2) for i in range(4)])]
    ppermute x38 -> x36, waiting for transfers between devices: 306 us -> 263 us  [to_z(): return lax.ppermute(value, 'seq', [(i, i ^ step) for i in range(4)])]
    ppermute x17, waiting for transfers between devices: 30.1 us -> 65.9 us  [to_tp(): return lax.ppermute(value, 'tp', [(0, 1), (1, 0)])]
    ppermute x17, starting transfers between devices: 17.4 us -> 38.9 us  [to_tp(): return lax.ppermute(value, 'tp', [(0, 1), (1, 0)])]
    unnamed x241 -> x285, local copies, waits for them, and re-layouts: 46.3 us -> 65.3 us
    pallas_call x10 -> x8, Pallas kernels: 17.3 us -> 14.6 us  [rows_call(): pl.pallas_call(kernel, grid_spec=pltpu.PrefetchScalarGridSpec(num_scalar_...]
    ppermute x38 -> x36, starting transfers between devices: 53 us -> 51.4 us  [to_z(): return lax.ppermute(value, 'seq', [(i, i ^ step) for i in range(4)])]
    pallas_call x20 -> x21, Pallas kernels: 43.2 us -> 42.9 us  [dense_call(): pl.pallas_call(kernel, out_shape=[jax.ShapeDtypeStruct(shape, kind) for s...]
  transfers between devices with their start and end apart: 83 -> 86, of which waited for: 35 -> 38; matrix products, arithmetic and copies ran while one was open for 3% -> 3% of each run, Pallas kernels for 26% -> 25%
where the time goes in v4:
time: 804 us; the launch traced here: 789 us
  waiting for transfers between devices  366 us (46%)
  Pallas kernels  229 us (28%)
  starting transfers between devices  108 us (13%)
  local copies, waits for them, and re-layouts  74 us (9%)
  other arithmetic  9.73 us (1%)
    ppermute x36, waiting for transfers between devices, to_z(): return lax.ppermute(value, 'seq', [(i, i ^ step) for i in range(4)])  263 us
    pallas_call x19, Pallas kernels, tiled_call(): pl.pallas_call(kernel, grid=(steps,), out_shape=[jax.ShapeDtypeStruct(sha...  123 us
    ppermute x17, waiting for transfers between devices, to_tp(): return lax.ppermute(value, 'tp', [(0, 1), (1, 0)])  65.9 us
    unnamed x285, local copies, waits for them, and re-layouts  65.3 us
    ppermute x36, starting transfers between devices, to_z(): return lax.ppermute(value, 'seq', [(i, i ^ step) for i in range(4)])  51.4 us
    pallas_call x21, Pallas kernels, dense_call(): pl.pallas_call(kernel, out_shape=[jax.ShapeDtypeStruct(shape, kind) for s...  42.9 us
    ppermute x17, starting transfers between devices, to_tp(): return lax.ppermute(value, 'tp', [(0, 1), (1, 0)])  38.9 us
    pallas_call x8, Pallas kernels, fill_rows(): pl.pallas_call(lambda *refs: fill_kernel(rows, part, start, *refs), out_s...  17.5 us
  transfers between devices with their start and end apart: 86, of which 38 were waited for; matrix products, arithmetic and copies ran while one was open for 3% of the time, Pallas kernels for 25%

profile of v4, /device:TPU:18, one launch (start us, length us, event | category | flops | bytes accessed | tf_op | source)
XLA Modules:
  0.0 789.3 jit_solution(15508520455559545024)
XLA Ops:
  11.9 16.9 %collective-permute-done.3 = bf16[1,2,160]{2,1,0:T(2,128)(2,1)S(1)} collective-permute-done((bf16[1,2,160]{2,1,0:T(2,128)(2,1)S(1)}, bf16[1,2,160]{2,1,0:T(2,128)(2,1)S(1)}, u32[]{:S(2)}, u32[]{:S(2)}) %collective-permute-start.3) | collective-permute-done | bytes 672 | tf_op jit(solution)/shard_map/ppermute | solution.py:372
  53.5 23.3 %collective-permute-done.6.two_far = bf16[256,1280]{1,0:T(8,128)(2,1)} collective-permute-done((bf16[256,1280]{1,0:T(8,128)(2,1)}, bf16[256,1280]{1,0:T(8,128)(2,1)}, u32[]{:S(2)}, u32[]{:S(2)}) %collective-permute-start.6) | collective-permute-done | bytes 655392 | tf_op jit(solution)/shard_map/ppermute | solution.py:372
  96.0 19.0 %collective-permute-done.13.refs_0_ = bf16[160,1792]{1,0:T(8,128)(2,1)S(1)} collective-permute-done((bf16[160,1792]{1,0:T(8,128)(2,1)S(1)}, bf16[160,1792]{1,0:T(8,128)(2,1)S(1)}, u32[]{:S(2)}, u32[]{:S(2)}) %collective-permute-start.13) | collective-permute-done | bytes 573472 | tf_op jit(solution)/shard_map/ppermute | solution.py:372
  124.5 18.5 %collective-permute-done.16.refs_0_ = bf16[160,1792]{1,0:T(8,128)(2,1)} collective-permute-done((bf16[160,1792]{1,0:T(8,128)(2,1)}, bf16[160,1792]{1,0:T(8,128)(2,1)}, u32[]{:S(2)}, u32[]{:S(2)}) %collective-permute-start.16) | collective-permute-done | bytes 573472 | tf_op jit(solution)/shard_map/ppermute | solution.py:372
  173.1 24.8 %collective-permute-done.20.two_far = bf16[256,1280]{1,0:T(8,128)(2,1)S(1)} collective-permute-done((bf16[256,1280]{1,0:T(8,128)(2,1)S(1)}, bf16[256,1280]{1,0:T(8,128)(2,1)S(1)}, u32[]{:S(2)}, u32[]{:S(2)}) %collective-permute-start.20) | collective-permute-done | bytes 655392 | tf_op jit(solution)/shard_map/ppermute | solution.py:372
  217.7 11.5 %collective-permute-done.21.early = bf16[512,320]{1,0:T(8,128)(2,1)S(1)} collective-permute-done((bf16[512,320]{1,0:T(8,128)(2,1)S(1)}, bf16[512,320]{1,0:T(8,128)(2,1)S(1)}, u32[]{:S(2)}, u32[]{:S(2)}) %collective-permute-start.21) | collective-permute-done | bytes 327712 | tf_op jit(solution)/shard_map/ppermute | solution.py:1290
  230.4 13.7 %attend.1 = (bf16[512,640]{1,0:T(8,128)(2,1)S(1)}, f32[8,512]{1,0:T(8,128)S(1)}) custom-call(bf16[512,640]{1,0:T(8,128)(2,1)S(1)} %copy-done.32, bf16[512,320]{1,0:T(8,128)(2,1)S(1)} %collective-permute-done.21.early, bf16[512,320]{1,0:T(8,128)(2,1)S(1)} %copy-done.39, s32[2,512]{1,0:T(2,128)S(1)} %pad_add_fusion.1.query_ids, s32[1024,2]{1,0:T(8,128)S(1)} %copy.62.key_ids), custom_call_target="tpu_custom_call" | custom-call | flops 1024 | bytes 4096 | tf_op jit(solution)/shard_map/attend/pallas_call | solution.py:523
  252.0 9.8 %collective-permute-start.23 = (bf16[256,1280]{1,0:T(8,128)(2,1)S(1)}, bf16[256,1280]{1,0:T(8,128)(2,1)S(1)}, u32[]{:S(2)}, u32[]{:S(2)}) collective-permute-start(bf16[256,1280]{1,0:T(8,128)(2,1)S(1)} %get-tuple-element.344), channel_id=1, source_target_pairs={{0,2},{2,0},{4,6},{6,4},{1,3},{3,1},{5,7},{7,5},{8,10},{10,8},{12,... | collective-permute-start | bytes 1966088 | tf_op jit(solution)/shard_map/ppermute | solution.py:372
  265.9 34.2 %collective-permute-done.23.got_two = bf16[256,1280]{1,0:T(8,128)(2,1)S(1)} collective-permute-done((bf16[256,1280]{1,0:T(8,128)(2,1)S(1)}, bf16[256,1280]{1,0:T(8,128)(2,1)S(1)}, u32[]{:S(2)}, u32[]{:S(2)}) %collective-permute-start.23) | collective-permute-done | bytes 655392 | tf_op jit(solution)/shard_map/ppermute | solution.py:372
  314.2 7.6 collective-permute-done.24.last_one
  325.5 8.1 %collective-permute-done.31.second.two_tp = bf16[128,1280]{1,0:T(8,128)(2,1)S(1)} collective-permute-done((bf16[128,1280]{1,0:T(8,128)(2,1)S(1)}, bf16[128,1280]{1,0:T(8,128)(2,1)S(1)}, u32[]{:S(2)}, u32[]{:S(2)}) %collective-permute-start.31) | collective-permute-done | bytes 327712 | tf_op jit(solution)/shard_map/ppermute | solution.py:376
  335.8 12.9 %collective-permute-done.32.two_far = bf16[256,1280]{1,0:T(8,128)(2,1)S(1)} collective-permute-done((bf16[256,1280]{1,0:T(8,128)(2,1)S(1)}, bf16[256,1280]{1,0:T(8,128)(2,1)S(1)}, u32[]{:S(2)}, u32[]{:S(2)}) %collective-permute-start.32) | collective-permute-done | bytes 655392 | tf_op jit(solution)/shard_map/ppermute | solution.py:372
  352.0 15.9 %hidden_units.1 = (bf16[512,1792]{1,0:T(8,128)(2,1)S(1)}, f32[512,1792]{1,0:T(8,128)}, f32[512,1792]{1,0:T(8,128)}) custom-call(bf16[512,2560]{1,0:T(8,128)(2,1)S(1)} %take_rows.6.normed.left, bf16[1280,1792]{1,0:T(8,128)(2,1)} %fill_rows.13.gate_m.refs_2_, bf16[1280,1792]{1,0:T(8,128)(2,1)} %collective-permute-done.33.gate_o.refs_3_, ...), custom_call_target="tpu_custom_call" | custom-call | flops 1024 | bytes 4096 | tf_op jit(solution)/shard_map/hidden_units/pallas_call | solution.py:668
  374.2 8.3 %collective-permute-done.36.left_other = bf16[512,640]{1,0:T(8,128)(2,1)S(1)} collective-permute-done((bf16[512,640]{1,0:T(8,128)(2,1)S(1)}, bf16[512,640]{1,0:T(8,128)(2,1)S(1)}, u32[]{:S(2)}, u32[]{:S(2)}) %collective-permute-start.36) | collective-permute-done | bytes 655392 | tf_op jit(solution)/shard_map/ppermute | solution.py:364
  397.1 7.9 %project_back.5 = (bf16[256,1280]{1,0:T(8,128)(2,1)S(1)}, bf16[256,1280]{1,0:T(8,128)(2,1)S(1)}, bf16[256,1280]{1,0:T(8,128)(2,1)S(1)}, bf16[256,1280]{1,0:T(8,128)(2,1)S(1)}) custom-call(bf16[512,1792]{1,0:T(8,128)(2,1)S(1)} %copy-done.12, bf16[1280,1792]{1,0:T(8,128)(2,1)} %fill_rows.15.refs_1_.down_m, ...), custom_call_target="tpu_custom_call" | custom-call | flops 1024 | bytes 4096 | tf_op jit(solution)/shard_map/project_back/pallas_call | solution.py:668
  405.1 11.5 %hidden_grads.1 = (bf16[512,1792]{1,0:T(8,128)(2,1)S(1)}, bf16[512,1792]{1,0:T(8,128)(2,1)S(1)}) custom-call(bf16[512,2560]{1,0:T(8,128)(2,1)} %copy-done.3, bf16[1280,1792]{1,0:T(8,128)(2,1)} %fill_rows.15.refs_1_.down_m, bf16[1280,1792]{1,0:T(8,128)(2,1)} %collective-permute-done.39.refs_2_.down_o, f32[512,1792]{1,0:T(8,128)} %get-tuple-element.390.gate_slope, ...), custom_call_target="tpu_custom_call" | custom-call | flops 1024 | bytes 4096 | tf_op jit(solution)/shard_map/hidden_grads/pallas_call | solution.py:668
  419.6 14.2 %collective-permute-done.40.got_one = bf16[256,1280]{1,0:T(8,128)(2,1)S(1)} collective-permute-done((bf16[256,1280]{1,0:T(8,128)(2,1)S(1)}, bf16[256,1280]{1,0:T(8,128)(2,1)S(1)}, u32[]{:S(2)}, u32[]{:S(2)}) %collective-permute-start.40) | collective-permute-done | bytes 655392 | tf_op jit(solution)/shard_map/ppermute | solution.py:376
  433.8 14.2 %project_back.6 = (bf16[256,1280]{1,0:T(8,128)(2,1)S(1)}, bf16[256,1280]{1,0:T(8,128)(2,1)S(1)}, bf16[256,1280]{1,0:T(8,128)(2,1)S(1)}, bf16[256,1280]{1,0:T(8,128)(2,1)S(1)}) custom-call(bf16[512,1792]{1,0:T(8,128)(2,1)S(1)} %get-tuple-element.426.refs_0_.right, bf16[512,1792]{1,0:T(8,128)(2,1)} %copy-done.9, bf16[1280,1792]{1,0:T(8,128)(2,1)} %fill_rows.13.gate_m.refs_2_, ...), custom_call_target="tpu_custom_call" | custom-call | flops 1024 | bytes 4096 | tf_op jit(solution)/shard_map/project_back/pallas_call | solution.py:668
  457.3 6.9 outer.12
  467.4 15.3 %collective-permute-done.47.got_one = bf16[256,1280]{1,0:T(8,128)(2,1)S(1)} collective-permute-done((bf16[256,1280]{1,0:T(8,128)(2,1)S(1)}, bf16[256,1280]{1,0:T(8,128)(2,1)S(1)}, u32[]{:S(2)}, u32[]{:S(2)}) %collective-permute-start.47) | collective-permute-done | bytes 655392 | tf_op jit(solution)/shard_map/ppermute | solution.py:376
  514.2 6.8 collective-permute-done.51.last_one
  541.2 13.5 %collective-permute-start.56 = (bf16[256,1280]{1,0:T(8,128)(2,1)S(1)}, bf16[256,1280]{1,0:T(8,128)(2,1)S(1)}, u32[]{:S(2)}, u32[]{:S(2)}) collective-permute-start(bf16[256,1280]{1,0:T(8,128)(2,1)S(1)} %pair_rows.14), channel_id=1, source_target_pairs={{0,1},{1,0},{2,3},{3,2},{4,5},{5,4},{6,7},{7,6},{8,9},{9,8},{10,11... | collective-permute-start | bytes 1966088 | tf_op jit(solution)/shard_map/ppermute | solution.py:376
  565.6 18.1 %collective-permute-done.58.refs_1_.refs_3_ = bf16[320,1792]{1,0:T(8,128)(2,1)S(1)} collective-permute-done((bf16[320,1792]{1,0:T(8,128)(2,1)S(1)}, bf16[320,1792]{1,0:T(8,128)(2,1)S(1)}, u32[]{:S(2)}, u32[]{:S(2)}) %collective-permute-start.58) | collective-permute-done | bytes 1146912 | tf_op jit(solution)/shard_map/ppermute | solution.py:372
  593.9 15.6 %attend_back.1 = (bf16[512,640]{1,0:T(8,128)(2,1)S(1)}, bf16[512,320]{1,0:T(8,128)(2,1)S(1)}, f32[512,320]{1,0:T(8,128)S(1)}) custom-call(bf16[512,640]{1,0:T(8,128)(2,1)S(1)} %copy-done.33, bf16[512,320]{1,0:T(8,128)(2,1)S(1)} %copy-done.42, bf16[512,320]{1,0:T(8,128)(2,1)S(1)} %copy-done.40, s32[2,512]{1,0:T(2,128)S(1)} %copy-done.95, ...), custom_call_target="tpu_custom_call" | custom-call | flops 1024 | bytes 4096 | tf_op jit(solution)/shard_map/attend_back/pallas_call | solution.py:523
  624.4 10.0 %collective-permute-done.65.late = bf16[512,320]{1,0:T(8,128)(2,1)S(1)} collective-permute-done((bf16[512,320]{1,0:T(8,128)(2,1)S(1)}, bf16[512,320]{1,0:T(8,128)(2,1)S(1)}, u32[]{:S(2)}, u32[]{:S(2)}) %collective-permute-start.65) | collective-permute-done | bytes 327712 | tf_op jit(solution)/shard_map/ppermute | solution.py:1404
  643.4 6.6 project_back.7
  662.4 15.2 %collective-permute-done.76 = f32[2,1280]{1,0:T(2,128)S(1)} collective-permute-done((f32[2,1280]{1,0:T(2,128)S(1)}, f32[2,1280]{1,0:T(2,128)S(1)}, u32[]{:S(2)}, u32[]{:S(2)}) %collective-permute-start.76) | collective-permute-done | bytes 10272 | tf_op jit(solution)/shard_map/ppermute | solution.py:376
  677.6 12.4 %collective-permute-done.74.got_two = bf16[256,1280]{1,0:T(8,128)(2,1)S(1)} collective-permute-done((bf16[256,1280]{1,0:T(8,128)(2,1)S(1)}, bf16[256,1280]{1,0:T(8,128)(2,1)S(1)}, u32[]{:S(2)}, u32[]{:S(2)}) %collective-permute-start.74) | collective-permute-done | bytes 655392 | tf_op jit(solution)/shard_map/ppermute | solution.py:372
  696.8 11.6 %collective-permute-done.78.refs_1_.refs_3_ = bf16[320,2432]{1,0:T(8,128)(2,1)S(1)} collective-permute-done((bf16[320,2432]{1,0:T(8,128)(2,1)}, bf16[320,2432]{1,0:T(8,128)(2,1)S(1)}, u32[]{:S(2)}, u32[]{:S(2)}) %collective-permute-start.78) | collective-permute-done | bytes 1556512 | tf_op jit(solution)/shard_map/ppermute | solution.py:372
  716.6 7.5 collective-permute-start.81
  724.1 8.7 %collective-permute-done.84 = f32[2,2,160]{2,1,0:T(2,128)S(1)} collective-permute-done((f32[2,2,160]{2,1,0:T(2,128)S(1)}, f32[2,2,160]{2,1,0:T(2,128)S(1)}, u32[]{:S(2)}, u32[]{:S(2)}) %collective-permute-start.84) | collective-permute-done | bytes 2592 | tf_op jit(solution)/shard_map/ppermute | solution.py:372
  732.9 18.8 %collective-permute-done.85 = f32[2,160]{1,0:T(2,128)S(1)} collective-permute-done((f32[2,160]{1,0:T(2,128)S(1)}, f32[2,160]{1,0:T(2,128)S(1)}, u32[]{:S(2)}, u32[]{:S(2)}) %collective-permute-start.85) | collective-permute-done | bytes 1312 | tf_op jit(solution)/shard_map/ppermute | solution.py:372
  (566 shorter events, 347.1 us)
Async XLA Ops:
  36.1 51.5 %collective-permute-start.9 = (bf16[320,1664]{1,0:T(8,128)(2,1)}, bf16[320,1664]{1,0:T(8,128)(2,1)}, u32[]{:S(2)}, u32[]{:S(2)}) collective-permute-start(bf16[320,1664]{1,0:T(8,128)(2,1)} %fill_rows.8.refs_1_), channel_id=1, source_target_pairs={{0,4},{2,6},{4,0},{6,2},{1,5},{3,7},{5,1},{7,3},{8,12},{10,14},{12... | collective-permute-start | bytes 3194888 | tf_op jit(solution)/shard_map/ppermute | solution.py:372
  37.3 39.5 %collective-permute-start.6 = (bf16[256,1280]{1,0:T(8,128)(2,1)}, bf16[256,1280]{1,0:T(8,128)(2,1)}, u32[]{:S(2)}, u32[]{:S(2)}) collective-permute-start(bf16[256,1280]{1,0:T(8,128)(2,1)} %pair_rows.9), channel_id=1, source_target_pairs={{0,2},{2,0},{4,6},{6,4},{1,3},{3,1},{5,7},{7,5},{8,10},{10,8},{12,... | collective-permute-start | bytes 1966088 | tf_op jit(solution)/shard_map/ppermute | solution.py:372
  39.8 37.0 %collective-permute-start.5 = (bf16[256,1280]{1,0:T(8,128)(2,1)}, bf16[256,1280]{1,0:T(8,128)(2,1)}, u32[]{:S(2)}, u32[]{:S(2)}) collective-permute-start(bf16[256,1280]{1,0:T(8,128)(2,1)} %pair_rows.8), channel_id=1, source_target_pairs={{0,1},{1,0},{2,3},{3,2},{4,5},{5,4},{6,7},{7,6},{8,9},{9,8},{10,11... | collective-permute-start | bytes 1966088 | tf_op jit(solution)/shard_map/ppermute | solution.py:376
  42.3 43.3 %collective-permute-start.10 = (bf16[160,1792]{1,0:T(8,128)(2,1)}, bf16[160,1792]{1,0:T(8,128)(2,1)}, u32[]{:S(2)}, u32[]{:S(2)}) collective-permute-start(bf16[160,1792]{1,0:T(8,128)(2,1)} %get-tuple-element.303), channel_id=1, source_target_pairs={{0,2},{2,0},{4,6},{6,4},{1,3},{3,1},{5,7},{7,5},{8,10},{10,8},{12,... | collective-permute-start | bytes 1720328 | tf_op jit(solution)/shard_map/ppermute | solution.py:372
  90.8 59.1 %collective-permute-start.11 = (bf16[640,1664]{1,0:T(8,128)(2,1)}, bf16[640,1664]{1,0:T(8,128)(2,1)}, u32[]{:S(2)}, u32[]{:S(2)}) collective-permute-start(bf16[640,1664]{1,0:T(8,128)(2,1)} %get-tuple-element.308), channel_id=1, source_target_pairs={{0,16},{8,24},{16,0},{24,8},{1,17},{9,25},{17,1},{25,9},{2,18},{10... | collective-permute-start | bytes 6389768 | tf_op jit(solution)/shard_map/ppermute | solution.py:368
  93.9 52.6 %collective-permute-start.12 = (bf16[320,1792]{1,0:T(8,128)(2,1)}, bf16[320,1792]{1,0:T(8,128)(2,1)}, u32[]{:S(2)}, u32[]{:S(2)}) collective-permute-start(bf16[320,1792]{1,0:T(8,128)(2,1)} %fill_rows.9.refs_1_), channel_id=1, source_target_pairs={{0,4},{2,6},{4,0},{6,2},{1,5},{3,7},{5,1},{7,3},{8,12},{10,14},{12... | collective-permute-start | bytes 3440648 | tf_op jit(solution)/shard_map/ppermute | solution.py:372
  94.5 48.5 %collective-permute-start.16 = (bf16[160,1792]{1,0:T(8,128)(2,1)}, bf16[160,1792]{1,0:T(8,128)(2,1)}, u32[]{:S(2)}, u32[]{:S(2)}) collective-permute-start(bf16[160,1792]{1,0:T(8,128)(2,1)} %get-tuple-element.316), channel_id=1, source_target_pairs={{0,2},{2,0},{4,6},{6,4},{1,3},{3,1},{5,7},{7,5},{8,10},{10,8},{12,... | collective-permute-start | bytes 1720328 | tf_op jit(solution)/shard_map/ppermute | solution.py:372
  152.4 58.1 %collective-permute-start.26 = (bf16[640,1792]{1,0:T(8,128)(2,1)}, bf16[640,1792]{1,0:T(8,128)(2,1)}, u32[]{:S(2)}, u32[]{:S(2)}) collective-permute-start(bf16[640,1792]{1,0:T(8,128)(2,1)} %get-tuple-element.351), channel_id=1, source_target_pairs={{0,16},{8,24},{16,0},{24,8},{1,17},{9,25},{17,1},{25,9},{2,18},{10... | collective-permute-start | bytes 6881288 | tf_op jit(solution)/shard_map/ppermute | solution.py:368
  155.3 51.9 %collective-permute-start.18 = (bf16[320,1792]{1,0:T(8,128)(2,1)}, bf16[320,1792]{1,0:T(8,128)(2,1)}, u32[]{:S(2)}, u32[]{:S(2)}) collective-permute-start(bf16[320,1792]{1,0:T(8,128)(2,1)} %fill_rows.10.refs_1_), channel_id=1, source_target_pairs={{0,4},{2,6},{4,0},{6,2},{1,5},{3,7},{5,1},{7,3},{8,12},{10,14},{12... | collective-permute-start | bytes 3440648 | tf_op jit(solution)/shard_map/ppermute | solution.py:372
  160.0 37.9 %collective-permute-start.20 = (bf16[256,1280]{1,0:T(8,128)(2,1)S(1)}, bf16[256,1280]{1,0:T(8,128)(2,1)S(1)}, u32[]{:S(2)}, u32[]{:S(2)}) collective-permute-start(bf16[256,1280]{1,0:T(8,128)(2,1)S(1)} %pair_rows.11), channel_id=1, source_target_pairs={{0,2},{2,0},{4,6},{6,4},{1,3},{3,1},{5,7},{7,5},{8,10},{10,8},{12,... | collective-permute-start | bytes 1966088 | tf_op jit(solution)/shard_map/ppermute | solution.py:372
  162.0 35.9 %collective-permute-start.19 = (bf16[256,1280]{1,0:T(8,128)(2,1)S(1)}, bf16[256,1280]{1,0:T(8,128)(2,1)S(1)}, u32[]{:S(2)}, u32[]{:S(2)}) collective-permute-start(bf16[256,1280]{1,0:T(8,128)(2,1)S(1)} %pair_rows.10), channel_id=1, source_target_pairs={{0,1},{1,0},{2,3},{3,2},{4,5},{5,4},{6,7},{7,6},{8,9},{9,8},{10,11... | collective-permute-start | bytes 1966088 | tf_op jit(solution)/shard_map/ppermute | solution.py:376
  213.1 94.1 %collective-permute-start.27 = (bf16[640,1792]{1,0:T(8,128)(2,1)}, bf16[640,1792]{1,0:T(8,128)(2,1)}, u32[]{:S(2)}, u32[]{:S(2)}) collective-permute-start(bf16[640,1792]{1,0:T(8,128)(2,1)} %get-tuple-element.354), channel_id=1, source_target_pairs={{0,16},{8,24},{16,0},{24,8},{1,17},{9,25},{17,1},{25,9},{2,18},{10... | collective-permute-start | bytes 6881288 | tf_op jit(solution)/shard_map/ppermute | solution.py:368
  244.1 58.7 %collective-permute-start.28 = (bf16[320,1792]{1,0:T(8,128)(2,1)S(1)}, bf16[320,1792]{1,0:T(8,128)(2,1)S(1)}, u32[]{:S(2)}, u32[]{:S(2)}) collective-permute-start(bf16[320,1792]{1,0:T(8,128)(2,1)S(1)} %copy-done.24), channel_id=1, source_target_pairs={{0,4},{2,6},{4,0},{6,2},{1,5},{3,7},{5,1},{7,3},{8,12},{10,14},{12... | collective-permute-start | bytes 3440648 | tf_op jit(solution)/shard_map/ppermute | solution.py:372
  252.0 48.2 %collective-permute-start.23 = (bf16[256,1280]{1,0:T(8,128)(2,1)S(1)}, bf16[256,1280]{1,0:T(8,128)(2,1)S(1)}, u32[]{:S(2)}, u32[]{:S(2)}) collective-permute-start(bf16[256,1280]{1,0:T(8,128)(2,1)S(1)} %get-tuple-element.344), channel_id=1, source_target_pairs={{0,2},{2,0},{4,6},{6,4},{1,3},{3,1},{5,7},{7,5},{8,10},{10,8},{12,... | collective-permute-start | bytes 1966088 | tf_op jit(solution)/shard_map/ppermute | solution.py:372
  261.8 87.9 %collective-permute-start.33 = (bf16[1280,1792]{1,0:T(8,128)(2,1)}, bf16[1280,1792]{1,0:T(8,128)(2,1)}, u32[]{:S(2)}, u32[]{:S(2)}) collective-permute-start(bf16[1280,1792]{1,0:T(8,128)(2,1)} %fill_rows.13.gate_m.refs_2_), channel_id=1, source_target_pairs={{0,8},{8,0},{16,24},{24,16},{1,9},{9,1},{17,25},{25,17},{2,10},{10... | collective-permute-start | bytes 13762568 | tf_op jit(solution)/shard_map/ppermute | solution.py:364
  309.9 39.9 %collective-permute-start.34 = (bf16[1280,1792]{1,0:T(8,128)(2,1)}, bf16[1280,1792]{1,0:T(8,128)(2,1)S(1)}, u32[]{:S(2)}, u32[]{:S(2)}) collective-permute-start(bf16[1280,1792]{1,0:T(8,128)(2,1)} %fill_rows.14.up_m.refs_4_), channel_id=1, source_target_pairs={{0,8},{8,0},{16,24},{24,16},{1,9},{9,1},{17,25},{25,17},{2,10},{10... | collective-permute-start | bytes 13762568 | tf_op jit(solution)/shard_map/ppermute | solution.py:364
  309.9 59.2 %collective-permute-start.38 = (bf16[640,1792]{1,0:T(8,128)(2,1)}, bf16[640,1792]{1,0:T(8,128)(2,1)}, u32[]{:S(2)}, u32[]{:S(2)}) collective-permute-start(bf16[640,1792]{1,0:T(8,128)(2,1)} %get-tuple-element.372), channel_id=1, source_target_pairs={{0,16},{8,24},{16,0},{24,8},{1,17},{9,25},{17,1},{25,9},{2,18},{10... | collective-permute-start | bytes 6881288 | tf_op jit(solution)/shard_map/ppermute | solution.py:368
  390.0 63.3 %collective-permute-start.46 = (bf16[640,1792]{1,0:T(8,128)(2,1)}, bf16[640,1792]{1,0:T(8,128)(2,1)S(1)}, u32[]{:S(2)}, u32[]{:S(2)}) collective-permute-start(bf16[640,1792]{1,0:T(8,128)(2,1)} %outer.10), channel_id=1, source_target_pairs={{0,16},{8,24},{16,0},{24,8},{1,17},{9,25},{17,1},{25,9},{2,18},{10... | collective-permute-start | bytes 6881288 | tf_op jit(solution)/shard_map/ppermute | solution.py:368
  416.6 40.6 %collective-permute-start.45 = (bf16[512,1792]{1,0:T(8,128)(2,1)S(1)}, bf16[512,1792]{1,0:T(8,128)(2,1)S(1)}, u32[]{:S(2)}, u32[]{:S(2)}) collective-permute-start(bf16[512,1792]{1,0:T(8,128)(2,1)S(1)} %get-tuple-element.426.refs_0_.right), channel_id=1, source_target_pairs={{0,8},{8,0},{16,24},{24,16},{1,9},{9,1},{17,25},{25,17},{2,10},{10... | collective-permute-start | bytes 5505032 | tf_op jit(solution)/shard_map/ppermute | solution.py:364
  419.6 37.6 %collective-permute-start.42 = (bf16[512,640]{1,0:T(8,128)(2,1)}, bf16[512,640]{1,0:T(8,128)(2,1)S(1)}, u32[]{:S(2)}, u32[]{:S(2)}) collective-permute-start(bf16[512,640]{1,0:T(8,128)(2,1)} %get-tuple-element.601), channel_id=1, source_target_pairs={{0,8},{8,0},{16,24},{24,16},{1,9},{9,1},{17,25},{25,17},{2,10},{10... | collective-permute-start | bytes 1966088 | tf_op jit(solution)/shard_map/ppermute | solution.py:364
  464.2 73.4 %collective-permute-start.49 = (bf16[640,1792]{1,0:T(8,128)(2,1)}, bf16[640,1792]{1,0:T(8,128)(2,1)}, u32[]{:S(2)}, u32[]{:S(2)}) collective-permute-start(bf16[640,1792]{1,0:T(8,128)(2,1)} %outer.12), channel_id=1, source_target_pairs={{0,16},{8,24},{16,0},{24,8},{1,17},{9,25},{17,1},{25,9},{2,18},{10... | collective-permute-start | bytes 6881288 | tf_op jit(solution)/shard_map/ppermute | solution.py:368
  465.5 35.7 %collective-permute-start.44 = (bf16[512,1792]{1,0:T(8,128)(2,1)S(1)}, bf16[512,1792]{1,0:T(8,128)(2,1)S(1)}, u32[]{:S(2)}, u32[]{:S(2)}) collective-permute-start(bf16[512,1792]{1,0:T(8,128)(2,1)S(1)} %copy-done.10), channel_id=1, source_target_pairs={{0,8},{8,0},{16,24},{24,16},{1,9},{9,1},{17,25},{25,17},{2,10},{10... | collective-permute-start | bytes 5505032 | tf_op jit(solution)/shard_map/ppermute | solution.py:364
  467.4 62.4 %collective-permute-start.50 = (bf16[320,1792]{1,0:T(8,128)(2,1)}, bf16[320,1792]{1,0:T(8,128)(2,1)S(1)}, u32[]{:S(2)}, u32[]{:S(2)}) collective-permute-start(bf16[320,1792]{1,0:T(8,128)(2,1)} %copy-done.98), channel_id=1, source_target_pairs={{0,4},{2,6},{4,0},{6,2},{1,5},{3,7},{5,1},{7,3},{8,12},{10,14},{12... | collective-permute-start | bytes 3440648 | tf_op jit(solution)/shard_map/ppermute | solution.py:372
  540.8 69.5 %collective-permute-start.55 = (bf16[640,1792]{1,0:T(8,128)(2,1)}, bf16[640,1792]{1,0:T(8,128)(2,1)S(1)}, u32[]{:S(2)}, u32[]{:S(2)}) collective-permute-start(bf16[640,1792]{1,0:T(8,128)(2,1)} %outer.14), channel_id=1, source_target_pairs={{0,16},{8,24},{16,0},{24,8},{1,17},{9,25},{17,1},{25,9},{2,18},{10... | collective-permute-start | bytes 6881288 | tf_op jit(solution)/shard_map/ppermute | solution.py:368
  563.8 47.9 %collective-permute-start.68 = (bf16[512,640]{1,0:T(8,128)(2,1)S(1)}, bf16[512,640]{1,0:T(8,128)(2,1)S(1)}, u32[]{:S(2)}, u32[]{:S(2)}) collective-permute-start(bf16[512,640]{1,0:T(8,128)(2,1)S(1)} %get-tuple-element.478.refs_0_.right), channel_id=1, source_target_pairs={{0,8},{8,0},{16,24},{24,16},{1,9},{9,1},{17,25},{25,17},{2,10},{10... | collective-permute-start | bytes 1966088 | tf_op jit(solution)/shard_map/ppermute | solution.py:364
  565.1 46.7 %collective-permute-start.66 = (bf16[512,640]{1,0:T(8,128)(2,1)}, bf16[512,640]{1,0:T(8,128)(2,1)S(1)}, u32[]{:S(2)}, u32[]{:S(2)}) collective-permute-start(bf16[512,640]{1,0:T(8,128)(2,1)} %get-tuple-element.597), channel_id=1, source_target_pairs={{0,8},{8,0},{16,24},{24,16},{1,9},{9,1},{17,25},{25,17},{2,10},{10... | collective-permute-start | bytes 1966088 | tf_op jit(solution)/shard_map/ppermute | solution.py:364
  640.5 67.9 %collective-permute-start.78 = (bf16[320,2432]{1,0:T(8,128)(2,1)}, bf16[320,2432]{1,0:T(8,128)(2,1)S(1)}, u32[]{:S(2)}, u32[]{:S(2)}) collective-permute-start(bf16[320,2432]{1,0:T(8,128)(2,1)} %get-tuple-element.483), channel_id=1, source_target_pairs={{0,4},{2,6},{4,0},{6,2},{1,5},{3,7},{5,1},{7,3},{8,12},{10,14},{12... | collective-permute-start | bytes 4669448 | tf_op jit(solution)/shard_map/ppermute | solution.py:372
  653.7 36.6 %collective-permute-start.72 = (bf16[640,1024]{1,0:T(8,128)(2,1)S(1)}, bf16[640,1024]{1,0:T(8,128)(2,1)S(1)}, u32[]{:S(2)}, u32[]{:S(2)}) collective-permute-start(bf16[640,1024]{1,0:T(8,128)(2,1)S(1)} %outer.19), channel_id=1, source_target_pairs={{0,16},{8,24},{16,0},{24,8},{1,17},{9,25},{17,1},{25,9},{2,18},{10... | collective-permute-start | bytes 3932168 | tf_op jit(solution)/shard_map/ppermute | solution.py:368
  711.0 47.8 %collective-permute-start.82 = (bf16[160,2432]{1,0:T(8,128)(2,1)}, bf16[160,2432]{1,0:T(8,128)(2,1)S(1)}, u32[]{:S(2)}, u32[]{:S(2)}) collective-permute-start(bf16[160,2432]{1,0:T(8,128)(2,1)} %get-tuple-element.516), channel_id=1, source_target_pairs={{0,2},{2,0},{4,6},{6,4},{1,3},{3,1},{5,7},{7,5},{8,10},{10,8},{12,... | collective-permute-start | bytes 2334728 | tf_op jit(solution)/shard_map/ppermute | solution.py:372
  714.4 44.3 %collective-permute-start.77 = (bf16[320,1024]{1,0:T(8,128)(2,1)}, bf16[320,1024]{1,0:T(8,128)(2,1)S(1)}, u32[]{:S(2)}, u32[]{:S(2)}) collective-permute-start(bf16[320,1024]{1,0:T(8,128)(2,1)} %copy-done.99), channel_id=1, source_target_pairs={{0,4},{2,6},{4,0},{6,2},{1,5},{3,7},{5,1},{7,3},{8,12},{10,14},{12... | collective-permute-start | bytes 1966088 | tf_op jit(solution)/shard_map/ppermute | solution.py:372
  716.2 36.0 %collective-permute-start.80 = (bf16[128,1280]{1,0:T(8,128)(2,1)}, bf16[128,1280]{1,0:T(8,128)(2,1)S(1)}, u32[]{:S(2)}, u32[]{:S(2)}) collective-permute-start(bf16[128,1280]{1,0:T(8,128)(2,1)} %copy-done.104), channel_id=1, source_target_pairs={{0,2},{2,0},{4,6},{6,4},{1,3},{3,1},{5,7},{7,5},{8,10},{10,8},{12,... | collective-permute-start | bytes 983048 | tf_op jit(solution)/shard_map/ppermute | solution.py:372
  716.6 35.7 %collective-permute-start.81 = (bf16[128,1280]{1,0:T(8,128)(2,1)S(1)}, bf16[128,1280]{1,0:T(8,128)(2,1)S(1)}, u32[]{:S(2)}, u32[]{:S(2)}) collective-permute-start(bf16[128,1280]{1,0:T(8,128)(2,1)S(1)} %get-tuple-element.520), channel_id=1, source_target_pairs={{0,1},{1,0},{2,3},{3,2},{4,5},{5,4},{6,7},{7,6},{8,9},{9,8},{10,11... | collective-permute-start | bytes 983048 | tf_op jit(solution)/shard_map/ppermute | solution.py:376
  (192 other events, 2086.6 us)

commit v5 on v4

--- a/solution.py
+++ b/solution.py
@@ -1304,9 +1304,9 @@
     attended_other = cross_right(attended_low, 1)
     down_far = to_z(hold(down_pair, log_total), 2)
     branch = scatter_first(
-        *project_back([attended_low], [first_weights], heads_width)
-    )
-    branch = scatter_middle(*branch)
+        *project_back([hold(attended_low, normed_other)], [first_weights], heads_width)
+    )
+    branch = scatter_middle(*hold(branch, attended_other))
     branch = scatter_second(*branch)
     down_plane, down_mine = place_rows(*hold((down_pair, down_far), branch[:2]), seq_index)
     up_mine = fill_rows(*hold((up_mine, up_x), down_plane))
@@ -1323,12 +1323,14 @@
     span_two = take_rows(*two_wait)
     span_other = cross_left(span_two)
     cot_other = cross_left(cot_span, log_total)
-    hidden_low, gate_slope, up_slope = hidden_units(span_two, gate_weights, up_weights)
+    hidden_low, gate_slope, up_slope = hidden_units(
+        hold(span_two, cot_other), gate_weights, up_weights
+    )
     hidden_other = cross_right(hidden_low, 1)
     down_mine = fill_rows(*hold((down_mine, down_x), hidden_low))
     down_weights = down_mine, to_core(down_mine)
 
-    down_parts = hold((cot_span, cot_other, hidden_low, hidden_other), down_mine)
+    down_parts = hold((cot_span, cot_other, hidden_low, hidden_other), down_mine, span_other)
     down_give = outer(*down_parts, 1)
     down_back = to_x(down_give)
     down_keep = outer(*hold(down_parts, down_give), 0)
@@ -1369,12 +1371,8 @@
     grad_wait = gather_second(*hold(grad_wait, gate_give))
     grad_span = take_rows(*grad_wait)
     down_near = to_z(hold(down_other, grad_span), 1)
-    gate_own, gate_other = near_halves(where, *hold((gate_keep, gate_far), grad_span))
-    gate_near = to_z(gate_other, 1)
     span_grad_other = cross_left(grad_span)
-    grad_attended = project(
-        hold(grad_span, gate_other), first_weights, heads_width, query_width, jnp.bfloat16
-    )
+    grad_attended = project(grad_span, first_weights, heads_width, query_width, jnp.bfloat16)
     grad_query, grad_early, grad_own = dense_call(
         functools.partial(attend_back_kernel, score_scale),
         "attend_back",
@@ -1400,15 +1398,17 @@
             sin_wide,
         ),
     )
-    up_terms = hold((up_keep, up_back), grad_early, down_near, gate_near)
+    gate_own, gate_other = near_halves(where, *hold((gate_keep, gate_far), grad_early))
+    up_terms = hold((up_keep, up_back), gate_other, down_near)
     late_kv = lax.ppermute(hold(grad_early, up_terms[1]), "seq", [(2, 0), (3, 1)])
     out_parts = hold((grad_span, span_grad_other, attended_low, attended_other), up_terms[1])
-    branch_mlp = scatter_second(*hold(branch_mlp, up_terms[1]))
+    gate_near = to_z(hold(gate_other, up_terms[1]), 1)
     out_give = outer(*out_parts, 1)
     out_back = to_x(out_give)
     out_keep = outer(*out_parts, 0)
-    both_keep, both_give = far_halves(where, up_terms, hold((out_keep, out_back), late_kv, branch_mlp[2:]))
+    both_keep, both_give = far_halves(where, up_terms, hold((out_keep, out_back), late_kv, gate_near))
     both_far = to_z(both_give, 2)
+    branch_mlp = scatter_second(*hold(branch_mlp, both_give))
     (grad_raw,) = dense_call(
         join_kernel,
         "join",
@@ -1439,7 +1439,9 @@
     heads_far = to_z(heads_give, 2)
     gain_rows = hold(gain_rows, heads_give)
     gain_rows = gain_rows[:, :quarter] + to_x(gain_rows[:, quarter:])
-    both_own, both_other = near_halves(where, *hold((both_keep, both_far), heads_give, gain_rows))
+    both_own, both_other = near_halves(
+        where, *hold((both_keep, both_far), heads_give, gain_rows, branch_mlp[2:])
+    )
     both_near = to_z(both_other, 1)
     first_back = scatter_second(*hold(first_back, both_other))
     (grad_rows,) = dense_call(

time: 804 us -> 788 us (0.980)
  waiting for transfers between devices: 366 us -> 347 us
    ppermute x17, waiting for transfers between devices: 65.9 us -> 39.4 us  [to_tp(): return lax.ppermute(value, 'tp', [(0, 1), (1, 0)])]
    ppermute x17, starting transfers between devices: 38.9 us -> 18.2 us  [to_tp(): return lax.ppermute(value, 'tp', [(0, 1), (1, 0)])]
    ppermute x36, starting transfers between devices: 51.4 us -> 71 us  [to_z(): return lax.ppermute(value, 'seq', [(i, i ^ step) for i in range(4)])]
    ppermute x11, waiting for transfers between devices: 5.47 us -> 13.7 us  [to_x(): return lax.ppermute(value, 'fsdp', [(i, i ^ 2) for i in range(4)])]
    unnamed x285 -> x281, local copies, waits for them, and re-layouts: 65.3 us -> 66.8 us
  transfers between devices with their start and end apart: 86 -> 86, of which waited for: 38 -> 39; matrix products, arithmetic and copies ran while one was open for 3% -> 4% of each run, Pallas kernels for 25% -> 26%
where the time goes in v5:
time: 788 us; the launch traced here: 778 us
  waiting for transfers between devices  347 us (44%)
  Pallas kernels  234 us (30%)
  starting transfers between devices  106 us (13%)
  local copies, waits for them, and re-layouts  75.5 us (10%)
  other arithmetic  12.7 us (2%)
    ppermute x36, waiting for transfers between devices, to_z(): return lax.ppermute(value, 'seq', [(i, i ^ step) for i in range(4)])  266 us
    pallas_call x19, Pallas kernels, tiled_call(): pl.pallas_call(kernel, grid=(steps,), out_shape=[jax.ShapeDtypeStruct(sha...  124 us
    ppermute x36, starting transfers between devices, to_z(): return lax.ppermute(value, 'seq', [(i, i ^ step) for i in range(4)])  71 us
    unnamed x281, local copies, waits for them, and re-layouts  66.8 us
    pallas_call x21, Pallas kernels, dense_call(): pl.pallas_call(kernel, out_shape=[jax.ShapeDtypeStruct(shape, kind) for s...  47.9 us
    ppermute x17, waiting for transfers between devices, to_tp(): return lax.ppermute(value, 'tp', [(0, 1), (1, 0)])  39.4 us
    ppermute x17, starting transfers between devices, to_tp(): return lax.ppermute(value, 'tp', [(0, 1), (1, 0)])  18.2 us
    pallas_call x8, Pallas kernels, fill_rows(): pl.pallas_call(lambda *refs: fill_kernel(rows, part, start, *refs), out_s...  17.5 us
  transfers between devices with their start and end apart: 86, of which 39 were waited for; matrix products, arithmetic and copies ran while one was open for 4% of the time, Pallas kernels for 26%

profile of v5, /device:TPU:18, one launch (start us, length us, event | category | flops | bytes accessed | tf_op | source)
XLA Modules:
  0.0 777.9 jit_solution(15073185740446031020)
XLA Ops:
  13.6 13.3 %collective-permute-done.3 = bf16[1,2,160]{2,1,0:T(2,128)(2,1)S(1)} collective-permute-done((bf16[1,2,160]{2,1,0:T(2,128)(2,1)S(1)}, bf16[1,2,160]{2,1,0:T(2,128)(2,1)S(1)}, u32[]{:S(2)}, u32[]{:S(2)}) %collective-permute-start.3) | collective-permute-done | bytes 672 | tf_op jit(solution)/shard_map/ppermute | solution.py:372
  53.7 21.3 %collective-permute-done.6.two_far = bf16[256,1280]{1,0:T(8,128)(2,1)} collective-permute-done((bf16[256,1280]{1,0:T(8,128)(2,1)}, bf16[256,1280]{1,0:T(8,128)(2,1)}, u32[]{:S(2)}, u32[]{:S(2)}) %collective-permute-start.6) | collective-permute-done | bytes 655392 | tf_op jit(solution)/shard_map/ppermute | solution.py:372
  94.6 19.2 %collective-permute-done.13.refs_0_ = bf16[160,1792]{1,0:T(8,128)(2,1)S(1)} collective-permute-done((bf16[160,1792]{1,0:T(8,128)(2,1)S(1)}, bf16[160,1792]{1,0:T(8,128)(2,1)S(1)}, u32[]{:S(2)}, u32[]{:S(2)}) %collective-permute-start.13) | collective-permute-done | bytes 573472 | tf_op jit(solution)/shard_map/ppermute | solution.py:372
  123.7 18.7 %collective-permute-done.16.refs_0_ = bf16[160,1792]{1,0:T(8,128)(2,1)} collective-permute-done((bf16[160,1792]{1,0:T(8,128)(2,1)}, bf16[160,1792]{1,0:T(8,128)(2,1)}, u32[]{:S(2)}, u32[]{:S(2)}) %collective-permute-start.16) | collective-permute-done | bytes 573472 | tf_op jit(solution)/shard_map/ppermute | solution.py:372
  175.3 23.2 %collective-permute-done.20.two_far = bf16[256,1280]{1,0:T(8,128)(2,1)S(1)} collective-permute-done((bf16[256,1280]{1,0:T(8,128)(2,1)S(1)}, bf16[256,1280]{1,0:T(8,128)(2,1)S(1)}, u32[]{:S(2)}, u32[]{:S(2)}) %collective-permute-start.20) | collective-permute-done | bytes 655392 | tf_op jit(solution)/shard_map/ppermute | solution.py:372
  201.2 6.4 collective-permute-done.18.refs_2_
  221.9 9.0 %collective-permute-done.21.early = bf16[512,320]{1,0:T(8,128)(2,1)} collective-permute-done((bf16[512,320]{1,0:T(8,128)(2,1)}, bf16[512,320]{1,0:T(8,128)(2,1)}, u32[]{:S(2)}, u32[]{:S(2)}) %collective-permute-start.21) | collective-permute-done | bytes 327712 | tf_op jit(solution)/shard_map/ppermute | solution.py:1290
  231.8 15.2 %attend.1 = (bf16[512,640]{1,0:T(8,128)(2,1)S(1)}, f32[8,512]{1,0:T(8,128)S(1)}) custom-call(bf16[512,640]{1,0:T(8,128)(2,1)S(1)} %copy-done.32, bf16[512,320]{1,0:T(8,128)(2,1)} %collective-permute-done.21.early, bf16[512,320]{1,0:T(8,128)(2,1)S(1)} %copy-done.41, s32[2,512]{1,0:T(2,128)S(1)} %pad_add_fusion.1.query_ids, s32[1024,2]{1,0:T(8,128)S(1)} %copy.62.key_ids), custom_call_target="tpu_custom_call" | custom-call | flops 1024 | bytes 4096 | tf_op jit(solution)/shard_map/attend/pallas_call | solution.py:523
  255.3 9.8 %collective-permute-start.25 = (bf16[256,1280]{1,0:T(8,128)(2,1)S(1)}, bf16[256,1280]{1,0:T(8,128)(2,1)S(1)}, u32[]{:S(2)}, u32[]{:S(2)}) collective-permute-start(bf16[256,1280]{1,0:T(8,128)(2,1)S(1)} %get-tuple-element.351), channel_id=1, source_target_pairs={{0,2},{2,0},{4,6},{6,4},{1,3},{3,1},{5,7},{7,5},{8,10},{10,8},{12,... | collective-permute-start | bytes 1966088 | tf_op jit(solution)/shard_map/ppermute | solution.py:372
  271.2 32.7 %collective-permute-done.25.got_two = bf16[256,1280]{1,0:T(8,128)(2,1)S(1)} collective-permute-done((bf16[256,1280]{1,0:T(8,128)(2,1)S(1)}, bf16[256,1280]{1,0:T(8,128)(2,1)S(1)}, u32[]{:S(2)}, u32[]{:S(2)}) %collective-permute-start.25) | collective-permute-done | bytes 655392 | tf_op jit(solution)/shard_map/ppermute | solution.py:372
  318.4 7.4 collective-permute-done.27.last_one
  329.7 7.8 %collective-permute-done.32.second.one_near = bf16[128,1280]{1,0:T(8,128)(2,1)S(1)} collective-permute-done((bf16[128,1280]{1,0:T(8,128)(2,1)S(1)}, bf16[128,1280]{1,0:T(8,128)(2,1)S(1)}, u32[]{:S(2)}, u32[]{:S(2)}) %collective-permute-start.32) | collective-permute-done | bytes 327712 | tf_op jit(solution)/shard_map/ppermute | solution.py:372
  340.4 12.0 %collective-permute-done.33.one_far = bf16[256,1280]{1,0:T(8,128)(2,1)S(1)} collective-permute-done((bf16[256,1280]{1,0:T(8,128)(2,1)S(1)}, bf16[256,1280]{1,0:T(8,128)(2,1)S(1)}, u32[]{:S(2)}, u32[]{:S(2)}) %collective-permute-start.33) | collective-permute-done | bytes 655392 | tf_op jit(solution)/shard_map/ppermute | solution.py:376
  357.7 15.7 %hidden_units.1 = (bf16[512,1792]{1,0:T(8,128)(2,1)S(1)}, f32[512,1792]{1,0:T(8,128)}, f32[512,1792]{1,0:T(8,128)}) custom-call(bf16[512,2560]{1,0:T(8,128)(2,1)S(1)} %take_rows.6.normed.left, bf16[1280,1792]{1,0:T(8,128)(2,1)} %fill_rows.13.gate_m.refs_2_, bf16[1280,1792]{1,0:T(8,128)(2,1)} %collective-permute-done.38.gate_o.refs_3_, ...), custom_call_target="tpu_custom_call" | custom-call | flops 1024 | bytes 4096 | tf_op jit(solution)/shard_map/hidden_units/pallas_call | solution.py:668
  379.9 9.8 %collective-permute-done.42.left_other = bf16[512,640]{1,0:T(8,128)(2,1)S(1)} collective-permute-done((bf16[512,640]{1,0:T(8,128)(2,1)S(1)}, bf16[512,640]{1,0:T(8,128)(2,1)S(1)}, u32[]{:S(2)}, u32[]{:S(2)}) %collective-permute-start.42) | collective-permute-done | bytes 655392 | tf_op jit(solution)/shard_map/ppermute | solution.py:364
  397.7 6.4 outer.11.refs_0_.refs_2_
  404.1 7.9 %project_back.5 = (bf16[256,1280]{1,0:T(8,128)(2,1)S(1)}, bf16[256,1280]{1,0:T(8,128)(2,1)S(1)}, bf16[256,1280]{1,0:T(8,128)(2,1)S(1)}, bf16[256,1280]{1,0:T(8,128)(2,1)S(1)}) custom-call(bf16[512,1792]{1,0:T(8,128)(2,1)S(1)} %copy-done.12, bf16[1280,1792]{1,0:T(8,128)(2,1)} %fill_rows.15.refs_1_.down_m, ...), custom_call_target="tpu_custom_call" | custom-call | flops 1024 | bytes 4096 | tf_op jit(solution)/shard_map/project_back/pallas_call | solution.py:668
  412.1 11.5 %hidden_grads.1 = (bf16[512,1792]{1,0:T(8,128)(2,1)S(1)}, bf16[512,1792]{1,0:T(8,128)(2,1)S(1)}) custom-call(bf16[512,2560]{1,0:T(8,128)(2,1)} %copy-done.2, bf16[1280,1792]{1,0:T(8,128)(2,1)} %fill_rows.15.refs_1_.down_m, bf16[1280,1792]{1,0:T(8,128)(2,1)} %collective-permute-done.44.refs_2_.down_o, f32[512,1792]{1,0:T(8,128)} %get-tuple-element.402.gate_slope, ...), custom_call_target="tpu_custom_call" | custom-call | flops 1024 | bytes 4096 | tf_op jit(solution)/shard_map/hidden_grads/pallas_call | solution.py:668
  426.8 14.2 %project_back.6 = (bf16[256,1280]{1,0:T(8,128)(2,1)S(1)}, bf16[256,1280]{1,0:T(8,128)(2,1)S(1)}, bf16[256,1280]{1,0:T(8,128)(2,1)S(1)}, bf16[256,1280]{1,0:T(8,128)(2,1)S(1)}) custom-call(bf16[512,1792]{1,0:T(8,128)(2,1)S(1)} %get-tuple-element.438.refs_0_.right, bf16[512,1792]{1,0:T(8,128)(2,1)} %copy-done.9, bf16[1280,1792]{1,0:T(8,128)(2,1)} %fill_rows.13.gate_m.refs_2_, ...), custom_call_target="tpu_custom_call" | custom-call | flops 1024 | bytes 4096 | tf_op jit(solution)/shard_map/project_back/pallas_call | solution.py:668
  452.8 6.6 outer.12
  461.7 15.4 %collective-permute-done.50.got_one = bf16[256,1280]{1,0:T(8,128)(2,1)S(1)} collective-permute-done((bf16[256,1280]{1,0:T(8,128)(2,1)S(1)}, bf16[256,1280]{1,0:T(8,128)(2,1)S(1)}, u32[]{:S(2)}, u32[]{:S(2)}) %collective-permute-start.50) | collective-permute-done | bytes 655392 | tf_op jit(solution)/shard_map/ppermute | solution.py:376
  489.3 6.5 outer.13.refs_0_.refs_2_
  495.9 6.6 outer.14
  502.5 6.6 outer.15.refs_0_.refs_4_
  509.1 6.5 collective-permute-done.54.last_one
  536.3 16.0 %collective-permute-done.61.two_far = bf16[256,1280]{1,0:T(8,128)(2,1)S(1)} collective-permute-done((bf16[256,1280]{1,0:T(8,128)(2,1)S(1)}, bf16[256,1280]{1,0:T(8,128)(2,1)S(1)}, u32[]{:S(2)}, u32[]{:S(2)}) %collective-permute-start.61) | collective-permute-done | bytes 655392 | tf_op jit(solution)/shard_map/ppermute | solution.py:372
  562.2 16.3 %attend_back.1 = (bf16[512,640]{1,0:T(8,128)(2,1)S(1)}, bf16[512,320]{1,0:T(8,128)(2,1)S(1)}, f32[512,320]{1,0:T(8,128)S(1)}) custom-call(bf16[512,640]{1,0:T(8,128)(2,1)S(1)} %copy-done.33, bf16[512,320]{1,0:T(8,128)(2,1)} %collective-permute-done.21.early, bf16[512,320]{1,0:T(8,128)(2,1)S(1)} %copy-done.42, s32[2,512]{1,0:T(2,128)S(1)} %copy-done.95, ...), custom_call_target="tpu_custom_call" | custom-call | flops 1024 | bytes 4096 | tf_op jit(solution)/shard_map/attend_back/pallas_call | solution.py:523
  615.1 6.6 project_back.7
  633.9 7.2 collective-permute-start.74
  651.6 37.8 %collective-permute-done.74.got_two = bf16[256,1280]{1,0:T(8,128)(2,1)S(1)} collective-permute-done((bf16[256,1280]{1,0:T(8,128)(2,1)S(1)}, bf16[256,1280]{1,0:T(8,128)(2,1)S(1)}, u32[]{:S(2)}, u32[]{:S(2)}) %collective-permute-start.74) | collective-permute-done | bytes 655392 | tf_op jit(solution)/shard_map/ppermute | solution.py:372
  711.7 9.1 %collective-permute-start.85 = (f32[2,160]{1,0:T(2,128)S(1)}, f32[2,160]{1,0:T(2,128)S(1)}, u32[]{:S(2)}, u32[]{:S(2)}) collective-permute-start(f32[2,160]{1,0:T(2,128)S(1)} %slice_bitcast_fusion), channel_id=1, source_target_pairs={{0,2},{2,0},{4,6},{6,4},{1,3},{3,1},{5,7},{7,5},{8,10},{10,8},{12,... | collective-permute-start | bytes 3848 | tf_op jit(solution)/shard_map/ppermute | solution.py:372
  720.7 19.1 %collective-permute-done.85 = f32[2,160]{1,0:T(2,128)S(1)} collective-permute-done((f32[2,160]{1,0:T(2,128)S(1)}, f32[2,160]{1,0:T(2,128)S(1)}, u32[]{:S(2)}, u32[]{:S(2)}) %collective-permute-start.85) | collective-permute-done | bytes 1312 | tf_op jit(solution)/shard_map/ppermute | solution.py:372
  (562 shorter events, 353.2 us)
Async XLA Ops:
  34.2 51.8 %collective-permute-start.9 = (bf16[320,1664]{1,0:T(8,128)(2,1)}, bf16[320,1664]{1,0:T(8,128)(2,1)}, u32[]{:S(2)}, u32[]{:S(2)}) collective-permute-start(bf16[320,1664]{1,0:T(8,128)(2,1)} %fill_rows.8.refs_1_), channel_id=1, source_target_pairs={{0,4},{2,6},{4,0},{6,2},{1,5},{3,7},{5,1},{7,3},{8,12},{10,14},{12... | collective-permute-start | bytes 3194888 | tf_op jit(solution)/shard_map/ppermute | solution.py:372
  35.5 39.5 %collective-permute-start.6 = (bf16[256,1280]{1,0:T(8,128)(2,1)}, bf16[256,1280]{1,0:T(8,128)(2,1)}, u32[]{:S(2)}, u32[]{:S(2)}) collective-permute-start(bf16[256,1280]{1,0:T(8,128)(2,1)} %pair_rows.9), channel_id=1, source_target_pairs={{0,2},{2,0},{4,6},{6,4},{1,3},{3,1},{5,7},{7,5},{8,10},{10,8},{12,... | collective-permute-start | bytes 1966088 | tf_op jit(solution)/shard_map/ppermute | solution.py:372
  37.9 37.0 %collective-permute-start.5 = (bf16[256,1280]{1,0:T(8,128)(2,1)}, bf16[256,1280]{1,0:T(8,128)(2,1)}, u32[]{:S(2)}, u32[]{:S(2)}) collective-permute-start(bf16[256,1280]{1,0:T(8,128)(2,1)} %pair_rows.8), channel_id=1, source_target_pairs={{0,1},{1,0},{2,3},{3,2},{4,5},{5,4},{6,7},{7,6},{8,9},{9,8},{10,11... | collective-permute-start | bytes 1966088 | tf_op jit(solution)/shard_map/ppermute | solution.py:376
  41.3 42.8 %collective-permute-start.10 = (bf16[160,1792]{1,0:T(8,128)(2,1)}, bf16[160,1792]{1,0:T(8,128)(2,1)}, u32[]{:S(2)}, u32[]{:S(2)}) collective-permute-start(bf16[160,1792]{1,0:T(8,128)(2,1)} %get-tuple-element.309), channel_id=1, source_target_pairs={{0,2},{2,0},{4,6},{6,4},{1,3},{3,1},{5,7},{7,5},{8,10},{10,8},{12,... | collective-permute-start | bytes 1720328 | tf_op jit(solution)/shard_map/ppermute | solution.py:372
  89.3 60.0 %collective-permute-start.11 = (bf16[640,1664]{1,0:T(8,128)(2,1)}, bf16[640,1664]{1,0:T(8,128)(2,1)}, u32[]{:S(2)}, u32[]{:S(2)}) collective-permute-start(bf16[640,1664]{1,0:T(8,128)(2,1)} %get-tuple-element.314), channel_id=1, source_target_pairs={{0,16},{8,24},{16,0},{24,8},{1,17},{9,25},{17,1},{25,9},{2,18},{10... | collective-permute-start | bytes 6389768 | tf_op jit(solution)/shard_map/ppermute | solution.py:368
  92.4 53.6 %collective-permute-start.12 = (bf16[320,1792]{1,0:T(8,128)(2,1)}, bf16[320,1792]{1,0:T(8,128)(2,1)}, u32[]{:S(2)}, u32[]{:S(2)}) collective-permute-start(bf16[320,1792]{1,0:T(8,128)(2,1)} %fill_rows.9.refs_1_), channel_id=1, source_target_pairs={{0,4},{2,6},{4,0},{6,2},{1,5},{3,7},{5,1},{7,3},{8,12},{10,14},{12... | collective-permute-start | bytes 3440648 | tf_op jit(solution)/shard_map/ppermute | solution.py:372
  93.0 49.5 %collective-permute-start.16 = (bf16[160,1792]{1,0:T(8,128)(2,1)}, bf16[160,1792]{1,0:T(8,128)(2,1)}, u32[]{:S(2)}, u32[]{:S(2)}) collective-permute-start(bf16[160,1792]{1,0:T(8,128)(2,1)} %get-tuple-element.322), channel_id=1, source_target_pairs={{0,2},{2,0},{4,6},{6,4},{1,3},{3,1},{5,7},{7,5},{8,10},{10,8},{12,... | collective-permute-start | bytes 1720328 | tf_op jit(solution)/shard_map/ppermute | solution.py:372
  151.8 59.2 %collective-permute-start.29 = (bf16[640,1792]{1,0:T(8,128)(2,1)}, bf16[640,1792]{1,0:T(8,128)(2,1)}, u32[]{:S(2)}, u32[]{:S(2)}) collective-permute-start(bf16[640,1792]{1,0:T(8,128)(2,1)} %get-tuple-element.362), channel_id=1, source_target_pairs={{0,16},{8,24},{16,0},{24,8},{1,17},{9,25},{17,1},{25,9},{2,18},{10... | collective-permute-start | bytes 6881288 | tf_op jit(solution)/shard_map/ppermute | solution.py:368
  156.4 51.3 %collective-permute-start.18 = (bf16[320,1792]{1,0:T(8,128)(2,1)}, bf16[320,1792]{1,0:T(8,128)(2,1)}, u32[]{:S(2)}, u32[]{:S(2)}) collective-permute-start(bf16[320,1792]{1,0:T(8,128)(2,1)} %fill_rows.10.refs_1_), channel_id=1, source_target_pairs={{0,4},{2,6},{4,0},{6,2},{1,5},{3,7},{5,1},{7,3},{8,12},{10,14},{12... | collective-permute-start | bytes 3440648 | tf_op jit(solution)/shard_map/ppermute | solution.py:372
  161.0 37.4 %collective-permute-start.20 = (bf16[256,1280]{1,0:T(8,128)(2,1)S(1)}, bf16[256,1280]{1,0:T(8,128)(2,1)S(1)}, u32[]{:S(2)}, u32[]{:S(2)}) collective-permute-start(bf16[256,1280]{1,0:T(8,128)(2,1)S(1)} %pair_rows.11), channel_id=1, source_target_pairs={{0,2},{2,0},{4,6},{6,4},{1,3},{3,1},{5,7},{7,5},{8,10},{10,8},{12,... | collective-permute-start | bytes 1966088 | tf_op jit(solution)/shard_map/ppermute | solution.py:372
  163.1 35.4 %collective-permute-start.19 = (bf16[256,1280]{1,0:T(8,128)(2,1)S(1)}, bf16[256,1280]{1,0:T(8,128)(2,1)S(1)}, u32[]{:S(2)}, u32[]{:S(2)}) collective-permute-start(bf16[256,1280]{1,0:T(8,128)(2,1)S(1)} %pair_rows.10), channel_id=1, source_target_pairs={{0,1},{1,0},{2,3},{3,2},{4,5},{5,4},{6,7},{7,6},{8,9},{9,8},{10,11... | collective-permute-start | bytes 1966088 | tf_op jit(solution)/shard_map/ppermute | solution.py:376
  213.5 97.4 %collective-permute-start.30 = (bf16[640,1792]{1,0:T(8,128)(2,1)}, bf16[640,1792]{1,0:T(8,128)(2,1)}, u32[]{:S(2)}, u32[]{:S(2)}) collective-permute-start(bf16[640,1792]{1,0:T(8,128)(2,1)} %get-tuple-element.365), channel_id=1, source_target_pairs={{0,16},{8,24},{16,0},{24,8},{1,17},{9,25},{17,1},{25,9},{2,18},{10... | collective-permute-start | bytes 6881288 | tf_op jit(solution)/shard_map/ppermute | solution.py:368
  247.6 59.0 %collective-permute-start.31 = (bf16[320,1792]{1,0:T(8,128)(2,1)S(1)}, bf16[320,1792]{1,0:T(8,128)(2,1)S(1)}, u32[]{:S(2)}, u32[]{:S(2)}) collective-permute-start(bf16[320,1792]{1,0:T(8,128)(2,1)S(1)} %copy-done.24), channel_id=1, source_target_pairs={{0,4},{2,6},{4,0},{6,2},{1,5},{3,7},{5,1},{7,3},{8,12},{10,14},{12... | collective-permute-start | bytes 3440648 | tf_op jit(solution)/shard_map/ppermute | solution.py:372
  255.3 48.6 %collective-permute-start.25 = (bf16[256,1280]{1,0:T(8,128)(2,1)S(1)}, bf16[256,1280]{1,0:T(8,128)(2,1)S(1)}, u32[]{:S(2)}, u32[]{:S(2)}) collective-permute-start(bf16[256,1280]{1,0:T(8,128)(2,1)S(1)} %get-tuple-element.351), channel_id=1, source_target_pairs={{0,2},{2,0},{4,6},{6,4},{1,3},{3,1},{5,7},{7,5},{8,10},{10,8},{12,... | collective-permute-start | bytes 1966088 | tf_op jit(solution)/shard_map/ppermute | solution.py:372
  265.1 90.5 %collective-permute-start.38 = (bf16[1280,1792]{1,0:T(8,128)(2,1)}, bf16[1280,1792]{1,0:T(8,128)(2,1)}, u32[]{:S(2)}, u32[]{:S(2)}) collective-permute-start(bf16[1280,1792]{1,0:T(8,128)(2,1)} %fill_rows.13.gate_m.refs_2_), channel_id=1, source_target_pairs={{0,8},{8,0},{16,24},{24,16},{1,9},{9,1},{17,25},{25,17},{2,10},{10... | collective-permute-start | bytes 13762568 | tf_op jit(solution)/shard_map/ppermute | solution.py:364
  313.6 41.9 %collective-permute-start.39 = (bf16[1280,1792]{1,0:T(8,128)(2,1)}, bf16[1280,1792]{1,0:T(8,128)(2,1)S(1)}, u32[]{:S(2)}, u32[]{:S(2)}) collective-permute-start(bf16[1280,1792]{1,0:T(8,128)(2,1)} %fill_rows.14.up_m.refs_4_), channel_id=1, source_target_pairs={{0,8},{8,0},{16,24},{24,16},{1,9},{9,1},{17,25},{25,17},{2,10},{10... | collective-permute-start | bytes 13762568 | tf_op jit(solution)/shard_map/ppermute | solution.py:364
  313.7 61.0 %collective-permute-start.41 = (bf16[640,1792]{1,0:T(8,128)(2,1)}, bf16[640,1792]{1,0:T(8,128)(2,1)S(1)}, u32[]{:S(2)}, u32[]{:S(2)}) collective-permute-start(bf16[640,1792]{1,0:T(8,128)(2,1)} %get-tuple-element.384), channel_id=1, source_target_pairs={{0,16},{8,24},{16,0},{24,8},{1,17},{9,25},{17,1},{25,9},{2,18},{10... | collective-permute-start | bytes 6881288 | tf_op jit(solution)/shard_map/ppermute | solution.py:368
  397.1 52.4 %collective-permute-start.49 = (bf16[640,1792]{1,0:T(8,128)(2,1)}, bf16[640,1792]{1,0:T(8,128)(2,1)}, u32[]{:S(2)}, u32[]{:S(2)}) collective-permute-start(bf16[640,1792]{1,0:T(8,128)(2,1)} %outer.10), channel_id=1, source_target_pairs={{0,16},{8,24},{16,0},{24,8},{1,17},{9,25},{17,1},{25,9},{2,18},{10... | collective-permute-start | bytes 6881288 | tf_op jit(solution)/shard_map/ppermute | solution.py:368
  459.4 71.1 %collective-permute-start.52 = (bf16[640,1792]{1,0:T(8,128)(2,1)}, bf16[640,1792]{1,0:T(8,128)(2,1)}, u32[]{:S(2)}, u32[]{:S(2)}) collective-permute-start(bf16[640,1792]{1,0:T(8,128)(2,1)} %outer.12), channel_id=1, source_target_pairs={{0,16},{8,24},{16,0},{24,8},{1,17},{9,25},{17,1},{25,9},{2,18},{10... | collective-permute-start | bytes 6881288 | tf_op jit(solution)/shard_map/ppermute | solution.py:368
  459.9 36.0 %collective-permute-start.47 = (bf16[512,1792]{1,0:T(8,128)(2,1)S(1)}, bf16[512,1792]{1,0:T(8,128)(2,1)S(1)}, u32[]{:S(2)}, u32[]{:S(2)}) collective-permute-start(bf16[512,1792]{1,0:T(8,128)(2,1)S(1)} %copy-done.10), channel_id=1, source_target_pairs={{0,8},{8,0},{16,24},{24,16},{1,9},{9,1},{17,25},{25,17},{2,10},{10... | collective-permute-start | bytes 5505032 | tf_op jit(solution)/shard_map/ppermute | solution.py:364
  461.7 60.5 %collective-permute-start.53 = (bf16[320,1792]{1,0:T(8,128)(2,1)}, bf16[320,1792]{1,0:T(8,128)(2,1)S(1)}, u32[]{:S(2)}, u32[]{:S(2)}) collective-permute-start(bf16[320,1792]{1,0:T(8,128)(2,1)} %get-tuple-element.420), channel_id=1, source_target_pairs={{0,4},{2,6},{4,0},{6,2},{1,5},{3,7},{5,1},{7,3},{8,12},{10,14},{12... | collective-permute-start | bytes 3440648 | tf_op jit(solution)/shard_map/ppermute | solution.py:372
  533.0 55.8 %collective-permute-start.58 = (bf16[640,1792]{1,0:T(8,128)(2,1)}, bf16[640,1792]{1,0:T(8,128)(2,1)}, u32[]{:S(2)}, u32[]{:S(2)}) collective-permute-start(bf16[640,1792]{1,0:T(8,128)(2,1)} %outer.14), channel_id=1, source_target_pairs={{0,16},{8,24},{16,0},{24,8},{1,17},{9,25},{17,1},{25,9},{2,18},{10... | collective-permute-start | bytes 6881288 | tf_op jit(solution)/shard_map/ppermute | solution.py:368
  536.3 46.4 %collective-permute-start.59 = (bf16[320,1792]{1,0:T(8,128)(2,1)S(1)}, bf16[320,1792]{1,0:T(8,128)(2,1)S(1)}, u32[]{:S(2)}, u32[]{:S(2)}) collective-permute-start(bf16[320,1792]{1,0:T(8,128)(2,1)S(1)} %get-tuple-element.464), channel_id=1, source_target_pairs={{0,4},{2,6},{4,0},{6,2},{1,5},{3,7},{5,1},{7,3},{8,12},{10,14},{12... | collective-permute-start | bytes 3440648 | tf_op jit(solution)/shard_map/ppermute | solution.py:372
  553.6 35.2 %collective-permute-start.63 = (bf16[512,640]{1,0:T(8,128)(2,1)}, bf16[512,640]{1,0:T(8,128)(2,1)S(1)}, u32[]{:S(2)}, u32[]{:S(2)}) collective-permute-start(bf16[512,640]{1,0:T(8,128)(2,1)} %get-tuple-element.609), channel_id=1, source_target_pairs={{0,8},{8,0},{16,24},{24,16},{1,9},{9,1},{17,25},{25,17},{2,10},{10... | collective-permute-start | bytes 1966088 | tf_op jit(solution)/shard_map/ppermute | solution.py:364
  553.6 35.1 %collective-permute-start.64 = (bf16[512,640]{1,0:T(8,128)(2,1)S(1)}, bf16[512,640]{1,0:T(8,128)(2,1)S(1)}, u32[]{:S(2)}, u32[]{:S(2)}) collective-permute-start(bf16[512,640]{1,0:T(8,128)(2,1)S(1)} %get-tuple-element.608), channel_id=1, source_target_pairs={{0,8},{8,0},{16,24},{24,16},{1,9},{9,1},{17,25},{25,17},{2,10},{10... | collective-permute-start | bytes 1966088 | tf_op jit(solution)/shard_map/ppermute | solution.py:364
  614.8 82.7 %collective-permute-start.78 = (bf16[320,2432]{1,0:T(8,128)(2,1)}, bf16[320,2432]{1,0:T(8,128)(2,1)S(1)}, u32[]{:S(2)}, u32[]{:S(2)}) collective-permute-start(bf16[320,2432]{1,0:T(8,128)(2,1)} %get-tuple-element.487), channel_id=1, source_target_pairs={{0,4},{2,6},{4,0},{6,2},{1,5},{3,7},{5,1},{7,3},{8,12},{10,14},{12... | collective-permute-start | bytes 4669448 | tf_op jit(solution)/shard_map/ppermute | solution.py:372
  625.6 65.2 %collective-permute-start.72 = (bf16[640,1024]{1,0:T(8,128)(2,1)S(1)}, bf16[640,1024]{1,0:T(8,128)(2,1)S(1)}, u32[]{:S(2)}, u32[]{:S(2)}) collective-permute-start(bf16[640,1024]{1,0:T(8,128)(2,1)S(1)} %outer.19), channel_id=1, source_target_pairs={{0,16},{8,24},{16,0},{24,8},{1,17},{9,25},{17,1},{25,9},{2,18},{10... | collective-permute-start | bytes 3932168 | tf_op jit(solution)/shard_map/ppermute | solution.py:368
  633.9 55.5 %collective-permute-start.74 = (bf16[256,1280]{1,0:T(8,128)(2,1)S(1)}, bf16[256,1280]{1,0:T(8,128)(2,1)S(1)}, u32[]{:S(2)}, u32[]{:S(2)}) collective-permute-start(bf16[256,1280]{1,0:T(8,128)(2,1)S(1)} %get-tuple-element.510.two_send), channel_id=1, source_target_pairs={{0,2},{2,0},{4,6},{6,4},{1,3},{3,1},{5,7},{7,5},{8,10},{10,8},{12,... | collective-permute-start | bytes 1966088 | tf_op jit(solution)/shard_map/ppermute | solution.py:372
  644.9 52.5 %collective-permute-start.68 = (bf16[128,1280]{1,0:T(8,128)(2,1)}, bf16[128,1280]{1,0:T(8,128)(2,1)S(1)}, u32[]{:S(2)}, u32[]{:S(2)}) collective-permute-start(bf16[128,1280]{1,0:T(8,128)(2,1)} %get-tuple-element.490), channel_id=1, source_target_pairs={{0,2},{2,0},{4,6},{6,4},{1,3},{3,1},{5,7},{7,5},{8,10},{10,8},{12,... | collective-permute-start | bytes 983048 | tf_op jit(solution)/shard_map/ppermute | solution.py:372
  650.3 47.1 %collective-permute-start.69 = (bf16[128,1280]{1,0:T(8,128)(2,1)}, bf16[128,1280]{1,0:T(8,128)(2,1)}, u32[]{:S(2)}, u32[]{:S(2)}) collective-permute-start(bf16[128,1280]{1,0:T(8,128)(2,1)} %get-tuple-element.491), channel_id=1, source_target_pairs={{0,1},{1,0},{2,3},{3,2},{4,5},{5,4},{6,7},{7,6},{8,9},{9,8},{10,11... | collective-permute-start | bytes 983048 | tf_op jit(solution)/shard_map/ppermute | solution.py:376
  700.0 46.9 %collective-permute-start.82 = (bf16[160,2432]{1,0:T(8,128)(2,1)}, bf16[160,2432]{1,0:T(8,128)(2,1)S(1)}, u32[]{:S(2)}, u32[]{:S(2)}) collective-permute-start(bf16[160,2432]{1,0:T(8,128)(2,1)} %get-tuple-element.528), channel_id=1, source_target_pairs={{0,2},{2,0},{4,6},{6,4},{1,3},{3,1},{5,7},{7,5},{8,10},{10,8},{12,... | collective-permute-start | bytes 2334728 | tf_op jit(solution)/shard_map/ppermute | solution.py:372
  702.8 44.1 %collective-permute-start.77 = (bf16[320,1024]{1,0:T(8,128)(2,1)}, bf16[320,1024]{1,0:T(8,128)(2,1)S(1)}, u32[]{:S(2)}, u32[]{:S(2)}) collective-permute-start(bf16[320,1024]{1,0:T(8,128)(2,1)} %copy-done.98), channel_id=1, source_target_pairs={{0,4},{2,6},{4,0},{6,2},{1,5},{3,7},{5,1},{7,3},{8,12},{10,14},{12... | collective-permute-start | bytes 1966088 | tf_op jit(solution)/shard_map/ppermute | solution.py:372
  (190 other events, 1998.0 us)

commit v6 on v5

--- a/solution.py
+++ b/solution.py
@@ -1308,29 +1308,29 @@
     )
     branch = scatter_middle(*hold(branch, attended_other))
     branch = scatter_second(*branch)
-    down_plane, down_mine = place_rows(*hold((down_pair, down_far), branch[:2]), seq_index)
-    up_mine = fill_rows(*hold((up_mine, up_x), down_plane))
-    up_weights = up_mine, to_core(up_mine)
-    down_x = to_x(hold(down_plane, up_mine))
     residual, two_one, two_two = dense_call(
         residual_kernel,
         "residual",
         [(row_shape, jnp.float32)] + [(half_shape, jnp.bfloat16)] * 2,
         [],
-        (*hold(branch, up_mine), tokens_in, gain_two),
-    )
-    two_wait = gather_second(*gather_first(two_one, two_two))
+        (*branch, tokens_in, gain_two),
+    )
+    down_plane, down_mine = place_rows(*hold((down_pair, down_far), residual), seq_index)
+    up_mine = fill_rows(*hold((up_mine, up_x), down_plane))
+    up_weights = up_mine, to_core(up_mine)
+    down_x = to_x(hold(down_plane, up_mine))
+    two_wait = gather_second(*hold(gather_first(two_one, two_two), up_mine))
     span_two = take_rows(*two_wait)
     span_other = cross_left(span_two)
     cot_other = cross_left(cot_span, log_total)
     hidden_low, gate_slope, up_slope = hidden_units(
-        hold(span_two, cot_other), gate_weights, up_weights
+        hold(span_two, cot_other, span_other), gate_weights, up_weights
     )
     hidden_other = cross_right(hidden_low, 1)
     down_mine = fill_rows(*hold((down_mine, down_x), hidden_low))
     down_weights = down_mine, to_core(down_mine)
 
-    down_parts = hold((cot_span, cot_other, hidden_low, hidden_other), down_mine, span_other)
+    down_parts = hold((cot_span, cot_other, hidden_low, hidden_other), down_mine)
     down_give = outer(*down_parts, 1)
     down_back = to_x(down_give)
     down_keep = outer(*hold(down_parts, down_give), 0)

time: 788 us -> 792 us (level)
  starting transfers between devices: 106 us -> 123 us
    ppermute x36, waiting for transfers between devices: 266 us -> 283 us  [to_z(): return lax.ppermute(value, 'seq', [(i, i ^ step) for i in range(4)])]
    ppermute x36, starting transfers between devices: 71 us -> 84.3 us  [to_z(): return lax.ppermute(value, 'seq', [(i, i ^ step) for i in range(4)])]
    ppermute x17, waiting for transfers between devices: 39.4 us -> 26.6 us  [to_tp(): return lax.ppermute(value, 'tp', [(0, 1), (1, 0)])]
    unnamed x281 -> x275, local copies, waits for them, and re-layouts: 66.8 us -> 65.6 us
  transfers between devices with their start and end apart: 86 -> 86, of which waited for: 39 -> 41; matrix products, arithmetic and copies ran while one was open for 4% -> 3% of each run, Pallas kernels for 26% -> 25%
where the time goes in v6:
time: 792 us; the launch traced here: 786 us
  waiting for transfers between devices  349 us (44%)
  Pallas kernels  232 us (29%)
  starting transfers between devices  123 us (16%)
  local copies, waits for them, and re-layouts  72.7 us (9%)
    ppermute x36, waiting for transfers between devices, to_z(): return lax.ppermute(value, 'seq', [(i, i ^ step) for i in range(4)])  283 us
    pallas_call x19, Pallas kernels, tiled_call(): pl.pallas_call(kernel, grid=(steps,), out_shape=[jax.ShapeDtypeStruct(sha...  124 us
    ppermute x36, starting transfers between devices, to_z(): return lax.ppermute(value, 'seq', [(i, i ^ step) for i in range(4)])  84.3 us
    unnamed x275, local copies, waits for them, and re-layouts  65.6 us
    pallas_call x21, Pallas kernels, dense_call(): pl.pallas_call(kernel, out_shape=[jax.ShapeDtypeStruct(shape, kind) for s...  45.4 us
    ppermute x17, waiting for transfers between devices, to_tp(): return lax.ppermute(value, 'tp', [(0, 1), (1, 0)])  26.6 us
    ppermute x17, starting transfers between devices, to_tp(): return lax.ppermute(value, 'tp', [(0, 1), (1, 0)])  19.8 us
    pallas_call x8, Pallas kernels, fill_rows(): pl.pallas_call(lambda *refs: fill_kernel(rows, part, start, *refs), out_s...  17.5 us
  transfers between devices with their start and end apart: 86, of which 41 were waited for; matrix products, arithmetic and copies ran while one was open for 3% of the time, Pallas kernels for 25%

profile of v6, /device:TPU:18, one launch (start us, length us, event | category | flops | bytes accessed | tf_op | source)
XLA Modules:
  0.0 785.5 jit_solution(13111925071560177349)
XLA Ops:
  13.7 13.3 %collective-permute-done.3 = bf16[1,2,160]{2,1,0:T(2,128)(2,1)S(1)} collective-permute-done((bf16[1,2,160]{2,1,0:T(2,128)(2,1)S(1)}, bf16[1,2,160]{2,1,0:T(2,128)(2,1)S(1)}, u32[]{:S(2)}, u32[]{:S(2)}) %collective-permute-start.3) | collective-permute-done | bytes 672 | tf_op jit(solution)/shard_map/ppermute | solution.py:372
  53.7 21.3 %collective-permute-done.6.two_far = bf16[256,1280]{1,0:T(8,128)(2,1)} collective-permute-done((bf16[256,1280]{1,0:T(8,128)(2,1)}, bf16[256,1280]{1,0:T(8,128)(2,1)}, u32[]{:S(2)}, u32[]{:S(2)}) %collective-permute-start.6) | collective-permute-done | bytes 655392 | tf_op jit(solution)/shard_map/ppermute | solution.py:372
  94.6 19.2 %collective-permute-done.13.refs_0_ = bf16[160,1792]{1,0:T(8,128)(2,1)S(1)} collective-permute-done((bf16[160,1792]{1,0:T(8,128)(2,1)S(1)}, bf16[160,1792]{1,0:T(8,128)(2,1)S(1)}, u32[]{:S(2)}, u32[]{:S(2)}) %collective-permute-start.13) | collective-permute-done | bytes 573472 | tf_op jit(solution)/shard_map/ppermute | solution.py:372
  123.8 18.7 %collective-permute-done.16.refs_0_ = bf16[160,1792]{1,0:T(8,128)(2,1)} collective-permute-done((bf16[160,1792]{1,0:T(8,128)(2,1)}, bf16[160,1792]{1,0:T(8,128)(2,1)}, u32[]{:S(2)}, u32[]{:S(2)}) %collective-permute-start.16) | collective-permute-done | bytes 573472 | tf_op jit(solution)/shard_map/ppermute | solution.py:372
  170.6 25.2 %collective-permute-done.20.two_far = bf16[256,1280]{1,0:T(8,128)(2,1)S(1)} collective-permute-done((bf16[256,1280]{1,0:T(8,128)(2,1)S(1)}, bf16[256,1280]{1,0:T(8,128)(2,1)S(1)}, u32[]{:S(2)}, u32[]{:S(2)}) %collective-permute-start.20) | collective-permute-done | bytes 655392 | tf_op jit(solution)/shard_map/ppermute | solution.py:372
  198.5 6.5 collective-permute-done.18.refs_2_
  214.6 12.2 %collective-permute-done.21.early = bf16[512,320]{1,0:T(8,128)(2,1)S(1)} collective-permute-done((bf16[512,320]{1,0:T(8,128)(2,1)S(1)}, bf16[512,320]{1,0:T(8,128)(2,1)S(1)}, u32[]{:S(2)}, u32[]{:S(2)}) %collective-permute-start.21) | collective-permute-done | bytes 327712 | tf_op jit(solution)/shard_map/ppermute | solution.py:1290
  226.8 13.8 %attend.1 = (bf16[512,640]{1,0:T(8,128)(2,1)S(1)}, f32[8,512]{1,0:T(8,128)S(1)}) custom-call(bf16[512,640]{1,0:T(8,128)(2,1)S(1)} %copy-done.34, bf16[512,320]{1,0:T(8,128)(2,1)S(1)} %collective-permute-done.21.early, bf16[512,320]{1,0:T(8,128)(2,1)S(1)} %copy-done.43, s32[2,512]{1,0:T(2,128)S(1)} %pad_add_fusion.1.query_ids, s32[1024,2]{1,0:T(8,128)S(1)} %copy.62.key_ids), custom_call_target="tpu_custom_call" | custom-call | flops 1024 | bytes 4096 | tf_op jit(solution)/shard_map/attend/pallas_call | solution.py:523
  240.6 11.2 %collective-permute-start.33 = (bf16[320,1792]{1,0:T(8,128)(2,1)S(1)}, bf16[320,1792]{1,0:T(8,128)(2,1)S(1)}, u32[]{:S(2)}, u32[]{:S(2)}) collective-permute-start(bf16[320,1792]{1,0:T(8,128)(2,1)S(1)} %copy-done.22), channel_id=1, source_target_pairs={{0,4},{2,6},{4,0},{6,2},{1,5},{3,7},{5,1},{7,3},{8,12},{10,14},{12... | collective-permute-start | bytes 3440648 | tf_op jit(solution)/shard_map/ppermute | solution.py:372
  251.8 6.7 project_back.4
  260.0 9.8 %collective-permute-start.25 = (bf16[256,1280]{1,0:T(8,128)(2,1)S(1)}, bf16[256,1280]{1,0:T(8,128)(2,1)S(1)}, u32[]{:S(2)}, u32[]{:S(2)}) collective-permute-start(bf16[256,1280]{1,0:T(8,128)(2,1)S(1)} %get-tuple-element.351), channel_id=1, source_target_pairs={{0,2},{2,0},{4,6},{6,4},{1,3},{3,1},{5,7},{7,5},{8,10},{10,8},{12,... | collective-permute-start | bytes 1966088 | tf_op jit(solution)/shard_map/ppermute | solution.py:372
  275.7 32.9 %collective-permute-done.25.got_two = bf16[256,1280]{1,0:T(8,128)(2,1)S(1)} collective-permute-done((bf16[256,1280]{1,0:T(8,128)(2,1)S(1)}, bf16[256,1280]{1,0:T(8,128)(2,1)S(1)}, u32[]{:S(2)}, u32[]{:S(2)}) %collective-permute-start.25) | collective-permute-done | bytes 655392 | tf_op jit(solution)/shard_map/ppermute | solution.py:372
  331.2 7.7 collective-permute-done.29.second.one_near
  342.5 12.8 %collective-permute-done.35.two_far = bf16[256,1280]{1,0:T(8,128)(2,1)S(1)} collective-permute-done((bf16[256,1280]{1,0:T(8,128)(2,1)S(1)}, bf16[256,1280]{1,0:T(8,128)(2,1)S(1)}, u32[]{:S(2)}, u32[]{:S(2)}) %collective-permute-start.35) | collective-permute-done | bytes 655392 | tf_op jit(solution)/shard_map/ppermute | solution.py:372
  363.8 15.7 %hidden_units.1 = (bf16[512,1792]{1,0:T(8,128)(2,1)S(1)}, f32[512,1792]{1,0:T(8,128)}, f32[512,1792]{1,0:T(8,128)}) custom-call(bf16[512,2560]{1,0:T(8,128)(2,1)S(1)} %take_rows.6.normed.left, bf16[1280,1792]{1,0:T(8,128)(2,1)} %fill_rows.13.gate_m.refs_2_, bf16[1280,1792]{1,0:T(8,128)(2,1)} %collective-permute-done.40.gate_o.refs_3_, ...), custom_call_target="tpu_custom_call" | custom-call | flops 1024 | bytes 4096 | tf_op jit(solution)/shard_map/hidden_units/pallas_call | solution.py:668
  386.4 9.5 %collective-permute-done.42.refs_0_ = bf16[512,1792]{1,0:T(8,128)(2,1)S(1)} collective-permute-done((bf16[512,1792]{1,0:T(8,128)(2,1)S(1)}, bf16[512,1792]{1,0:T(8,128)(2,1)S(1)}, u32[]{:S(2)}, u32[]{:S(2)}) %collective-permute-start.42) | collective-permute-done | bytes 1835040 | tf_op jit(solution)/shard_map/ppermute | solution.py:364
  397.0 6.4 outer.10
  411.2 7.9 %project_back.5 = (bf16[256,1280]{1,0:T(8,128)(2,1)S(1)}, bf16[256,1280]{1,0:T(8,128)(2,1)S(1)}, bf16[256,1280]{1,0:T(8,128)(2,1)S(1)}, bf16[256,1280]{1,0:T(8,128)(2,1)S(1)}) custom-call(bf16[512,1792]{1,0:T(8,128)(2,1)S(1)} %copy-done.12, bf16[1280,1792]{1,0:T(8,128)(2,1)} %fill_rows.15.refs_1_.down_m, ...), custom_call_target="tpu_custom_call" | custom-call | flops 1024 | bytes 4096 | tf_op jit(solution)/shard_map/project_back/pallas_call | solution.py:668
  419.1 11.5 %hidden_grads.1 = (bf16[512,1792]{1,0:T(8,128)(2,1)S(1)}, bf16[512,1792]{1,0:T(8,128)(2,1)S(1)}) custom-call(bf16[512,2560]{1,0:T(8,128)(2,1)} %copy-done.2, bf16[1280,1792]{1,0:T(8,128)(2,1)} %fill_rows.15.refs_1_.down_m, bf16[1280,1792]{1,0:T(8,128)(2,1)} %collective-permute-done.44.refs_2_.down_o, f32[512,1792]{1,0:T(8,128)} %get-tuple-element.403.gate_slope, ...), custom_call_target="tpu_custom_call" | custom-call | flops 1024 | bytes 4096 | tf_op jit(solution)/shard_map/hidden_grads/pallas_call | solution.py:668
  435.1 14.2 %project_back.6 = (bf16[256,1280]{1,0:T(8,128)(2,1)S(1)}, bf16[256,1280]{1,0:T(8,128)(2,1)S(1)}, bf16[256,1280]{1,0:T(8,128)(2,1)S(1)}, bf16[256,1280]{1,0:T(8,128)(2,1)S(1)}) custom-call(bf16[512,1792]{1,0:T(8,128)(2,1)S(1)} %get-tuple-element.439.refs_0_.right, bf16[512,1792]{1,0:T(8,128)(2,1)} %copy-done.9, bf16[1280,1792]{1,0:T(8,128)(2,1)} %fill_rows.13.gate_m.refs_2_, ...), custom_call_target="tpu_custom_call" | custom-call | flops 1024 | bytes 4096 | tf_op jit(solution)/shard_map/project_back/pallas_call | solution.py:668
  458.4 7.0 outer.12
  470.0 13.9 %collective-permute-done.50.got_one = bf16[256,1280]{1,0:T(8,128)(2,1)S(1)} collective-permute-done((bf16[256,1280]{1,0:T(8,128)(2,1)S(1)}, bf16[256,1280]{1,0:T(8,128)(2,1)S(1)}, u32[]{:S(2)}, u32[]{:S(2)}) %collective-permute-start.50) | collective-permute-done | bytes 655392 | tf_op jit(solution)/shard_map/ppermute | solution.py:376
  497.7 6.5 outer.13.refs_0_.refs_2_
  510.6 6.6 outer.15.refs_0_.refs_4_
  517.2 6.6 collective-permute-done.54.last_one
  544.6 16.5 %collective-permute-done.61.two_far = bf16[256,1280]{1,0:T(8,128)(2,1)S(1)} collective-permute-done((bf16[256,1280]{1,0:T(8,128)(2,1)S(1)}, bf16[256,1280]{1,0:T(8,128)(2,1)S(1)}, u32[]{:S(2)}, u32[]{:S(2)}) %collective-permute-start.61) | collective-permute-done | bytes 655392 | tf_op jit(solution)/shard_map/ppermute | solution.py:372
  570.4 15.4 %attend_back.1 = (bf16[512,640]{1,0:T(8,128)(2,1)S(1)}, bf16[512,320]{1,0:T(8,128)(2,1)S(1)}, f32[512,320]{1,0:T(8,128)S(1)}) custom-call(bf16[512,640]{1,0:T(8,128)(2,1)S(1)} %copy-done.35, bf16[512,320]{1,0:T(8,128)(2,1)S(1)} %copy-done.46, bf16[512,320]{1,0:T(8,128)(2,1)S(1)} %copy-done.44, s32[2,512]{1,0:T(2,128)S(1)} %pad_add_fusion.1.query_ids, ...), custom_call_target="tpu_custom_call" | custom-call | flops 1024 | bytes 4096 | tf_op jit(solution)/shard_map/attend_back/pallas_call | solution.py:523
  623.3 6.6 project_back.7
  641.8 7.0 collective-permute-start.74
  659.5 37.6 %collective-permute-done.74.got_two = bf16[256,1280]{1,0:T(8,128)(2,1)S(1)} collective-permute-done((bf16[256,1280]{1,0:T(8,128)(2,1)S(1)}, bf16[256,1280]{1,0:T(8,128)(2,1)S(1)}, u32[]{:S(2)}, u32[]{:S(2)}) %collective-permute-start.74) | collective-permute-done | bytes 655392 | tf_op jit(solution)/shard_map/ppermute | solution.py:372
  718.4 10.0 %collective-permute-start.85 = (f32[2,160]{1,0:T(2,128)S(1)}, f32[2,160]{1,0:T(2,128)S(1)}, u32[]{:S(2)}, u32[]{:S(2)}) collective-permute-start(f32[2,160]{1,0:T(2,128)S(1)} %slice_bitcast_fusion), channel_id=1, source_target_pairs={{0,2},{2,0},{4,6},{6,4},{1,3},{3,1},{5,7},{7,5},{8,10},{10,8},{12,... | collective-permute-start | bytes 3848 | tf_op jit(solution)/shard_map/ppermute | solution.py:372
  728.5 19.1 %collective-permute-done.85 = f32[2,160]{1,0:T(2,128)S(1)} collective-permute-done((f32[2,160]{1,0:T(2,128)S(1)}, f32[2,160]{1,0:T(2,128)S(1)}, u32[]{:S(2)}, u32[]{:S(2)}) %collective-permute-start.85) | collective-permute-done | bytes 1312 | tf_op jit(solution)/shard_map/ppermute | solution.py:372
  (556 shorter events, 353.7 us)
Async XLA Ops:
  34.2 51.8 %collective-permute-start.9 = (bf16[320,1664]{1,0:T(8,128)(2,1)}, bf16[320,1664]{1,0:T(8,128)(2,1)}, u32[]{:S(2)}, u32[]{:S(2)}) collective-permute-start(bf16[320,1664]{1,0:T(8,128)(2,1)} %fill_rows.8.refs_1_), channel_id=1, source_target_pairs={{0,4},{2,6},{4,0},{6,2},{1,5},{3,7},{5,1},{7,3},{8,12},{10,14},{12... | collective-permute-start | bytes 3194888 | tf_op jit(solution)/shard_map/ppermute | solution.py:372
  35.5 39.5 %collective-permute-start.6 = (bf16[256,1280]{1,0:T(8,128)(2,1)}, bf16[256,1280]{1,0:T(8,128)(2,1)}, u32[]{:S(2)}, u32[]{:S(2)}) collective-permute-start(bf16[256,1280]{1,0:T(8,128)(2,1)} %pair_rows.9), channel_id=1, source_target_pairs={{0,2},{2,0},{4,6},{6,4},{1,3},{3,1},{5,7},{7,5},{8,10},{10,8},{12,... | collective-permute-start | bytes 1966088 | tf_op jit(solution)/shard_map/ppermute | solution.py:372
  38.0 37.0 %collective-permute-start.5 = (bf16[256,1280]{1,0:T(8,128)(2,1)}, bf16[256,1280]{1,0:T(8,128)(2,1)}, u32[]{:S(2)}, u32[]{:S(2)}) collective-permute-start(bf16[256,1280]{1,0:T(8,128)(2,1)} %pair_rows.8), channel_id=1, source_target_pairs={{0,1},{1,0},{2,3},{3,2},{4,5},{5,4},{6,7},{7,6},{8,9},{9,8},{10,11... | collective-permute-start | bytes 1966088 | tf_op jit(solution)/shard_map/ppermute | solution.py:376
  41.3 42.8 %collective-permute-start.10 = (bf16[160,1792]{1,0:T(8,128)(2,1)}, bf16[160,1792]{1,0:T(8,128)(2,1)}, u32[]{:S(2)}, u32[]{:S(2)}) collective-permute-start(bf16[160,1792]{1,0:T(8,128)(2,1)} %get-tuple-element.309), channel_id=1, source_target_pairs={{0,2},{2,0},{4,6},{6,4},{1,3},{3,1},{5,7},{7,5},{8,10},{10,8},{12,... | collective-permute-start | bytes 1720328 | tf_op jit(solution)/shard_map/ppermute | solution.py:372
  89.3 59.9 %collective-permute-start.11 = (bf16[640,1664]{1,0:T(8,128)(2,1)}, bf16[640,1664]{1,0:T(8,128)(2,1)}, u32[]{:S(2)}, u32[]{:S(2)}) collective-permute-start(bf16[640,1664]{1,0:T(8,128)(2,1)} %get-tuple-element.314), channel_id=1, source_target_pairs={{0,16},{8,24},{16,0},{24,8},{1,17},{9,25},{17,1},{25,9},{2,18},{10... | collective-permute-start | bytes 6389768 | tf_op jit(solution)/shard_map/ppermute | solution.py:368
  92.4 53.6 %collective-permute-start.12 = (bf16[320,1792]{1,0:T(8,128)(2,1)}, bf16[320,1792]{1,0:T(8,128)(2,1)}, u32[]{:S(2)}, u32[]{:S(2)}) collective-permute-start(bf16[320,1792]{1,0:T(8,128)(2,1)} %fill_rows.9.refs_1_), channel_id=1, source_target_pairs={{0,4},{2,6},{4,0},{6,2},{1,5},{3,7},{5,1},{7,3},{8,12},{10,14},{12... | collective-permute-start | bytes 3440648 | tf_op jit(solution)/shard_map/ppermute | solution.py:372
  93.0 49.5 %collective-permute-start.16 = (bf16[160,1792]{1,0:T(8,128)(2,1)}, bf16[160,1792]{1,0:T(8,128)(2,1)}, u32[]{:S(2)}, u32[]{:S(2)}) collective-permute-start(bf16[160,1792]{1,0:T(8,128)(2,1)} %get-tuple-element.322), channel_id=1, source_target_pairs={{0,2},{2,0},{4,6},{6,4},{1,3},{3,1},{5,7},{7,5},{8,10},{10,8},{12,... | collective-permute-start | bytes 1720328 | tf_op jit(solution)/shard_map/ppermute | solution.py:372
  151.8 56.6 %collective-permute-start.31 = (bf16[640,1792]{1,0:T(8,128)(2,1)}, bf16[640,1792]{1,0:T(8,128)(2,1)}, u32[]{:S(2)}, u32[]{:S(2)}) collective-permute-start(bf16[640,1792]{1,0:T(8,128)(2,1)} %get-tuple-element.364), channel_id=1, source_target_pairs={{0,16},{8,24},{16,0},{24,8},{1,17},{9,25},{17,1},{25,9},{2,18},{10... | collective-permute-start | bytes 6881288 | tf_op jit(solution)/shard_map/ppermute | solution.py:368
  153.6 51.3 %collective-permute-start.18 = (bf16[320,1792]{1,0:T(8,128)(2,1)}, bf16[320,1792]{1,0:T(8,128)(2,1)}, u32[]{:S(2)}, u32[]{:S(2)}) collective-permute-start(bf16[320,1792]{1,0:T(8,128)(2,1)} %fill_rows.10.refs_1_), channel_id=1, source_target_pairs={{0,4},{2,6},{4,0},{6,2},{1,5},{3,7},{5,1},{7,3},{8,12},{10,14},{12... | collective-permute-start | bytes 3440648 | tf_op jit(solution)/shard_map/ppermute | solution.py:372
  156.3 39.5 %collective-permute-start.20 = (bf16[256,1280]{1,0:T(8,128)(2,1)S(1)}, bf16[256,1280]{1,0:T(8,128)(2,1)S(1)}, u32[]{:S(2)}, u32[]{:S(2)}) collective-permute-start(bf16[256,1280]{1,0:T(8,128)(2,1)S(1)} %pair_rows.11), channel_id=1, source_target_pairs={{0,2},{2,0},{4,6},{6,4},{1,3},{3,1},{5,7},{7,5},{8,10},{10,8},{12,... | collective-permute-start | bytes 1966088 | tf_op jit(solution)/shard_map/ppermute | solution.py:372
  158.4 37.4 %collective-permute-start.19 = (bf16[256,1280]{1,0:T(8,128)(2,1)S(1)}, bf16[256,1280]{1,0:T(8,128)(2,1)S(1)}, u32[]{:S(2)}, u32[]{:S(2)}) collective-permute-start(bf16[256,1280]{1,0:T(8,128)(2,1)S(1)} %pair_rows.10), channel_id=1, source_target_pairs={{0,1},{1,0},{2,3},{3,2},{4,5},{5,4},{6,7},{7,6},{8,9},{9,8},{10,11... | collective-permute-start | bytes 1966088 | tf_op jit(solution)/shard_map/ppermute | solution.py:376
  210.9 115.2 %collective-permute-start.32 = (bf16[640,1792]{1,0:T(8,128)(2,1)}, bf16[640,1792]{1,0:T(8,128)(2,1)}, u32[]{:S(2)}, u32[]{:S(2)}) collective-permute-start(bf16[640,1792]{1,0:T(8,128)(2,1)} %get-tuple-element.367), channel_id=1, source_target_pairs={{0,16},{8,24},{16,0},{24,8},{1,17},{9,25},{17,1},{25,9},{2,18},{10... | collective-permute-start | bytes 6881288 | tf_op jit(solution)/shard_map/ppermute | solution.py:368
  212.1 39.7 %collective-permute-start.22 = (bf16[512,640]{1,0:T(8,128)(2,1)S(1)}, bf16[512,640]{1,0:T(8,128)(2,1)S(1)}, u32[]{:S(2)}, u32[]{:S(2)}) collective-permute-start(bf16[512,640]{1,0:T(8,128)(2,1)S(1)} %get-tuple-element.615), channel_id=1, source_target_pairs={{0,8},{8,0},{16,24},{24,16},{1,9},{9,1},{17,25},{25,17},{2,10},{10... | collective-permute-start | bytes 1966088 | tf_op jit(solution)/shard_map/ppermute | solution.py:364
  212.1 39.7 %collective-permute-start.23 = (bf16[512,640]{1,0:T(8,128)(2,1)S(1)}, bf16[512,640]{1,0:T(8,128)(2,1)S(1)}, u32[]{:S(2)}, u32[]{:S(2)}) collective-permute-start(bf16[512,640]{1,0:T(8,128)(2,1)S(1)} %get-tuple-element.614), channel_id=1, source_target_pairs={{0,8},{8,0},{16,24},{24,16},{1,9},{9,1},{17,25},{25,17},{2,10},{10... | collective-permute-start | bytes 1966088 | tf_op jit(solution)/shard_map/ppermute | solution.py:364
  240.6 81.2 %collective-permute-start.33 = (bf16[320,1792]{1,0:T(8,128)(2,1)S(1)}, bf16[320,1792]{1,0:T(8,128)(2,1)S(1)}, u32[]{:S(2)}, u32[]{:S(2)}) collective-permute-start(bf16[320,1792]{1,0:T(8,128)(2,1)S(1)} %copy-done.22), channel_id=1, source_target_pairs={{0,4},{2,6},{4,0},{6,2},{1,5},{3,7},{5,1},{7,3},{8,12},{10,14},{12... | collective-permute-start | bytes 3440648 | tf_op jit(solution)/shard_map/ppermute | solution.py:372
  260.0 48.6 %collective-permute-start.25 = (bf16[256,1280]{1,0:T(8,128)(2,1)S(1)}, bf16[256,1280]{1,0:T(8,128)(2,1)S(1)}, u32[]{:S(2)}, u32[]{:S(2)}) collective-permute-start(bf16[256,1280]{1,0:T(8,128)(2,1)S(1)} %get-tuple-element.351), channel_id=1, source_target_pairs={{0,2},{2,0},{4,6},{6,4},{1,3},{3,1},{5,7},{7,5},{8,10},{10,8},{12,... | collective-permute-start | bytes 1966088 | tf_op jit(solution)/shard_map/ppermute | solution.py:372
  312.2 49.4 %collective-permute-start.40 = (bf16[1280,1792]{1,0:T(8,128)(2,1)}, bf16[1280,1792]{1,0:T(8,128)(2,1)}, u32[]{:S(2)}, u32[]{:S(2)}) collective-permute-start(bf16[1280,1792]{1,0:T(8,128)(2,1)} %fill_rows.13.gate_m.refs_2_), channel_id=1, source_target_pairs={{0,8},{8,0},{16,24},{24,16},{1,9},{9,1},{17,25},{25,17},{2,10},{10... | collective-permute-start | bytes 13762568 | tf_op jit(solution)/shard_map/ppermute | solution.py:364
  329.9 51.8 %collective-permute-start.43 = (bf16[640,1792]{1,0:T(8,128)(2,1)}, bf16[640,1792]{1,0:T(8,128)(2,1)S(1)}, u32[]{:S(2)}, u32[]{:S(2)}) collective-permute-start(bf16[640,1792]{1,0:T(8,128)(2,1)} %get-tuple-element.385), channel_id=1, source_target_pairs={{0,16},{8,24},{16,0},{24,8},{1,17},{9,25},{17,1},{25,9},{2,18},{10... | collective-permute-start | bytes 6881288 | tf_op jit(solution)/shard_map/ppermute | solution.py:368
  403.4 52.4 %collective-permute-start.49 = (bf16[640,1792]{1,0:T(8,128)(2,1)}, bf16[640,1792]{1,0:T(8,128)(2,1)}, u32[]{:S(2)}, u32[]{:S(2)}) collective-permute-start(bf16[640,1792]{1,0:T(8,128)(2,1)} %outer.10), channel_id=1, source_target_pairs={{0,16},{8,24},{16,0},{24,8},{1,17},{9,25},{17,1},{25,9},{2,18},{10... | collective-permute-start | bytes 6881288 | tf_op jit(solution)/shard_map/ppermute | solution.py:368
  465.4 74.9 %collective-permute-start.52 = (bf16[640,1792]{1,0:T(8,128)(2,1)}, bf16[640,1792]{1,0:T(8,128)(2,1)}, u32[]{:S(2)}, u32[]{:S(2)}) collective-permute-start(bf16[640,1792]{1,0:T(8,128)(2,1)} %outer.12), channel_id=1, source_target_pairs={{0,16},{8,24},{16,0},{24,8},{1,17},{9,25},{17,1},{25,9},{2,18},{10... | collective-permute-start | bytes 6881288 | tf_op jit(solution)/shard_map/ppermute | solution.py:368
  466.7 37.4 %collective-permute-start.47 = (bf16[512,1792]{1,0:T(8,128)(2,1)S(1)}, bf16[512,1792]{1,0:T(8,128)(2,1)S(1)}, u32[]{:S(2)}, u32[]{:S(2)}) collective-permute-start(bf16[512,1792]{1,0:T(8,128)(2,1)S(1)} %copy-done.10), channel_id=1, source_target_pairs={{0,8},{8,0},{16,24},{24,16},{1,9},{9,1},{17,25},{25,17},{2,10},{10... | collective-permute-start | bytes 5505032 | tf_op jit(solution)/shard_map/ppermute | solution.py:364
  470.0 61.3 %collective-permute-start.53 = (bf16[320,1792]{1,0:T(8,128)(2,1)}, bf16[320,1792]{1,0:T(8,128)(2,1)S(1)}, u32[]{:S(2)}, u32[]{:S(2)}) collective-permute-start(bf16[320,1792]{1,0:T(8,128)(2,1)} %copy-done.98), channel_id=1, source_target_pairs={{0,4},{2,6},{4,0},{6,2},{1,5},{3,7},{5,1},{7,3},{8,12},{10,14},{12... | collective-permute-start | bytes 3440648 | tf_op jit(solution)/shard_map/ppermute | solution.py:372
  542.7 54.5 %collective-permute-start.58 = (bf16[640,1792]{1,0:T(8,128)(2,1)}, bf16[640,1792]{1,0:T(8,128)(2,1)}, u32[]{:S(2)}, u32[]{:S(2)}) collective-permute-start(bf16[640,1792]{1,0:T(8,128)(2,1)} %outer.14), channel_id=1, source_target_pairs={{0,16},{8,24},{16,0},{24,8},{1,17},{9,25},{17,1},{25,9},{2,18},{10... | collective-permute-start | bytes 6881288 | tf_op jit(solution)/shard_map/ppermute | solution.py:368
  544.6 46.3 %collective-permute-start.59 = (bf16[320,1792]{1,0:T(8,128)(2,1)S(1)}, bf16[320,1792]{1,0:T(8,128)(2,1)S(1)}, u32[]{:S(2)}, u32[]{:S(2)}) collective-permute-start(bf16[320,1792]{1,0:T(8,128)(2,1)S(1)} %get-tuple-element.464), channel_id=1, source_target_pairs={{0,4},{2,6},{4,0},{6,2},{1,5},{3,7},{5,1},{7,3},{8,12},{10,14},{12... | collective-permute-start | bytes 3440648 | tf_op jit(solution)/shard_map/ppermute | solution.py:372
  623.3 81.9 %collective-permute-start.78 = (bf16[320,2432]{1,0:T(8,128)(2,1)}, bf16[320,2432]{1,0:T(8,128)(2,1)S(1)}, u32[]{:S(2)}, u32[]{:S(2)}) collective-permute-start(bf16[320,2432]{1,0:T(8,128)(2,1)} %get-tuple-element.487), channel_id=1, source_target_pairs={{0,4},{2,6},{4,0},{6,2},{1,5},{3,7},{5,1},{7,3},{8,12},{10,14},{12... | collective-permute-start | bytes 4669448 | tf_op jit(solution)/shard_map/ppermute | solution.py:372
  633.7 64.8 %collective-permute-start.72 = (bf16[640,1024]{1,0:T(8,128)(2,1)S(1)}, bf16[640,1024]{1,0:T(8,128)(2,1)S(1)}, u32[]{:S(2)}, u32[]{:S(2)}) collective-permute-start(bf16[640,1024]{1,0:T(8,128)(2,1)S(1)} %outer.19), channel_id=1, source_target_pairs={{0,16},{8,24},{16,0},{24,8},{1,17},{9,25},{17,1},{25,9},{2,18},{10... | collective-permute-start | bytes 3932168 | tf_op jit(solution)/shard_map/ppermute | solution.py:368
  641.8 55.3 %collective-permute-start.74 = (bf16[256,1280]{1,0:T(8,128)(2,1)S(1)}, bf16[256,1280]{1,0:T(8,128)(2,1)S(1)}, u32[]{:S(2)}, u32[]{:S(2)}) collective-permute-start(bf16[256,1280]{1,0:T(8,128)(2,1)S(1)} %get-tuple-element.510.two_send), channel_id=1, source_target_pairs={{0,2},{2,0},{4,6},{6,4},{1,3},{3,1},{5,7},{7,5},{8,10},{10,8},{12,... | collective-permute-start | bytes 1966088 | tf_op jit(solution)/shard_map/ppermute | solution.py:372
  652.6 52.6 %collective-permute-start.68 = (bf16[128,1280]{1,0:T(8,128)(2,1)}, bf16[128,1280]{1,0:T(8,128)(2,1)S(1)}, u32[]{:S(2)}, u32[]{:S(2)}) collective-permute-start(bf16[128,1280]{1,0:T(8,128)(2,1)} %get-tuple-element.490), channel_id=1, source_target_pairs={{0,2},{2,0},{4,6},{6,4},{1,3},{3,1},{5,7},{7,5},{8,10},{10,8},{12,... | collective-permute-start | bytes 983048 | tf_op jit(solution)/shard_map/ppermute | solution.py:372
  658.7 46.4 %collective-permute-start.69 = (bf16[128,1280]{1,0:T(8,128)(2,1)}, bf16[128,1280]{1,0:T(8,128)(2,1)}, u32[]{:S(2)}, u32[]{:S(2)}) collective-permute-start(bf16[128,1280]{1,0:T(8,128)(2,1)} %get-tuple-element.491), channel_id=1, source_target_pairs={{0,1},{1,0},{2,3},{3,2},{4,5},{5,4},{6,7},{7,6},{8,9},{9,8},{10,11... | collective-permute-start | bytes 983048 | tf_op jit(solution)/shard_map/ppermute | solution.py:376
  707.8 46.9 %collective-permute-start.82 = (bf16[160,2432]{1,0:T(8,128)(2,1)}, bf16[160,2432]{1,0:T(8,128)(2,1)S(1)}, u32[]{:S(2)}, u32[]{:S(2)}) collective-permute-start(bf16[160,2432]{1,0:T(8,128)(2,1)} %get-tuple-element.528), channel_id=1, source_target_pairs={{0,2},{2,0},{4,6},{6,4},{1,3},{3,1},{5,7},{7,5},{8,10},{10,8},{12,... | collective-permute-start | bytes 2334728 | tf_op jit(solution)/shard_map/ppermute | solution.py:372
  710.5 44.1 %collective-permute-start.77 = (bf16[320,1024]{1,0:T(8,128)(2,1)}, bf16[320,1024]{1,0:T(8,128)(2,1)S(1)}, u32[]{:S(2)}, u32[]{:S(2)}) collective-permute-start(bf16[320,1024]{1,0:T(8,128)(2,1)} %copy-done.99), channel_id=1, source_target_pairs={{0,4},{2,6},{4,0},{6,2},{1,5},{3,7},{5,1},{7,3},{8,12},{10,14},{12... | collective-permute-start | bytes 1966088 | tf_op jit(solution)/shard_map/ppermute | solution.py:372
  713.4 34.8 %collective-permute-start.80 = (bf16[128,1280]{1,0:T(8,128)(2,1)}, bf16[128,1280]{1,0:T(8,128)(2,1)S(1)}, u32[]{:S(2)}, u32[]{:S(2)}) collective-permute-start(bf16[128,1280]{1,0:T(8,128)(2,1)} %copy-done.109), channel_id=1, source_target_pairs={{0,2},{2,0},{4,6},{6,4},{1,3},{3,1},{5,7},{7,5},{8,10},{10,8},{12,... | collective-permute-start | bytes 983048 | tf_op jit(solution)/shard_map/ppermute | solution.py:372
  (187 other events, 1881.5 us)
